TPU v7x, 32 devices: a whole 2x2x4 slice. The times are simulated.
32 devices in a mesh: dp: 8 (over y, x, core), tensor: 4 (over z).
Axes of the slice: x: 2, y: 2, z: 4, core: 2. Of those that a mesh axis runs over, the one named last changes fastest.
Arguments:
- tokens: bfloat16 [16384, 1152], P(('dp', 'tensor')), may hold values from -6 to 6
- conditioning: float32 [16, 1152], P('dp'), may hold values from -6 to 6
- master: float32 [4608, 72, 72], P(('dp', 'tensor')), may hold values from -1.06066017 to 1.06066017
- moment: float32 [4608, 72, 72], P(('dp', 'tensor')), may hold values from -384 to 384
- stats: float32 [2, 4608, 72, 72], P(None, ('dp', 'tensor')), may hold values from -187680.85 to 1179648, as said below
- roots: float32 [2, 4608, 72, 72], P(None, ('dp', 'tensor')), may hold values from -1 to 1
- cotangent: bfloat16 [16384, 1152], P(('dp', 'tensor')), may hold values from -6 to 6
Outputs:
- out_tokens: bfloat16 [16384, 1152], P(('dp', 'tensor'))
- grad_tokens: float32 [16384, 1152], P(('dp', 'tensor'))
- grad_conditioning: float32 [16, 1152], P('dp')
- new_master: float32 [4608, 72, 72], P(('dp', 'tensor'))
- new_moment: float32 [4608, 72, 72], P(('dp', 'tensor'))
- new_stats: float32 [2, 4608, 72, 72], P(None, ('dp', 'tensor'))
Inputs may be any that keep to these rules, and one draw needn't show every extreme that they name: `stats`: each block of both statistics is symmetric.
All inputs are finite; a program needn't handle non-finite values.
Results may differ from a plain program's by a relative error of at most 0.015.
The roundings to bfloat16 on the way count: a program that leaves them out, or rounds other values in their place, can miss the bound.
Values may be sent and summed in bfloat16 or wider, within the bound.
No kernel may reach another device: no remote copies, remote signals or barrier semaphores. Data moves between devices by JAX's collectives and lax.ppermute only.
A program may use at most 256 MiB of HBM per device.

v0:
```python
from functools import partial

import jax
import jax.numpy as jnp
from jax import lax
from jax.sharding import PartitionSpec as P

HEADS = 16
HEAD_DIM = 72
FF = 4608
LEN = 1024


epsilon = 1e-06
momentum_decay = 0.9
learning_rate = 0.4
HIGHEST = lax.Precision.HIGHEST


def layer_norm(values):
    center = values - jnp.mean(values, axis=-1, keepdims=True)
    variance = jnp.mean(center * center, axis=-1, keepdims=True)
    return center * lax.rsqrt(variance + epsilon)


def norm_back(values, gradient):
    _, pullback = jax.vjp(layer_norm, values)
    return pullback(gradient)[0]


def grid_shapes(model_width, block_size, tensor_size):
    row_blocks = model_width // block_size
    split_size = block_size * tensor_size
    return [
        (row_blocks, 3 * model_width // split_size),
        (model_width // split_size, row_blocks),
        (row_blocks, FF // split_size),
        (FF // split_size, row_blocks),
        (row_blocks, 6 * model_width // split_size),
    ]


def unpack(gathered, shapes, dp_size):
    block_size = gathered.shape[1]
    grouped = gathered.reshape(dp_size, gathered.shape[0] // dp_size, block_size, block_size)
    matrices = []
    offset = 0
    for row_blocks, col_blocks in shapes:
        count_here = row_blocks * col_blocks // dp_size
        matrices.append(
            grouped[:, offset : offset + count_here].reshape(
                row_blocks, col_blocks, block_size, block_size
            )
        )
        offset += count_here
    return matrices


def apply_blocks(activations, blocks):
    row_blocks, col_blocks, block_size = (blocks.shape[0], blocks.shape[1], blocks.shape[2])
    shaped = activations.reshape(activations.shape[0], row_blocks, block_size)
    product_out = jnp.einsum("tra,rcab->tcb", shaped, blocks, preferred_element_type=jnp.float32)
    return product_out.reshape(activations.shape[0], col_blocks * block_size)


def apply_back(gradients, blocks):
    row_blocks, col_blocks, block_size = (blocks.shape[0], blocks.shape[1], blocks.shape[2])
    shaped = gradients.reshape(gradients.shape[0], col_blocks, block_size)
    product_out = jnp.einsum("tcb,rcab->tra", shaped, blocks, preferred_element_type=jnp.float32)
    return product_out.reshape(gradients.shape[0], row_blocks * block_size)


def blocks_grad(activations, gradients, block_size):
    rows_total = activations.shape[0]
    shaped_in = activations.reshape(rows_total, activations.shape[1] // block_size, block_size)
    shaped_out = gradients.reshape(rows_total, gradients.shape[1] // block_size, block_size)
    return jnp.einsum("tra,tcb->rcab", shaped_in, shaped_out, preferred_element_type=jnp.float32)


def owner_split(member, dp_size):
    return member.reshape((dp_size, -1) + member.shape[2:])


def attend(pieces):
    query_rows, key_rows, value_rows = pieces
    factor = query_rows.shape[-1] ** (-0.5)
    scores = (
        jnp.einsum("qhd,khd->hqk", query_rows, key_rows, preferred_element_type=jnp.float32)
        * factor
    )
    highest = jnp.max(scores, axis=-1, keepdims=True)
    weights = jnp.exp(scores - highest)
    totals = jnp.sum(weights, axis=-1, keepdims=True)
    rounded = (weights / totals).astype(jnp.bfloat16)
    attended = jnp.einsum("hqk,khd->qhd", rounded, value_rows, preferred_element_type=jnp.float32)
    return (attended.astype(jnp.bfloat16), (highest + jnp.log(totals))[..., 0])


def attend_back(pieces):
    query_rows, key_rows, value_rows, grad_attended, log_totals = pieces
    factor = query_rows.shape[-1] ** (-0.5)
    scores = (
        jnp.einsum("qhd,khd->hqk", query_rows, key_rows, preferred_element_type=jnp.float32)
        * factor
    )
    weights = jnp.exp(scores - log_totals[..., None])
    grad_weights = jnp.einsum(
        "qhd,khd->hqk", grad_attended, value_rows, preferred_element_type=jnp.float32
    )
    grad_values = jnp.einsum(
        "hqk,qhd->khd",
        weights.astype(jnp.bfloat16),
        grad_attended,
        preferred_element_type=jnp.float32,
    )
    row_inner = jnp.sum(weights * grad_weights, axis=-1, keepdims=True)
    grad_scores = (weights * (grad_weights - row_inner)).astype(jnp.bfloat16)
    grad_queries = (
        jnp.einsum("hqk,khd->qhd", grad_scores, key_rows, preferred_element_type=jnp.float32)
        * factor
    )
    grad_keys = (
        jnp.einsum("hqk,qhd->khd", grad_scores, query_rows, preferred_element_type=jnp.float32)
        * factor
    )
    return jnp.stack([grad_queries, grad_keys, grad_values], axis=1).astype(jnp.bfloat16)


def local(tokens, conditioning, master, moment, stats, roots, cotangent):
    dp_size = lax.axis_size("dp")
    tensor_size = lax.axis_size("tensor")
    model_width = tokens.shape[1]
    block_size = master.shape[1]
    rows_dev = tokens.shape[0]
    sequences = conditioning.shape[0]
    group_rows = rows_dev * tensor_size
    heads_local = HEADS // tensor_size
    shapes = grid_shapes(model_width, block_size, tensor_size)
    low_master = master.astype(jnp.bfloat16)
    gathered = lax.all_gather(low_master, "dp", axis=0, tiled=True)
    w_qkv, w_out, w_up, w_down, w_ada = unpack(gathered, shapes, dp_size)
    silu_low = jax.nn.silu(conditioning).astype(jnp.bfloat16)
    own_modulation = apply_blocks(silu_low, w_ada)
    modulation = lax.all_gather(own_modulation, "tensor", axis=1, tiled=True)
    first_row = lax.axis_index("tensor") * rows_dev
    latent = (first_row + lax.iota(jnp.int32, rows_dev)) // LEN
    onehot = (latent[:, None] == lax.iota(jnp.int32, sequences)[None, :]).astype(jnp.float32)
    row_mods = jnp.dot(onehot, modulation, precision=HIGHEST).reshape(rows_dev, 6, model_width)
    shift_attention, scale_attention, gate_attention = (
        row_mods[:, 0],
        row_mods[:, 1],
        row_mods[:, 2],
    )
    shift_feed, scale_feed, gate_feed = (row_mods[:, 3], row_mods[:, 4], row_mods[:, 5])
    inputs = tokens.astype(jnp.float32)
    normed_one = layer_norm(inputs)
    modulated_one = (normed_one * (1.0 + scale_attention) + shift_attention).astype(jnp.bfloat16)
    modulated_one_all = lax.all_gather(modulated_one, "tensor", axis=0, tiled=True)
    projected = apply_blocks(modulated_one_all, w_qkv).astype(jnp.bfloat16)
    projected = projected.reshape(sequences, LEN, 3, heads_local, HEAD_DIM)
    query_rows, key_rows, value_rows = (projected[:, :, 0], projected[:, :, 1], projected[:, :, 2])
    attended, log_totals = lax.map(attend, (query_rows, key_rows, value_rows))
    flat_attended = attended.reshape(group_rows, heads_local * HEAD_DIM)
    branch = lax.psum_scatter(
        apply_blocks(flat_attended, w_out).astype(jnp.bfloat16),
        "tensor",
        scatter_dimension=0,
        tiled=True,
    ).astype(jnp.float32)
    middle = inputs + gate_attention * branch
    normed_two = layer_norm(middle)
    modulated_two = (normed_two * (1.0 + scale_feed) + shift_feed).astype(jnp.bfloat16)
    modulated_two_all = lax.all_gather(modulated_two, "tensor", axis=0, tiled=True)
    pre_gelu = apply_blocks(modulated_two_all, w_up)
    hidden = jax.nn.gelu(pre_gelu, approximate=True).astype(jnp.bfloat16)
    feed_out = lax.psum_scatter(
        apply_blocks(hidden, w_down).astype(jnp.bfloat16), "tensor", scatter_dimension=0, tiled=True
    ).astype(jnp.float32)
    result = middle + gate_feed * feed_out
    gathered_back = lax.all_gather(low_master, "dp", axis=0, tiled=True)
    w_qkv, w_out, w_up, w_down, w_ada = unpack(gathered_back, shapes, dp_size)
    grad_out = cotangent.astype(jnp.float32)
    grad_gate_feed = grad_out * feed_out
    grad_feed = (grad_out * gate_feed).astype(jnp.bfloat16)
    grad_feed_all = lax.all_gather(grad_feed, "tensor", axis=0, tiled=True)
    grad_hidden = apply_back(grad_feed_all, w_down)
    grad_down = blocks_grad(hidden, grad_feed_all, block_size)
    _, gelu_pullback = jax.vjp(partial(jax.nn.gelu, approximate=True), pre_gelu)
    grad_pre = gelu_pullback(grad_hidden)[0].astype(jnp.bfloat16)
    grad_up = blocks_grad(modulated_two_all, grad_pre, block_size)
    grad_modulated_two = lax.psum_scatter(
        apply_back(grad_pre, w_up).astype(jnp.bfloat16), "tensor", scatter_dimension=0, tiled=True
    ).astype(jnp.float32)
    grad_middle = grad_out + norm_back(middle, grad_modulated_two * (1.0 + scale_feed))
    grad_gate_attention = grad_middle * branch
    grad_branch = (grad_middle * gate_attention).astype(jnp.bfloat16)
    grad_branch_all = lax.all_gather(grad_branch, "tensor", axis=0, tiled=True)
    grad_attended = apply_back(grad_branch_all, w_out).astype(jnp.bfloat16)
    grad_out_proj = blocks_grad(flat_attended, grad_branch_all, block_size)
    grad_heads = lax.map(
        attend_back,
        (
            query_rows,
            key_rows,
            value_rows,
            grad_attended.reshape(sequences, LEN, heads_local, HEAD_DIM),
            log_totals,
        ),
    )
    grad_projected = grad_heads.reshape(group_rows, 3 * heads_local * HEAD_DIM)
    grad_qkv = blocks_grad(modulated_one_all, grad_projected, block_size)
    grad_modulated_one = lax.psum_scatter(
        apply_back(grad_projected, w_qkv).astype(jnp.bfloat16),
        "tensor",
        scatter_dimension=0,
        tiled=True,
    ).astype(jnp.float32)
    grad_inputs = grad_middle + norm_back(inputs, grad_modulated_one * (1.0 + scale_attention))
    row_gradients = jnp.stack(
        [
            grad_modulated_one,
            grad_modulated_one * normed_one,
            grad_gate_attention,
            grad_modulated_two,
            grad_modulated_two * normed_two,
            grad_gate_feed,
        ],
        axis=1,
    ).reshape(rows_dev, 6 * model_width)
    latent_gradients = jnp.dot(onehot.T, row_gradients, precision=HIGHEST)
    grad_mods = lax.psum_scatter(
        latent_gradients.astype(jnp.bfloat16), "tensor", scatter_dimension=1, tiled=True
    ).astype(jnp.float32)
    col_blocks = w_ada.shape[1]
    shaped_mods = grad_mods.reshape(sequences, col_blocks, block_size)
    shaped_silu = silu_low.astype(jnp.float32).reshape(
        sequences, model_width // block_size, block_size
    )
    grad_ada = jnp.einsum("sra,scb->rcab", shaped_silu, shaped_mods, precision=HIGHEST)
    partial_silu = jnp.einsum(
        "scb,rcab->sra", shaped_mods, w_ada.astype(jnp.float32), precision=HIGHEST
    ).reshape(sequences, model_width)
    grad_silu = lax.psum(partial_silu, "tensor")
    _, silu_pullback = jax.vjp(jax.nn.silu, conditioning)
    grad_conditioning = silu_pullback(grad_silu)[0]
    gradients = [grad_qkv, grad_out_proj, grad_up, grad_down, grad_ada]
    stacked = jnp.concatenate([owner_split(member, dp_size) for member in gradients], axis=1)
    summed = lax.psum_scatter(stacked, "dp", scatter_dimension=0, tiled=True)[0]
    left_stats = 0.5 * stats[0] + 0.5 * jnp.einsum(
        "nij,nkj->nik", summed, summed, precision=HIGHEST
    )
    right_stats = 0.5 * stats[1] + 0.5 * jnp.einsum(
        "nji,njk->nik", summed, summed, precision=HIGHEST
    )
    new_moment = momentum_decay * moment + (1.0 - momentum_decay) * summed
    update = jnp.einsum("nij,njk->nik", roots[0], new_moment, precision=HIGHEST)
    update = jnp.einsum("nij,njk->nik", update, roots[1], precision=HIGHEST)
    new_master = master - learning_rate * update
    return (
        result.astype(jnp.bfloat16),
        grad_inputs,
        grad_conditioning,
        new_master,
        new_moment,
        jnp.stack([left_stats, right_stats]),
    )


def solution(mesh):
    placed = (
        P(("dp", "tensor"), None),
        P("dp", None),
        P(("dp", "tensor"), None, None),
        P(("dp", "tensor"), None, None),
        P(None, ("dp", "tensor"), None, None),
        P(None, ("dp", "tensor"), None, None),
        P(("dp", "tensor"), None),
    )
    return jax.shard_map(
        local,
        mesh=mesh,
        in_specs=placed,
        out_specs=(
            P(("dp", "tensor"), None),
            P(("dp", "tensor"), None),
            P("dp", None),
            P(("dp", "tensor"), None, None),
            P(("dp", "tensor"), None, None),
            P(None, ("dp", "tensor"), None, None),
        ),
        check_vma=False,
    )
```

profile of v0, /device:TPU:0, one launch (start us, length us, event | category | flops | bytes accessed | tf_op | source)
XLA Modules:
  0.0 1587.2 jit_solution(7860415014819056380)
XLA Ops:
  12.7 110.6 %all-gather.7.cloned.1.call-done = bf16[1152,72,72]{2,1,0:T(8,128)(2,1)} async-done(((bf16[144,72,72]{2,1,0:T(8,128)(2,1)}), bf16[1152,72,72]{2,1,0:T(8,128)(2,1)}) %all-gather.7.cloned.1.call-update) | async-done | bytes 11943952 | tf_op jit(solution)/shard_map/all_gather | solution.py:140
  134.7 11.1 dot_general.125
  148.8 13.2 all-gather
  162.2 9.3 fusion.113
  171.5 9.8 fusion.132
  208.1 70.8 %all-gather.9.cloned.1.call-done = bf16[2048,1152]{1,0:T(8,128)(2,1)} async-done(((bf16[512,1152]{1,0:T(8,128)(2,1)}), bf16[2048,1152]{1,0:T(8,128)(2,1)}) %all-gather.9.cloned.1.call-update) | async-done | bytes 4718608 | tf_op jit(solution)/shard_map/all_gather | solution.py:158
  285.5 8.9 bitcast_convert_fusion.4
  306.9 51.6 %while.22 = (s32[]{:T(128)}, bf16[2,1024,4,72]{1,3,2,0:T(8,128)(2,1)}, f32[2,4,1024]{2,1,0:T(4,128)}, bf16[2,1024,4,72]{1,3,2,0:T(8,128)(2,1)}, bf16[2,1024,4,72...) while((s32[]{:T(128)}, bf16[2,1024,4,72]{1,3,2,0:T(8,128)(2,1)}, ...), condition=%wide.region_5.6_spmd, body=%wide.region_2.5_spmd.sunk | while | flops 1245999104 | bytes 66980012 | solution.py:162
  315.3 8.7 fusion.182
  341.0 8.7 fusion.182
  380.6 67.6 %reduce-scatter.9.cloned.1.call-done = bf16[512,1152]{1,0:T(8,128)(2,1)} async-done(((bf16[2048,1152]{1,0:T(8,128)(2,1)}), bf16[512,1152]{1,0:T(8,128)(2,1)}) %reduce-scatter.9.cloned.1.call-update) | async-done | bytes 1179664 | tf_op jit(solution)/shard_map/reduce_scatter | solution.py:164
  467.9 8.4 dot_general.135
  484.5 8.5 dot_general.141
  501.2 8.4 dot_general.144
  509.7 29.9 %all-gather.13.cloned.1.call-done = bf16[2048,1152]{1,0:T(8,128)(2,1)} async-done(((bf16[512,1152]{1,0:T(8,128)(2,1)}), bf16[2048,1152]{1,0:T(8,128)(2,1)}) %all-gather.13.cloned.1.call-update) | async-done | bytes 4718608 | tf_op jit(solution)/shard_map/all_gather | solution.py:185
  546.3 83.2 %all-gather.11.cloned.1.call-done = bf16[2048,1152]{1,0:T(8,128)(2,1)} async-done(((bf16[512,1152]{1,0:T(8,128)(2,1)}), bf16[2048,1152]{1,0:T(8,128)(2,1)}) %all-gather.11.cloned.1.call-update) | async-done | bytes 4718608 | tf_op jit(solution)/shard_map/all_gather | solution.py:173
  636.2 14.2 fusion.60
  650.4 14.8 fusion.56
  667.5 8.7 bitcast_convert_fusion.1
  682.1 8.6 dot_general.138
  690.7 11.1 bitcast_convert_fusion.2
  701.9 58.2 %reduce-scatter.13.cloned.1.call-done = bf16[512,1152]{1,0:T(8,128)(2,1)} async-done(((bf16[2048,1152]{1,0:T(8,128)(2,1)}), bf16[512,1152]{1,0:T(8,128)(2,1)}) %reduce-scatter.13.cloned.1.call-update) | async-done | bytes 1179664 | tf_op jit(solution)/shard_map/reduce_scatter | solution.py:191
  763.3 84.9 %reduce-scatter.11.cloned.1.call-done = bf16[512,1152]{1,0:T(8,128)(2,1)} async-done(((bf16[2048,1152]{1,0:T(8,128)(2,1)}), bf16[512,1152]{1,0:T(8,128)(2,1)}) %reduce-scatter.11.cloned.1.call-update) | async-done | bytes 1179664 | tf_op jit(solution)/shard_map/reduce_scatter | solution.py:176
  876.1 71.1 %all-gather.15.cloned.1.call-done = bf16[2048,1152]{1,0:T(8,128)(2,1)} async-done(((bf16[512,1152]{1,0:T(8,128)(2,1)}), bf16[2048,1152]{1,0:T(8,128)(2,1)}) %all-gather.15.cloned.1.call-update) | async-done | bytes 4718608 | tf_op jit(solution)/shard_map/all_gather | solution.py:197
  965.5 75.9 %while.23 = (s32[]{:T(128)}, bf16[2,1024,3,4,72]{1,4,3,2,0:T(8,128)(2,1)}, bf16[2,1024,4,72]{1,3,2,0:T(8,128)(2,1)S(1)}, bf16[2,1024,4,72]{1,3,2,0:T(8,128)(2,1)...) while((s32[]{:T(128)}, ...), condition=%wide.region_15.16_spmd, body=%wide.region_13.15_spmd.sunk | while | flops 3077009408 | bytes 199608528 | solution.py:200
  973.1 9.2 multiply_reduce_fusion.7
  982.4 10.6 multiply_convert_fusion.3
  1010.7 9.2 multiply_reduce_fusion.7
  1020.0 10.6 multiply_convert_fusion.3
  1051.2 9.3 bitcast_convert_fusion
  1068.4 14.8 convolution_bitcast_fusion.2
  1083.2 10.6 copy.126
  1093.8 14.8 convolution_bitcast_fusion.1
  1108.6 10.7 copy.127
  1123.5 12.3 fusion.82
  1179.1 15.2 copy.121
  1194.2 9.8 convolution_convert_fusion
  1213.9 28.8 %reduce-scatter.19.cloned.1.call-done = bf16[1728,2]{1,0:T(8,128)(2,1)} async-done(((bf16[6912,2]{1,0:T(8,128)(2,1)}), bf16[1728,2]{1,0:T(8,128)(2,1)}) %reduce-scatter.19.cloned.1.call-update) | async-done | bytes 6928
  1251.0 14.9 copy.130
  1265.9 11.2 bitcast_dynamic-update-slice_fusion.1
  1277.1 10.8 copy.122
  1287.9 12.9 dot_general.154
  1310.5 10.6 psum.7
  1321.7 201.8 %reduce-scatter.17.cloned.1.call-done = f32[1,144,72,72]{3,2,1,0:T(8,128)} async-done(((f32[8,144,72,72]{3,2,1,0:T(8,128)}), f32[1,144,72,72]{3,2,1,0:T(8,128)}) %reduce-scatter.17.cloned.1.call-update) | async-done | bytes 2986000 | tf_op jit(solution)/shard_map/reduce_scatter | solution.py:248
  1528.5 12.8 fusion.67
  1541.4 12.2 multiply_subtract_fusion
  1553.6 11.4 fusion.62
  1565.0 10.7 fusion.64
  (285 shorter events, 367.5 us)
Async XLA Ops:
  7.2 116.1 %all-gather.7.cloned.1.call-start = ((), (), s32[]{:S(2)}) async-start(), calls=%async_computation.6 | async-start | bytes 23887872 | tf_op jit(solution)/shard_map/all_gather | solution.py:140
  11.7 267.2 %all-gather.9.cloned.1.call-start = ((), (), s32[]{:S(2)}) async-start(), calls=%async_computation.7 | async-start | bytes 5898240 | tf_op jit(solution)/shard_map/all_gather | solution.py:158
  11.9 133.9 %copy-start.43 = (bf16[2,16,72]{2,1,0:T(8,128)(2,1)}, bf16[2,16,72]{2,1,0:T(8,128)(2,1)S(1)}, u32[]{:S(2)}) copy-start(bf16[2,16,72]{2,1,0:T(8,128)(2,1)S(1)} %reshape.259) | copy-start | bytes 13828
  11.9 150.2 %copy-start.38 = (s32[512]{0:T(512)}, s32[512]{0:T(512)S(1)}, u32[]{:S(2)}) copy-start(s32[512]{0:T(512)S(1)} %add_select_fusion) | copy-start | bytes 6148
  12.2 173.1 %copy-start.45 = (f32[512]{0:T(512)}, f32[512]{0:T(512)S(1)}, u32[]{:S(2)}) copy-start(f32[512]{0:T(512)S(1)} %broadcast_multiply_fusion.1) | copy-start | bytes 6148
  12.6 114.8 %copy-start.55 = (f32[512]{0:T(512)}, f32[512]{0:T(512)S(1)}, u32[]{:S(2)}) copy-start(f32[512]{0:T(512)S(1)} %fusion.99) | copy-start | bytes 6148
  12.7 172.6 %copy-start.51 = (f32[512]{0:T(512)}, f32[512]{0:T(512)S(1)}, u32[]{:S(2)}) copy-start(f32[512]{0:T(512)S(1)} %fusion.126) | copy-start | bytes 6148
  189.4 258.8 %reduce-scatter.9.cloned.1.call-start = ((), (), s32[]{:S(2)}) async-start(), calls=%async_computation.8 | async-start | bytes 5898240 | tf_op jit(solution)/shard_map/reduce_scatter | solution.py:164
  194.9 10.8 copy-start.24
  208.1 77.4 %copy-start.34 = (bf16[864,72,16]{0,1,2:T(8,128)(2,1)S(1)}, bf16[864,72,16]{0,1,2:T(8,128)(2,1)}, u32[]{:S(2)}) copy-start(bf16[864,72,16]{0,1,2:T(8,128)(2,1)} %reshape.304) | copy-start | bytes 5971972
  306.9 53.0 %copy-start.37 = (bf16[1152,72,4]{0,1,2:T(8,128)(2,1)S(1)}, bf16[1152,72,4]{0,1,2:T(8,128)(2,1)}, u32[]{:S(2)}) copy-start(bf16[1152,72,4]{0,1,2:T(8,128)(2,1)} %dot_general.132) | copy-start | bytes 1990660
  315.3 8.7 copy-start.23
  315.3 8.7 copy-start.26
  341.0 8.7 copy-start.23
  341.0 8.7 copy-start.26
  364.3 175.3 %all-gather.13.cloned.1.call-start = ((), (), s32[]{:S(2)}) async-start(), calls=%async_computation.11 | async-start | bytes 5898240 | tf_op jit(solution)/shard_map/all_gather | solution.py:185
  371.4 258.1 %all-gather.11.cloned.1.call-start = ((), (), s32[]{:S(2)}) async-start(), calls=%async_computation.9 | async-start | bytes 5898240 | tf_op jit(solution)/shard_map/all_gather | solution.py:173
  451.2 397.0 %copy-start.41 = (f32[512]{0:T(512)}, f32[512]{0:T(512)S(1)}, u32[]{:S(2)}) copy-start(f32[512]{0:T(512)S(1)} %broadcast_multiply_fusion) | copy-start | bytes 6148
  452.6 395.6 %copy-start.49 = (f32[512]{0:T(512)}, f32[512]{0:T(512)S(1)}, u32[]{:S(2)}) copy-start(f32[512]{0:T(512)S(1)} %fusion.127) | copy-start | bytes 6148
  454.1 305.9 %reduce-scatter.13.cloned.1.call-start = ((), (), s32[]{:S(2)}) async-start(), calls=%async_computation.12 | async-start | bytes 5898240 | tf_op jit(solution)/shard_map/reduce_scatter | solution.py:191
  629.5 20.9 %slice-start.7 = ((s8[4718592]{0:T(1024)(128)(4,1)}), s8[524288]{0:T(1024)(128)(4,1)S(1)}, s32[]{:S(2)}) async-start(s8[4718592]{0:T(1024)(128)(4,1)} %bitcast.443), calls=%async_computation.24 | async-start | bytes 1048576
  636.2 14.3 slice-start.8
  636.2 14.3 copy-start.32
  650.4 17.1 %copy-start.33 = (bf16[1152,72,16]{0,1,2:T(8,128)(2,1)S(1)}, bf16[1152,72,16]{0,1,2:T(8,128)(2,1)}, u32[]{:S(2)}) copy-start(bf16[1152,72,16]{0,1,2:T(8,128)(2,1)} %dot_general.144) | copy-start | bytes 7962628
  676.2 172.0 %reduce-scatter.11.cloned.1.call-start = ((), (), s32[]{:S(2)}) async-start(), calls=%async_computation.10 | async-start | bytes 5898240 | tf_op jit(solution)/shard_map/reduce_scatter | solution.py:176
  701.8 245.3 %all-gather.15.cloned.1.call-start = ((), (), s32[]{:S(2)}) async-start(), calls=%async_computation.13 | async-start | bytes 5898240 | tf_op jit(solution)/shard_map/all_gather | solution.py:197
  848.2 7.4 copy-start.15
  848.2 7.4 copy-start.19
  857.0 307.9 %reduce-scatter.15.cloned.1.call-start = ((), (), s32[]{:S(2)}) async-start(), calls=%async_computation.14 | async-start | bytes 5898240 | tf_op jit(solution)/shard_map/reduce_scatter | solution.py:212
  958.9 6.6 copy-start.40
  1030.5 6.2 copy-start
  1060.6 182.1 %reduce-scatter.19.cloned.1.call-start = ((), (), s32[]{:S(2)}) async-start(), calls=%async_computation.16 | async-start | bytes 2211840
  1135.8 8.2 copy-start.36
  1151.7 9.0 slice-start.2
  1151.7 8.9 slice-start.3
  1151.7 8.9 slice-start.4
  1160.7 7.3 copy-start.46
  1160.7 7.2 copy-start.52
  1179.1 15.2 copy-start.39
  1205.8 317.7 %reduce-scatter.17.cloned.1.call-start = ((), (), s32[]{:S(2)}) async-start(), calls=%async_computation.15 | async-start | bytes 47775744 | tf_op jit(solution)/shard_map/reduce_scatter | solution.py:248
  1205.8 38.1 %copy-start.44 = (bf16[2,16,72]{2,1,0:T(8,128)(2,1)S(1)}, bf16[2,16,72]{2,1,0:T(8,128)(2,1)}, u32[]{:S(2)}) copy-start(bf16[2,16,72]{2,1,0:T(8,128)(2,1)} %copy-done.43) | copy-start | bytes 13828
  1287.9 12.9 copy-start.9
  1309.8 11.2 copy-start.48
  1523.5 17.9 %slice-start.5 = ((s8[5308416]{0:T(1024)(128)(4,1)}), s8[1114112]{0:T(1024)(128)(4,1)S(1)}, s32[]{:S(2)}) async-start(s8[5308416]{0:T(1024)(128)(4,1)} %bitcast.433), calls=%async_computation.22 | async-start | bytes 2228224
  1528.5 12.9 copy-start.18
  1528.5 12.9 slice-start.6
  1528.5 25.1 %slice-start = ((s8[5308416]{0:T(1024)(128)(4,1)}), s8[4194304]{0:T(1024)(128)(4,1)S(1)}, s32[]{:S(2)}) async-start(s8[5308416]{0:T(1024)(128)(4,1)} %bitcast.416), calls=%async_computation.17 | async-start | bytes 8388608
  1541.4 12.2 slice-start.1
  (37 other events, 111.6 us)
Sparse Core Ops, SparseCore 0:
  11.8 111.3 all-gather.6
  189.6 89.3 all-gather.8
  364.5 83.6 reduce-scatter.8
  449.6 89.9 all-gather.12
  541.6 87.8 all-gather.10
  676.3 83.6 reduce-scatter.12
  762.4 85.7 reduce-scatter.10
  857.2 89.9 all-gather.14
  1060.7 83.6 reduce-scatter.14
  1205.9 36.7 reduce-scatter.18
  1277.2 246.2 reduce-scatter.16
where the time goes:
time: 1600 us; the launch traced here: 1590 us
  waiting for transfers between devices  807 us (50%)
  local copies, waits for them, and re-layouts  360 us (22%)
  matrix products  282 us (18%)
  other arithmetic  97.6 us (6%)
  blocking collectives  23.8 us (1%)
    reduce_scatter x1, waiting for transfers between devices, local(): summed = lax.psum_scatter(stacked, 'dp', scatter_dimension=0, tiled=True)[0]  202 us
    all_gather x1, waiting for transfers between devices, local(): gathered = lax.all_gather(low_master, 'dp', axis=0, tiled=True)  111 us
    reduce_scatter x1, waiting for transfers between devices, local(): lax.psum_scatter(apply_blocks(hidden, w_down).astype(jnp.bfloat16), 'tens...  84.9 us
    all_gather x1, waiting for transfers between devices, local(): lax.all_gather(modulated_two, 'tensor', axis=0, tiled=True)  83.2 us
    all_gather x1, waiting for transfers between devices, local(): grad_branch_all = lax.all_gather(grad_branch, 'tensor', axis=0, tiled=True)  71.1 us
    all_gather x1, waiting for transfers between devices, local(): lax.all_gather(modulated_one, 'tensor', axis=0, tiled=True)  70.8 us
    reduce_scatter x1, waiting for transfers between devices, local(): lax.psum_scatter(apply_blocks(flat_attended, w_out).astype(jnp.bfloat16),...  67.6 us
    reduce_scatter x1, waiting for transfers between devices, local(): lax.psum_scatter(apply_back(grad_pre, w_up).astype(jnp.bfloat16), 'tensor...  58.2 us
  transfers between devices with their start and end apart: 11, of which 10 were waited for; matrix products, arithmetic and copies ran while one was open for 18% of the time, Pallas kernels for 0%

commit v1 on v0

v1 whole, which is shorter than its diff:
```python
from functools import partial
import math

import jax
import jax.numpy as jnp
from jax import lax
from jax.experimental import pallas as pl
from jax.experimental.pallas import tpu as pltpu
from jax.sharding import PartitionSpec as P

HEADS = 16
HEAD_DIM = 72
FF = 4608
LEN = 1024

epsilon = 1e-06
momentum_decay = 0.9
learning_rate = 0.4
HIGHEST = lax.Precision.HIGHEST
bf16 = jnp.bfloat16
f32 = jnp.float32
VMEM_LIMIT = 56 * 1024 * 1024


def layer_norm(values):
    center = values - jnp.mean(values, axis=-1, keepdims=True)
    variance = jnp.mean(center * center, axis=-1, keepdims=True)
    return center * lax.rsqrt(variance + epsilon)


def norm_back(values, gradient):
    center = values - jnp.mean(values, axis=-1, keepdims=True)
    variance = jnp.mean(center * center, axis=-1, keepdims=True)
    inverse = lax.rsqrt(variance + epsilon)
    normed = center * inverse
    mean_grad = jnp.mean(gradient, axis=-1, keepdims=True)
    mean_inner = jnp.mean(gradient * normed, axis=-1, keepdims=True)
    return (gradient - mean_grad - normed * mean_inner) * inverse


def grid_shapes(model_width, block_size, tensor_size):
    row_blocks = model_width // block_size
    split_size = block_size * tensor_size
    return [
        (row_blocks, 3 * model_width // split_size),
        (model_width // split_size, row_blocks),
        (row_blocks, FF // split_size),
        (FF // split_size, row_blocks),
        (row_blocks, 6 * model_width // split_size),
    ]


def to_dense(blocks, col_blocks):
    count, size = blocks.shape[0], blocks.shape[1]
    if count >= col_blocks:
        shaped = blocks.reshape(count // col_blocks, col_blocks, size, size)
        return jnp.transpose(shaped, (0, 2, 1, 3)).reshape(-1, col_blocks * size)
    return jnp.transpose(blocks, (1, 0, 2)).reshape(size, count * size)


def to_blocks(dense, size):
    rows, cols = dense.shape
    shaped = dense.reshape(rows // size, size, cols // size, size)
    return jnp.transpose(shaped, (0, 2, 1, 3)).reshape(-1, size, size)


def whole_from_runs(runs, rows, cols):
    tensor_size, dp_size, r, c = runs.shape
    per = cols // c
    if per == 1:
        return runs.reshape(tensor_size, rows, cols)
    shaped = runs.reshape(tensor_size, dp_size // per, per, r, c)
    return jnp.transpose(shaped, (0, 1, 3, 2, 4)).reshape(tensor_size, rows, cols)


def runs_from_whole(whole, dp_size, r, c):
    tensor_size, rows, cols = whole.shape
    per = cols // c
    if per == 1:
        return whole.reshape(tensor_size, dp_size, r, c)
    shaped = whole.reshape(tensor_size, dp_size // per, r, per, c)
    return jnp.transpose(shaped, (0, 1, 3, 2, 4)).reshape(tensor_size, dp_size, r, c)


def bit_swap(values, bit):
    size = lax.axis_size("dp")
    return lax.ppermute(values, "dp", [(k, k ^ bit) for k in range(size)])


def ring(values):
    size = lax.axis_size("tensor")
    return lax.ppermute(values, "tensor", [(k, (k + 1) % size) for k in range(size)])


def pair_swap(values):
    size = lax.axis_size("tensor")
    return lax.ppermute(values, "tensor", [(k, k ^ 1) for k in range(size)])


def gather(piece, order):
    hops = [piece]
    for _ in range(lax.axis_size("tensor") - 1):
        hops.append(ring(hops[-1]))
    found = [(0, jnp.stack(hops))]
    for bit in list(order) + [1]:
        found = found + [(mask ^ bit, bit_swap(stack, bit)) for mask, stack in found]
    return found, hops[-1]


def assemble_kernel(plan, where, *refs):
    stacks, out, sems = refs[: len(plan)], refs[len(plan)], refs[len(plan) + 1]
    i, t = where[0], where[1]
    tensor_size = out.shape[0]
    copies = []
    for number, (mask, row, rows) in enumerate(plan):
        for k in range(tensor_size):
            src_t = lax.rem(t + tensor_size - k, tensor_size)
            copies.append(
                pltpu.make_async_copy(
                    stacks[number].at[k],
                    out.at[src_t, i ^ mask, pl.ds(row, rows)],
                    sems.at[number, k],
                )
            )
    for copy in copies:
        copy.start()
    for copy in copies:
        copy.wait()


def assemble(streams, dp_size, where):
    plan, stacks, row = [], [], 0
    for found in streams:
        rows = found[0][1].shape[1]
        for mask, stack in found:
            plan.append((mask, row, rows))
            stacks.append(stack)
        row += rows
    tensor_size, _, cols = stacks[0].shape
    return pl.pallas_call(
        partial(assemble_kernel, plan),
        out_shape=jax.ShapeDtypeStruct((tensor_size, dp_size, row, cols), stacks[0].dtype),
        in_specs=[pl.BlockSpec(memory_space=pltpu.SMEM)]
        + [pl.BlockSpec(memory_space=pl.ANY)] * len(stacks),
        out_specs=pl.BlockSpec(memory_space=pl.ANY),
        scratch_shapes=[pltpu.SemaphoreType.DMA((len(stacks), tensor_size))],
        name="assemble",
    )(where, *stacks)


def scatter_sum(runs, order, t, i):
    tensor_size, dp_size, r, c = runs.shape
    bits = dp_size.bit_length() - 1
    left = list(range(bits))[::-1]
    current = runs.reshape((tensor_size,) + (2,) * bits + (r, c))
    for bit in order:
        axis = 1 + left.index(bit.bit_length() - 1)
        left.remove(bit.bit_length() - 1)
        mine = (i // bit) % 2
        send = lax.dynamic_index_in_dim(current, 1 - mine, axis, keepdims=False)
        keep = lax.dynamic_index_in_dim(current, mine, axis, keepdims=False)
        got = bit_swap(send, bit)
        current = (keep.astype(f32) + got.astype(f32)).astype(bf16)
    carry = lax.dynamic_index_in_dim(current, (t + tensor_size - 1) % tensor_size, 0, keepdims=False)
    for k in range(2, tensor_size + 1):
        got = ring(carry)
        part = lax.dynamic_index_in_dim(
            current, (t + 2 * tensor_size - k) % tensor_size, 0, keepdims=False
        )
        total = part.astype(f32) + got.astype(f32)
        carry = total.astype(bf16)
    return total


def contract(left, right, dims):
    return lax.dot_general(left, right, ((dims[:1], dims[1:]), ((), ())), preferred_element_type=f32)


def attend_kernel(qkv_ref, other_ref, out_ref, log_ref):
    factor = HEAD_DIM ** (-0.5) * math.log2(math.e)
    q, k, v = qkv_ref[0, 0, 0], qkv_ref[0, 1, 0], qkv_ref[0, 2, 0]
    scores = [contract(keys, q, (0, 0)) for keys in (k, other_ref[0, 0, 0])]
    highest = jnp.max(scores[0], axis=0, keepdims=True)
    for piece in scores[1:]:
        highest = jnp.maximum(highest, jnp.max(piece, axis=0, keepdims=True))
    shift = highest * factor
    total = jnp.zeros_like(shift)
    attended = jnp.zeros(q.shape, f32)
    for piece, values in zip(scores, (v, other_ref[0, 1, 0])):
        weights = jnp.exp2(piece * factor - shift)
        total = total + jnp.sum(weights, axis=0, keepdims=True)
        attended = attended + contract(values, weights.astype(bf16), (1, 0))
    out_ref[0] = (attended / total).astype(bf16)
    log_ref[0] = shift + jnp.log2(total)


def attend(own, other):
    groups, _, heads, size, rows = own.shape
    return pl.pallas_call(
        attend_kernel,
        grid=(groups * heads,),
        in_specs=[
            pl.BlockSpec((1, 3, 1, size, rows), lambda n: (n // heads, 0, n % heads, 0, 0)),
            pl.BlockSpec((1, 2, 1, size, rows), lambda n: (n // heads, 0, n % heads, 0, 0)),
        ],
        out_specs=[
            pl.BlockSpec((1, size, rows), lambda n: (n, 0, 0)),
            pl.BlockSpec((1, 1, rows), lambda n: (n, 0, 0)),
        ],
        out_shape=[
            jax.ShapeDtypeStruct((groups * heads, size, rows), bf16),
            jax.ShapeDtypeStruct((groups * heads, 1, rows), f32),
        ],
        compiler_params=pltpu.CompilerParams(vmem_limit_bytes=VMEM_LIMIT),
        name="attend",
    )(own, other)


def attend_back_kernel(qkv_ref, other_ref, grad_ref, log_ref, own_ref, out_ref):
    scale = HEAD_DIM ** (-0.5)
    factor = scale * math.log2(math.e)
    q, k, v = qkv_ref[0, 0, 0], qkv_ref[0, 1, 0], qkv_ref[0, 2, 0]
    grad, log = grad_ref[0], log_ref[0]
    both = ((k, v), (other_ref[0, 0, 0], other_ref[0, 1, 0]))
    weights = [jnp.exp2(contract(keys, q, (0, 0)) * factor - log) for keys, _ in both]
    grads = [contract(values, grad, (0, 0)) for _, values in both]
    inner = jnp.zeros_like(log)
    for w, g in zip(weights, grads):
        inner = inner + jnp.sum(w * g, axis=0, keepdims=True)
    grad_q = jnp.zeros(q.shape, f32)
    for place, ((keys, _), w, g) in enumerate(zip(both, weights, grads)):
        grad_v = contract(grad, w.astype(bf16), (1, 1))
        grad_scores = (w * (g - inner)).astype(bf16)
        grad_k = contract(q, grad_scores, (1, 1)) * scale
        grad_q = grad_q + contract(keys, grad_scores, (1, 0))
        if place == 0:
            own_ref[0, 1, 0] = grad_k.astype(bf16)
            own_ref[0, 2, 0] = grad_v.astype(bf16)
        else:
            out_ref[0, 0, 0] = grad_k.astype(bf16)
            out_ref[0, 1, 0] = grad_v.astype(bf16)
    own_ref[0, 0, 0] = (grad_q * scale).astype(bf16)


def attend_back(own, other, grad, log):
    groups, _, heads, size, rows = own.shape
    three = pl.BlockSpec((1, 3, 1, size, rows), lambda n: (n // heads, 0, n % heads, 0, 0))
    two = pl.BlockSpec((1, 2, 1, size, rows), lambda n: (n // heads, 0, n % heads, 0, 0))
    return pl.pallas_call(
        attend_back_kernel,
        grid=(groups * heads,),
        in_specs=[
            three,
            two,
            pl.BlockSpec((1, size, rows), lambda n: (n, 0, 0)),
            pl.BlockSpec((1, 1, rows), lambda n: (n, 0, 0)),
        ],
        out_specs=[three, two],
        out_shape=[
            jax.ShapeDtypeStruct(own.shape, bf16),
            jax.ShapeDtypeStruct(other.shape, bf16),
        ],
        compiler_params=pltpu.CompilerParams(vmem_limit_bytes=VMEM_LIMIT),
        name="attend_back",
    )(own, other, grad, log)


def local(tokens, conditioning, master, moment, stats, roots, cotangent):
    dp_size = lax.axis_size("dp")
    tensor_size = lax.axis_size("tensor")
    i, t = lax.axis_index("dp"), lax.axis_index("tensor")
    where = jnp.stack([i, t]).astype(jnp.int32)
    rows, width = tokens.shape
    size = master.shape[1]
    sequences = conditioning.shape[0]
    latents = sequences * dp_size
    heads = HEADS // tensor_size
    shapes = grid_shapes(width, size, tensor_size)
    bits = [1 << b for b in range(1, dp_size.bit_length() - 1)]
    orders = [bits, bits[::-1]]

    low = master.astype(bf16)
    pieces, spans, offset = [], [], 0
    for row_blocks, col_blocks in shapes:
        count = row_blocks * col_blocks // dp_size
        pieces.append(to_dense(low[offset : offset + count], col_blocks))
        spans.append((offset, offset + count))
        offset += count
    w_ada = pieces[4]

    silu_low = jax.nn.silu(conditioning).astype(bf16)
    silu_all = lax.all_gather(silu_low, "dp", axis=0, tiled=True)
    ada_cols = 6 * width // tensor_size
    ada_r, ada_c = w_ada.shape
    ada_per = ada_cols // ada_c
    row_at, col_at = (i // ada_per) * ada_r, (i % ada_per) * ada_c
    silu_mine = lax.dynamic_slice(silu_all, (0, row_at), (latents, ada_r))
    share = jnp.dot(silu_mine, w_ada, preferred_element_type=f32)
    if ada_per > 1:
        share = lax.dynamic_update_slice(jnp.zeros((latents, ada_cols), f32), share, (0, col_at))
    shares = lax.all_to_all(share, "dp", split_axis=0, concat_axis=0, tiled=True)
    own_mods = jnp.sum(shares.reshape(dp_size, sequences, ada_cols), axis=0)
    all_mods = lax.all_gather(own_mods, "tensor", axis=0, tiled=False)
    mine = (t * rows) // LEN
    mods = lax.dynamic_index_in_dim(all_mods, mine, 1, keepdims=False).reshape(6, 1, width)
    shift1, scale1, gate1, shift2, scale2, gate2 = (mods[k] for k in range(6))

    others = pair_swap(tokens)
    weights, after = [], None
    for number in range(4):
        piece = pieces[number]
        if number == 1:
            piece = jnp.pad(piece, ((0, -piece.shape[0] % 16), (0, 0)))
        if after is not None:
            piece, _ = lax.optimization_barrier((piece, after))
        total = piece.shape[0]
        if total >= 144:
            cut = (total // 32 * 16) + 16 if (total // 16) % 2 else total // 2
            parts = [(piece[:cut], orders[0]), (piece[cut:], orders[1])]
        else:
            parts = [(piece, orders[number % 2])]
        streams, after = [], []
        for part, order in parts:
            found, last = gather(part, order)
            streams.append(found)
            after.append(last)
        runs = assemble(streams, dp_size, where)
        row_blocks, col_blocks = shapes[number]
        r = pieces[number].shape[0]
        weights.append(whole_from_runs(runs[:, :, :r], row_blocks * size, col_blocks * size))
    w_qkv, w_out, w_up, w_down = weights
    w_out = w_out.reshape(width, width)

    inputs = tokens.astype(f32)
    normed_one = layer_norm(inputs)
    h1 = (normed_one * (1.0 + scale1) + shift1).astype(bf16)
    h1_other = (layer_norm(others.astype(f32)) * (1.0 + scale1) + shift1).astype(bf16)
    head_cols = heads * HEAD_DIM
    own = jnp.einsum("tdc,rd->tcr", w_qkv, h1, preferred_element_type=f32).astype(bf16)
    own = own.reshape(tensor_size, 3, heads, HEAD_DIM, rows)
    w_kv = w_qkv[:, :, head_cols:]
    other = jnp.einsum("tdc,rd->tcr", w_kv, h1_other, preferred_element_type=f32).astype(bf16)
    other = other.reshape(tensor_size, 2, heads, HEAD_DIM, rows)
    attended, log_totals = attend(own, other)
    attended = attended.reshape(width, rows)
    branch = jnp.einsum("er,ed->rd", attended, w_out, preferred_element_type=f32)
    middle = inputs + gate1 * branch
    normed_two = layer_norm(middle)
    h2 = (normed_two * (1.0 + scale2) + shift2).astype(bf16)
    pre_gelu = jnp.einsum("rd,tdc->trc", h2, w_up, preferred_element_type=f32)
    hidden = jax.nn.gelu(pre_gelu, approximate=True).astype(bf16)
    feed = jnp.einsum("trc,tcd->rd", hidden, w_down, preferred_element_type=f32)
    result = (middle + gate2 * feed).astype(bf16)

    grad_out = cotangent.astype(f32)
    gm = (grad_out * gate2).astype(bf16)
    grad_down = jnp.einsum("trc,rd->tcd", hidden, gm, preferred_element_type=f32).astype(bf16)
    grad_hidden = jnp.einsum("rd,tcd->trc", gm, w_down, preferred_element_type=f32)
    _, gelu_pullback = jax.vjp(partial(jax.nn.gelu, approximate=True), pre_gelu)
    gz = gelu_pullback(grad_hidden)[0].astype(bf16)
    grad_up = jnp.einsum("rd,trc->tdc", h2, gz, preferred_element_type=f32).astype(bf16)
    gh2 = jnp.einsum("trc,tdc->rd", gz, w_up, preferred_element_type=f32)
    gx1 = grad_out + norm_back(middle, gh2 * (1.0 + scale2))
    ga = (gx1 * gate1).astype(bf16)
    go = jnp.einsum("ed,rd->er", w_out, ga, preferred_element_type=f32).astype(bf16)
    grad_wo = jnp.einsum("er,rd->ed", attended, ga, preferred_element_type=f32).astype(bf16)
    grad_wo = grad_wo.reshape(tensor_size, width // tensor_size, width)
    g_own, g_other = attend_back(own, other, go.reshape(HEADS, HEAD_DIM, rows), log_totals)
    g_own = g_own.reshape(tensor_size, 3 * head_cols, rows)
    g_other = g_other.reshape(tensor_size, 2 * head_cols, rows)
    gh1_other = jnp.einsum("tcr,tdc->rd", g_other, w_kv, preferred_element_type=f32)
    gh1 = jnp.einsum("tcr,tdc->rd", g_own, w_qkv, preferred_element_type=f32)
    gh1 = gh1 + pair_swap(gh1_other.astype(bf16)).astype(f32)
    grad_qkv = jnp.einsum("rd,tcr->tdc", h1, g_own, preferred_element_type=f32)
    more = jnp.einsum("rd,tcr->tdc", h1_other, g_other, preferred_element_type=f32)
    grad_qkv = (
        jnp.concatenate([grad_qkv[:, :, :head_cols], grad_qkv[:, :, head_cols:] + more], axis=2)
    ).astype(bf16)
    grad_tokens = gx1 + norm_back(inputs, gh1 * (1.0 + scale1))

    grad_mods = jnp.stack(
        [
            jnp.sum(gh1, axis=0),
            jnp.sum(gh1 * normed_one, axis=0),
            jnp.sum(gx1 * branch, axis=0),
            jnp.sum(gh2, axis=0),
            jnp.sum(gh2 * normed_two, axis=0),
            jnp.sum(grad_out * feed, axis=0),
        ]
    ).reshape(tensor_size, ada_cols)
    grad_mods = lax.all_to_all(grad_mods, "tensor", split_axis=0, concat_axis=0, tiled=True)
    grad_mods = jnp.sum(grad_mods.reshape(sequences, tensor_size // sequences, ada_cols), axis=1)
    grad_mods = lax.all_gather(grad_mods, "dp", axis=0, tiled=True)
    grad_mods = lax.dynamic_slice(grad_mods, (0, col_at), (latents, ada_c))
    grad_ada = jnp.einsum("sr,sc->rc", silu_mine.astype(f32), grad_mods, precision=HIGHEST)
    grad_silu = jnp.einsum("sc,rc->sr", grad_mods, w_ada.astype(f32), precision=HIGHEST)
    grad_silu = lax.dynamic_update_slice(jnp.zeros((latents, width), f32), grad_silu, (0, row_at))
    grad_silu = lax.all_to_all(grad_silu, "dp", split_axis=0, concat_axis=0, tiled=True)
    grad_silu = jnp.sum(grad_silu.reshape(dp_size, sequences, width), axis=0)
    grad_silu = lax.psum(grad_silu, "tensor")
    _, silu_pullback = jax.vjp(jax.nn.silu, conditioning)
    grad_conditioning = silu_pullback(grad_silu)[0]

    summed = [None] * 5
    for number, whole in ((3, grad_down), (2, grad_up), (1, grad_wo), (0, grad_qkv)):
        r, c = pieces[number].shape
        runs = runs_from_whole(whole, dp_size, r, c)
        if r >= 144:
            cut = (r // 32 * 16) + 16 if (r // 16) % 2 else r // 2
            parts = [(runs[:, :, :cut], orders[0]), (runs[:, :, cut:], orders[1])]
        else:
            parts = [(runs, orders[number % 2])]
        done = [scatter_sum(part, [1] + order[::-1], t, i) for part, order in parts]
        summed[number] = to_blocks(jnp.concatenate(done, axis=0), size)
    summed[4] = to_blocks(grad_ada, size)

    masters, moments, lefts, rights = [], [], [], []
    for (low_at, high_at), grads in zip(spans, summed):
        left = 0.5 * stats[0, low_at:high_at] + 0.5 * jnp.einsum("nij,nkj->nik", grads, grads)
        right = 0.5 * stats[1, low_at:high_at] + 0.5 * jnp.einsum("nji,njk->nik", grads, grads)
        new_moment = momentum_decay * moment[low_at:high_at] + (1.0 - momentum_decay) * grads
        update = jnp.einsum("nij,njk->nik", roots[0, low_at:high_at], new_moment)
        update = jnp.einsum("nij,njk->nik", update, roots[1, low_at:high_at])
        masters.append(master[low_at:high_at] - learning_rate * update)
        moments.append(new_moment)
        lefts.append(left)
        rights.append(right)
    return (
        result,
        grad_tokens,
        grad_conditioning,
        jnp.concatenate(masters),
        jnp.concatenate(moments),
        jnp.stack([jnp.concatenate(lefts), jnp.concatenate(rights)]),
    )


def solution(mesh):
    both = ("dp", "tensor")
    rows, blocks, pairs = P(both, None), P(both, None, None), P(None, both, None, None)
    return jax.shard_map(
        local,
        mesh=mesh,
        in_specs=(rows, P("dp", None), blocks, blocks, pairs, pairs, rows),
        out_specs=(rows, rows, P("dp", None), blocks, blocks, pairs),
        check_vma=False,
    )
```

time: 1600 us -> 1850 us (1.16)
  Pallas kernels: 0 us -> 1050 us
  waiting for transfers between devices: 807 us -> 277 us
  local copies, waits for them, and re-layouts: 360 us -> 123 us
  matrix products: 282 us -> 188 us
  starting transfers between devices: 1.13 us -> 65.9 us
  blocking collectives: 23.8 us -> 43.7 us
    pallas_call x0 -> x6, Pallas kernels: none -> 1050 us  [the longest x4 1000 us: assemble(): pl.pallas_call(partial(assemble_kernel, plan), out_shape=jax.ShapeDtypeSt...]
    reduce_scatter x5 -> x0, waiting for transfers between devices: 412 us -> none  [the longest x1 202 us: local(): summed = lax.psum_scatter(stacked, 'dp', scatter_dimension=0, tiled=True)[0]]
    all_gather x5 -> x0, waiting for transfers between devices: 366 us -> none  [the longest x1 111 us: local(): gathered = lax.all_gather(low_master, 'dp', axis=0, tiled=True)]
    ppermute x0 -> x114, waiting for transfers between devices: none -> 273 us  [the longest x42 157 us: ring(): lax.ppermute(values, 'tensor', [(k, (k + 1) % size) for k in range(size)])]
    dot_general x20 -> x2, local copies, waits for them, and re-layouts: 131 us -> 0.73 us  [local(): share = jnp.dot(silu_mine, w_ada, preferred_element_type=f32)]
    dot_general x35 -> x33, matrix products: 282 us -> 188 us  [the longest x5 19.7 us: local(): update = jnp.einsum('nij,njk->nik', update, roots[1, low_at:high_at])]
    ppermute x0 -> x114, starting transfers between devices: none -> 55.1 us  [the longest x70 40.9 us: bit_swap(): return lax.ppermute(values, 'dp', [(k, k ^ bit) for k in range(size)])]
    unnamed x133 -> x217, local copies, waits for them, and re-layouts: 55.4 us -> 13.2 us
  transfers between devices with their start and end apart: 11 -> 117, of which waited for: 10 -> 51; matrix products, arithmetic and copies ran while one was open for 18% -> 17% of each run, Pallas kernels for 0% -> 57%
where the time goes in v1:
time: 1850 us; the launch traced here: 1830 us
  Pallas kernels  1050 us (57%)
  waiting for transfers between devices  277 us (15%)
  matrix products  188 us (10%)
  local copies, waits for them, and re-layouts  123 us (7%)
  other arithmetic  80.8 us (4%)
  starting transfers between devices  65.9 us (4%)
  blocking collectives  43.7 us (2%)
    pallas_call x4, Pallas kernels, assemble(): pl.pallas_call(partial(assemble_kernel, plan), out_shape=jax.ShapeDtypeSt...  1000 us
    ppermute x42, waiting for transfers between devices, ring(): lax.ppermute(values, 'tensor', [(k, (k + 1) % size) for k in range(size)])  157 us
    ppermute x70, waiting for transfers between devices, bit_swap(): return lax.ppermute(values, 'dp', [(k, k ^ bit) for k in range(size)])  107 us
    ppermute x70, starting transfers between devices, bit_swap(): return lax.ppermute(values, 'dp', [(k, k ^ bit) for k in range(size)])  40.9 us
  transfers between devices with their start and end apart: 117, of which 51 were waited for; matrix products, arithmetic and copies ran while one was open for 17% of the time, Pallas kernels for 57%

profile of v1, /device:TPU:0, one launch (start us, length us, event | category | flops | bytes accessed | tf_op | source)
XLA Modules:
  0.0 1834.6 jit_solution(17267499715272487494)
XLA Ops:
  11.4 9.2 all-gather.1
  34.3 25.3 %collective-permute-done.11 = bf16[64,864]{1,0:T(8,128)(2,1)} collective-permute-done((bf16[64,864]{1,0:T(8,128)(2,1)}, bf16[64,864]{1,0:T(8,128)(2,1)}, u32[]{:S(2)}, u32[]{:S(2)}) %collective-permute-start.11) | collective-permute-done | bytes 110624 | tf_op jit(solution)/shard_map/ppermute | solution.py:92
  69.5 6.6 collective-permute-done.21
  92.8 6.2 collective-permute-done.41
  107.5 14.5 all-gather.2
  128.6 6.7 collective-permute-done.33
  153.2 7.9 collective-permute-done.15.refs_11_
  162.4 6.8 collective-permute-done.61
  171.3 7.8 collective-permute-done.51
  181.4 5.4 collective-permute-done.52
  197.0 101.3 %assemble.5 = bf16[4,8,80,576]{3,2,1,0:T(8,128)(2,1)} custom-call(s32[2]{0:T(128)} %pad_add_fusion.where, bf16[4,80,576]{2,1,0:T(8,128)(2,1)} %copy-done.39, bf16[4,80,576]{2,1,0:T(8,128)(2,1)} %copy-done.65, bf16[4,80,576]{2,1,0:T(8,128)(2,1)} %copy-done.66, bf16[4,80,576]{2,1,0:T(8,128)(2,1)} %copy-done.68, bf16[4,80,576]{2,1,0:T(8,128)(2,1)} %copy-done.67, ...), custom_call_target="tpu_custom_call" | custom-call | tf_op jit(solution)/shard_map/assemble/pallas_call | solution.py:140
  304.0 6.8 reshape_reshape.9
  314.2 252.5 %assemble.4 = bf16[4,8,144,864]{3,2,1,0:T(8,128)(2,1)} custom-call(s32[2]{0:T(128)} %pad_add_fusion.where, bf16[4,80,864]{2,1,0:T(8,128)(2,1)} %copy-done.37, bf16[4,80,864]{2,1,0:T(8,128)(2,1)} %copy-done.53, bf16[4,80,864]{2,1,0:T(8,128)(2,1)} %copy-done.54, bf16[4,80,864]{2,1,0:T(8,128)(2,1)} %collective-permute-done.5.refs_3_, ...), custom_call_target="tpu_custom_call" | custom-call | tf_op jit(solution)/shard_map/assemble/pallas_call | solution.py:140
  568.5 10.1 convolution_convert_fusion.4
  583.4 8.5 fusion.58
  591.9 19.6 %attend.1 = (bf16[16,72,512]{2,1,0:T(8,128)(2,1)}, f32[16,1,512]{2,1,0:T(1,128)}) custom-call(bf16[4,3,4,72,512]{4,3,2,1,0:T(8,128)(2,1)} %bitcast.516, bf16[4,2,4,72,512]{4,3,2,1,0:T(8,128)(2,1)} %bitcast.533), custom_call_target="tpu_custom_call" | custom-call | tf_op jit(solution)/shard_map/attend/pallas_call | solution.py:199
  620.9 324.0 %assemble.6 = bf16[4,8,144,1152]{3,2,1,0:T(8,128)(2,1)} custom-call(s32[2]{0:T(128)} %pad_add_fusion.where, bf16[4,80,1152]{2,1,0:T(8,128)(2,1)} %pad_maximum_fusion.2.refs_0_, bf16[4,80,1152]{2,1,0:T(8,128)(2,1)} %collective-permute-done.34.refs_1_, bf16[4,80,1152]{2,1,0:T(8,128)(2,1)} %collective-permute-done.35.refs_2_, ...), custom_call_target="tpu_custom_call" | custom-call | tf_op jit(solution)/shard_map/assemble/pallas_call | solution.py:140
  947.1 12.3 fusion.199
  965.7 11.3 convolution_convert_fusion
  985.1 324.0 %assemble.7 = bf16[4,8,144,1152]{3,2,1,0:T(8,128)(2,1)} custom-call(s32[2]{0:T(128)} %pad_add_fusion.where, bf16[4,80,1152]{2,1,0:T(8,128)(2,1)} %copy-done.29, bf16[4,80,1152]{2,1,0:T(8,128)(2,1)} %collective-permute-done.54.refs_1_, bf16[4,80,1152]{2,1,0:T(8,128)(2,1)} %collective-permute-done.55.refs_2_, bf16[4,80,1152]{2,1,0:T(8,128)(2,1)} %copy-done.45, ...), custom_call_target="tpu_custom_call" | custom-call | tf_op jit(solution)/shard_map/assemble/pallas_call | solution.py:140
  1309.0 17.8 fusion.7
  1326.8 13.3 multiply_reduce_fusion
  1340.2 12.4 fusion.54
  1358.6 31.2 %attend_back.1 = (bf16[4,3,4,72,512]{4,3,2,1,0:T(8,128)(2,1)}, bf16[4,2,4,72,512]{4,3,2,1,0:T(8,128)(2,1)}) custom-call(bf16[4,3,4,72,512]{4,3,2,1,0:T(8,128)(2,1)} %bitcast.517, bf16[4,2,4,72,512]{4,3,2,1,0:T(8,128)(2,1)} %bitcast.534, bf16[16,72,512]{2,1,0:T(8,128)(2,1)} %bitcast.557, f32[16,1,512]{2,1,0:T(1,128)} %get-tuple-element.17.log_ref), custom_call_target="tpu_custom_call" | custom-call | tf_op jit(solution)/shard_map/attend_back/pallas_call | solution.py:249
  1389.9 7.0 convolution_bitcast_fusion
  1399.5 6.6 fusion
  1406.2 8.5 copy.139
  1419.5 6.0 fusion.20
  1428.9 9.0 convolution_convert_fusion.1
  1443.9 9.4 fusion.27
  1453.3 7.8 reshape_reshape.10
  1472.5 6.6 constant_dynamic-slice_fusion.1
  1486.1 8.9 collective-permute-done.71
  1495.0 10.7 fusion.47
  1515.5 8.4 all-gather.3
  1535.7 11.5 psum.7
  1553.3 12.6 collective-permute-done.85
  1570.4 6.8 collective-permute-done.86
  1608.6 8.9 collective-permute-done.80
  1644.1 7.0 collective-permute-done.109
  1653.6 8.4 collective-permute-done.74
  1669.5 27.7 %collective-permute-done.98 = bf16[4,64,1152]{2,1,0:T(8,128)(2,1)S(1)} collective-permute-done((bf16[4,64,1152]{2,1,0:T(8,128)(2,1)S(1)}, bf16[4,64,1152]{2,1,0:T(8,128)(2,1)S(1)}, u32[]{:S(2)}, u32[]{:S(2)}) %collective-permute-start.98) | collective-permute-done | bytes 589856 | tf_op jit(solution)/shard_map/ppermute | solution.py:87
  1697.4 7.0 collective-permute-done.110
  1706.6 5.6 collective-permute-done.111
  1749.2 8.1 collective-permute-done.105
  1757.9 6.9 collective-permute-done.106
  1766.9 5.3 collective-permute-done.107
  1825.2 8.9 pad_maximum_fusion
  (631 shorter events, 375.8 us)
Async XLA Ops:
  5.1 26.7 %collective-permute-start = (bf16[80,864]{1,0:T(8,128)(2,1)}, bf16[80,864]{1,0:T(8,128)(2,1)}, u32[]{:S(2)}, u32[]{:S(2)}) collective-permute-start(bf16[80,864]{1,0:T(8,128)(2,1)} %get-tuple-element.61), channel_id=1, source_target_pairs={{0,1},{1,2},{2,3},{3,0},{4,5},{5,6},{6,7},{7,4},{8,9},{9,10},{10,1... | collective-permute-start | bytes 414728 | tf_op jit(solution)/shard_map/ppermute | solution.py:92
  24.2 81.6 %all-to-all-start = ((f32[8,2,1728]{2,1,0:T(2,128)}), f32[8,2,1728]{2,1,0:T(2,128)S(1)}, u32[]{:S(2)}, u32[]{:S(2)}) async-start(f32[8,2,1728]{2,1,0:T(2,128)} %copy.126), calls=%async_computation | async-start | bytes 229376 | tf_op jit(solution)/shard_map/all_to_all | solution.py:301
  27.6 99.7 %collective-permute-start.20 = (bf16[512,1152]{1,0:T(8,128)(2,1)S(1)}, bf16[512,1152]{1,0:T(8,128)(2,1)}, u32[]{:S(2)}, u32[]{:S(2)}) collective-permute-start(bf16[512,1152]{1,0:T(8,128)(2,1)S(1)} %copy-done.3), channel_id=1, source_target_pairs={{0,1},{1,0},{2,3},{3,2},{4,5},{5,4},{6,7},{7,6},{8,9},{9,8},{10,11... | collective-permute-start | bytes 3538952 | tf_op jit(solution)/shard_map/ppermute | solution.py:97
  31.3 28.3 %collective-permute-start.11 = (bf16[64,864]{1,0:T(8,128)(2,1)}, bf16[64,864]{1,0:T(8,128)(2,1)}, u32[]{:S(2)}, u32[]{:S(2)}) collective-permute-start(bf16[64,864]{1,0:T(8,128)(2,1)} %collective-permute-done.10), channel_id=1, source_target_pairs={{0,1},{1,2},{2,3},{3,0},{4,5},{5,6},{6,7},{7,4},{8,9},{9,10},{10,1... | collective-permute-start | bytes 331784 | tf_op jit(solution)/shard_map/ppermute | solution.py:92
  31.8 30.2 %collective-permute-start.1 = (bf16[80,864]{1,0:T(8,128)(2,1)}, bf16[80,864]{1,0:T(8,128)(2,1)S(1)}, u32[]{:S(2)}, u32[]{:S(2)}) collective-permute-start(bf16[80,864]{1,0:T(8,128)(2,1)} %collective-permute-done), channel_id=1, source_target_pairs={{0,1},{1,2},{2,3},{3,0},{4,5},{5,6},{6,7},{7,4},{8,9},{9,10},{10,1... | collective-permute-start | bytes 414728 | tf_op jit(solution)/shard_map/ppermute | solution.py:92
  84.7 38.6 %collective-permute-start.13 = (bf16[4,64,864]{2,1,0:T(8,128)(2,1)}, bf16[4,64,864]{2,1,0:T(8,128)(2,1)}, u32[]{:S(2)}, u32[]{:S(2)}) collective-permute-start(bf16[4,64,864]{2,1,0:T(8,128)(2,1)} %pad_maximum_fusion.10.refs_8_), channel_id=1, source_target_pairs={{0,16},{4,20},{8,24},{12,28},{16,0},{20,4},{24,8},{28,12},{1,17},{... | collective-permute-start | bytes 1327112 | tf_op jit(solution)/shard_map/ppermute | solution.py:87
  86.6 38.3 %collective-permute-start.14 = (bf16[4,64,864]{2,1,0:T(8,128)(2,1)}, bf16[4,64,864]{2,1,0:T(8,128)(2,1)}, u32[]{:S(2)}, u32[]{:S(2)}) collective-permute-start(bf16[4,64,864]{2,1,0:T(8,128)(2,1)} %pad_maximum_fusion.10.refs_8_), channel_id=1, source_target_pairs={{0,8},{4,12},{8,0},{12,4},{16,24},{20,28},{24,16},{28,20},{1,9},{5... | collective-permute-start | bytes 1327112 | tf_op jit(solution)/shard_map/ppermute | solution.py:87
  102.9 23.5 %collective-permute-start.32 = (bf16[80,1152]{1,0:T(8,128)(2,1)S(1)}, bf16[80,1152]{1,0:T(8,128)(2,1)S(1)}, u32[]{:S(2)}, u32[]{:S(2)}) collective-permute-start(bf16[80,1152]{1,0:T(8,128)(2,1)S(1)} %collective-permute-done.31), channel_id=1, source_target_pairs={{0,1},{1,2},{2,3},{3,0},{4,5},{5,6},{6,7},{7,4},{8,9},{9,10},{10,1... | collective-permute-start | bytes 552968 | tf_op jit(solution)/shard_map/ppermute | solution.py:92
  151.1 29.8 %collective-permute-start.5 = (bf16[4,80,864]{2,1,0:T(8,128)(2,1)S(1)}, bf16[4,80,864]{2,1,0:T(8,128)(2,1)}, u32[]{:S(2)}, u32[]{:S(2)}) collective-permute-start(bf16[4,80,864]{2,1,0:T(8,128)(2,1)S(1)} %collective-permute-done.3.refs_1_), channel_id=1, source_target_pairs={{0,16},{4,20},{8,24},{12,28},{16,0},{20,4},{24,8},{28,12},{1,17},{... | collective-permute-start | bytes 1658888 | tf_op jit(solution)/shard_map/ppermute | solution.py:87
  187.3 379.5 %collective-permute-start.44 = (bf16[4,64,1152]{2,1,0:T(8,128)(2,1)S(1)}, bf16[4,64,1152]{2,1,0:T(8,128)(2,1)}, u32[]{:S(2)}, u32[]{:S(2)}) collective-permute-start(bf16[4,64,1152]{2,1,0:T(8,128)(2,1)S(1)} %pad_maximum_fusion.6.refs_8_), channel_id=1, source_target_pairs={{0,16},{4,20},{8,24},{12,28},{16,0},{20,4},{24,8},{28,12},{1,17},{... | collective-permute-start | bytes 1769480 | tf_op jit(solution)/shard_map/ppermute | solution.py:87
  188.8 378.0 %collective-permute-start.45 = (bf16[4,64,1152]{2,1,0:T(8,128)(2,1)S(1)}, bf16[4,64,1152]{2,1,0:T(8,128)(2,1)}, u32[]{:S(2)}, u32[]{:S(2)}) collective-permute-start(bf16[4,64,1152]{2,1,0:T(8,128)(2,1)S(1)} %pad_maximum_fusion.6.refs_8_), channel_id=1, source_target_pairs={{0,8},{4,12},{8,0},{12,4},{16,24},{20,28},{24,16},{28,20},{1,9},{5... | collective-permute-start | bytes 1769480 | tf_op jit(solution)/shard_map/ppermute | solution.py:87
  189.9 378.5 %collective-permute-start.47 = (bf16[4,64,1152]{2,1,0:T(8,128)(2,1)S(1)}, bf16[4,64,1152]{2,1,0:T(8,128)(2,1)}, u32[]{:S(2)}, u32[]{:S(2)}) collective-permute-start(bf16[4,64,1152]{2,1,0:T(8,128)(2,1)S(1)} %pad_maximum_fusion.6.refs_8_), channel_id=1, source_target_pairs={{0,4},{4,0},{8,12},{12,8},{16,20},{20,16},{24,28},{28,24},{1,5},{5... | collective-permute-start | bytes 1769480 | tf_op jit(solution)/shard_map/ppermute | solution.py:87
  195.2 117.5 %collective-permute-start.9 = (bf16[4,80,864]{2,1,0:T(8,128)(2,1)}, bf16[4,80,864]{2,1,0:T(8,128)(2,1)}, u32[]{:S(2)}, u32[]{:S(2)}) collective-permute-start(bf16[4,80,864]{2,1,0:T(8,128)(2,1)} %collective-permute-done.5.refs_3_), channel_id=1, source_target_pairs={{0,4},{4,0},{8,12},{12,8},{16,20},{20,16},{24,28},{28,24},{1,5},{5... | collective-permute-start | bytes 1658888 | tf_op jit(solution)/shard_map/ppermute | solution.py:87
  196.2 115.9 %collective-permute-start.19 = (bf16[4,64,864]{2,1,0:T(8,128)(2,1)}, bf16[4,64,864]{2,1,0:T(8,128)(2,1)}, u32[]{:S(2)}, u32[]{:S(2)}) collective-permute-start(bf16[4,64,864]{2,1,0:T(8,128)(2,1)} %collective-permute-done.15.refs_11_), channel_id=1, source_target_pairs={{0,4},{4,0},{8,12},{12,8},{16,20},{20,16},{24,28},{28,24},{1,5},{5... | collective-permute-start | bytes 1327112 | tf_op jit(solution)/shard_map/ppermute | solution.py:87
  312.1 266.5 %collective-permute-start.34 = (bf16[4,80,1152]{2,1,0:T(8,128)(2,1)}, bf16[4,80,1152]{2,1,0:T(8,128)(2,1)}, u32[]{:S(2)}, u32[]{:S(2)}) collective-permute-start(bf16[4,80,1152]{2,1,0:T(8,128)(2,1)} %pad_maximum_fusion.2.refs_0_), channel_id=1, source_target_pairs={{0,8},{4,12},{8,0},{12,4},{16,24},{20,28},{24,16},{28,20},{1,9},{5... | collective-permute-start | bytes 2211848 | tf_op jit(solution)/shard_map/ppermute | solution.py:87
  312.7 266.3 %collective-permute-start.35 = (bf16[4,80,1152]{2,1,0:T(8,128)(2,1)}, bf16[4,80,1152]{2,1,0:T(8,128)(2,1)}, u32[]{:S(2)}, u32[]{:S(2)}) collective-permute-start(bf16[4,80,1152]{2,1,0:T(8,128)(2,1)} %pad_maximum_fusion.2.refs_0_), channel_id=1, source_target_pairs={{0,16},{4,20},{8,24},{12,28},{16,0},{20,4},{24,8},{28,12},{1,17},{... | collective-permute-start | bytes 2211848 | tf_op jit(solution)/shard_map/ppermute | solution.py:87
  578.7 32.8 %collective-permute-start.49 = (bf16[4,64,1152]{2,1,0:T(8,128)(2,1)}, bf16[4,64,1152]{2,1,0:T(8,128)(2,1)S(1)}, u32[]{:S(2)}, u32[]{:S(2)}) collective-permute-start(bf16[4,64,1152]{2,1,0:T(8,128)(2,1)} %collective-permute-done.45.refs_10_), channel_id=1, source_target_pairs={{0,4},{4,0},{8,12},{12,8},{16,20},{20,16},{24,28},{28,24},{1,5},{5... | collective-permute-start | bytes 1769480 | tf_op jit(solution)/shard_map/ppermute | solution.py:87
  579.0 34.0 %collective-permute-start.36 = (bf16[4,80,1152]{2,1,0:T(8,128)(2,1)}, bf16[4,80,1152]{2,1,0:T(8,128)(2,1)}, u32[]{:S(2)}, u32[]{:S(2)}) collective-permute-start(bf16[4,80,1152]{2,1,0:T(8,128)(2,1)} %collective-permute-done.34.refs_1_), channel_id=1, source_target_pairs={{0,16},{4,20},{8,24},{12,28},{16,0},{20,4},{24,8},{28,12},{1,17},{... | collective-permute-start | bytes 2211848 | tf_op jit(solution)/shard_map/ppermute | solution.py:87
  579.6 38.1 %collective-permute-start.38 = (bf16[4,80,1152]{2,1,0:T(8,128)(2,1)}, bf16[4,80,1152]{2,1,0:T(8,128)(2,1)}, u32[]{:S(2)}, u32[]{:S(2)}) collective-permute-start(bf16[4,80,1152]{2,1,0:T(8,128)(2,1)} %collective-permute-done.34.refs_1_), channel_id=1, source_target_pairs={{0,4},{4,0},{8,12},{12,8},{16,20},{20,16},{24,28},{28,24},{1,5},{5... | collective-permute-start | bytes 2211848 | tf_op jit(solution)/shard_map/ppermute | solution.py:87
  582.9 35.3 %collective-permute-start.39 = (bf16[4,80,1152]{2,1,0:T(8,128)(2,1)}, bf16[4,80,1152]{2,1,0:T(8,128)(2,1)}, u32[]{:S(2)}, u32[]{:S(2)}) collective-permute-start(bf16[4,80,1152]{2,1,0:T(8,128)(2,1)} %collective-permute-done.35.refs_2_), channel_id=1, source_target_pairs={{0,4},{4,0},{8,12},{12,8},{16,20},{20,16},{24,28},{28,24},{1,5},{5... | collective-permute-start | bytes 2211848 | tf_op jit(solution)/shard_map/ppermute | solution.py:87
  582.9 36.1 %collective-permute-start.50 = (bf16[4,64,1152]{2,1,0:T(8,128)(2,1)}, bf16[4,64,1152]{2,1,0:T(8,128)(2,1)}, u32[]{:S(2)}, u32[]{:S(2)}) collective-permute-start(bf16[4,64,1152]{2,1,0:T(8,128)(2,1)} %collective-permute-done.46.refs_11_), channel_id=1, source_target_pairs={{0,4},{4,0},{8,12},{12,8},{16,20},{20,16},{24,28},{28,24},{1,5},{5... | collective-permute-start | bytes 1769480 | tf_op jit(solution)/shard_map/ppermute | solution.py:87
  611.5 335.0 %collective-permute-start.54 = (bf16[4,80,1152]{2,1,0:T(8,128)(2,1)S(1)}, bf16[4,80,1152]{2,1,0:T(8,128)(2,1)}, u32[]{:S(2)}, u32[]{:S(2)}) collective-permute-start(bf16[4,80,1152]{2,1,0:T(8,128)(2,1)S(1)} %pad_maximum_fusion.3.refs_0_), channel_id=1, source_target_pairs={{0,8},{4,12},{8,0},{12,4},{16,24},{20,28},{24,16},{28,20},{1,9},{5... | collective-permute-start | bytes 2211848 | tf_op jit(solution)/shard_map/ppermute | solution.py:87
  617.7 327.2 %collective-permute-start.64 = (bf16[4,64,1152]{2,1,0:T(8,128)(2,1)S(1)}, bf16[4,64,1152]{2,1,0:T(8,128)(2,1)}, u32[]{:S(2)}, u32[]{:S(2)}) collective-permute-start(bf16[4,64,1152]{2,1,0:T(8,128)(2,1)S(1)} %pad_maximum_fusion.7.refs_8_), channel_id=1, source_target_pairs={{0,16},{4,20},{8,24},{12,28},{16,0},{20,4},{24,8},{28,12},{1,17},{... | collective-permute-start | bytes 1769480 | tf_op jit(solution)/shard_map/ppermute | solution.py:87
  618.2 327.0 %collective-permute-start.65 = (bf16[4,64,1152]{2,1,0:T(8,128)(2,1)S(1)}, bf16[4,64,1152]{2,1,0:T(8,128)(2,1)}, u32[]{:S(2)}, u32[]{:S(2)}) collective-permute-start(bf16[4,64,1152]{2,1,0:T(8,128)(2,1)S(1)} %pad_maximum_fusion.7.refs_8_), channel_id=1, source_target_pairs={{0,8},{4,12},{8,0},{12,4},{16,24},{20,28},{24,16},{28,20},{1,9},{5... | collective-permute-start | bytes 1769480 | tf_op jit(solution)/shard_map/ppermute | solution.py:87
  619.0 327.6 %collective-permute-start.67 = (bf16[4,64,1152]{2,1,0:T(8,128)(2,1)S(1)}, bf16[4,64,1152]{2,1,0:T(8,128)(2,1)S(1)}, u32[]{:S(2)}, u32[]{:S(2)}) collective-permute-start(bf16[4,64,1152]{2,1,0:T(8,128)(2,1)S(1)} %pad_maximum_fusion.7.refs_8_), channel_id=1, source_target_pairs={{0,4},{4,0},{8,12},{12,8},{16,20},{20,16},{24,28},{28,24},{1,5},{5... | collective-permute-start | bytes 1769480 | tf_op jit(solution)/shard_map/ppermute | solution.py:87
  619.6 339.9 %collective-permute-start.55 = (bf16[4,80,1152]{2,1,0:T(8,128)(2,1)S(1)}, bf16[4,80,1152]{2,1,0:T(8,128)(2,1)}, u32[]{:S(2)}, u32[]{:S(2)}) collective-permute-start(bf16[4,80,1152]{2,1,0:T(8,128)(2,1)S(1)} %pad_maximum_fusion.3.refs_0_), channel_id=1, source_target_pairs={{0,16},{4,20},{8,24},{12,28},{16,0},{20,4},{24,8},{28,12},{1,17},{... | collective-permute-start | bytes 2211848 | tf_op jit(solution)/shard_map/ppermute | solution.py:87
  959.5 24.2 %collective-permute-start.69 = (bf16[4,64,1152]{2,1,0:T(8,128)(2,1)}, bf16[4,64,1152]{2,1,0:T(8,128)(2,1)}, u32[]{:S(2)}, u32[]{:S(2)}) collective-permute-start(bf16[4,64,1152]{2,1,0:T(8,128)(2,1)} %collective-permute-done.65.refs_10_), channel_id=1, source_target_pairs={{0,4},{4,0},{8,12},{12,8},{16,20},{20,16},{24,28},{28,24},{1,5},{5... | collective-permute-start | bytes 1769480 | tf_op jit(solution)/shard_map/ppermute | solution.py:87
  959.7 24.2 %collective-permute-start.58 = (bf16[4,80,1152]{2,1,0:T(8,128)(2,1)}, bf16[4,80,1152]{2,1,0:T(8,128)(2,1)S(1)}, u32[]{:S(2)}, u32[]{:S(2)}) collective-permute-start(bf16[4,80,1152]{2,1,0:T(8,128)(2,1)} %collective-permute-done.54.refs_1_), channel_id=1, source_target_pairs={{0,4},{4,0},{8,12},{12,8},{16,20},{20,16},{24,28},{28,24},{1,5},{5... | collective-permute-start | bytes 2211848 | tf_op jit(solution)/shard_map/ppermute | solution.py:87
  983.7 602.7 %collective-permute-start.102 = (bf16[4,2,2,80,1152]{4,3,2,1,0:T(8,128)(2,1)}, bf16[4,2,2,80,1152]{4,3,2,1,0:T(8,128)(2,1)}, u32[]{:S(2)}, u32[]{:S(2)}) collective-permute-start(bf16[4,2,2,80,1152]{4,3,2,1,0:T(8,128)(2,1)} %dynamic-slice_bitcast_fusion), channel_id=1, source_target_pairs={{0,4},{4,0},{8,12},{12,8},{16,20},{20,16},{24,28},{28,24},{1,5},{5... | collective-permute-start | bytes 8847368 | tf_op jit(solution)/shard_map/ppermute | solution.py:87
  1466.3 81.0 %collective-permute-start.84 = (bf16[4,2,2,72,576]{4,3,2,1,0:T(8,128)(2,1)}, bf16[4,2,2,72,576]{4,3,2,1,0:T(8,128)(2,1)}, u32[]{:S(2)}, u32[]{:S(2)}) collective-permute-start(bf16[4,2,2,72,576]{4,3,2,1,0:T(8,128)(2,1)} %dynamic-slice_bitcast_fusion.6), channel_id=1, source_target_pairs={{0,4},{4,0},{8,12},{12,8},{16,20},{20,16},{24,28},{28,24},{1,5},{5... | collective-permute-start | bytes 3981320 | tf_op jit(solution)/shard_map/ppermute | solution.py:87
  1466.6 28.4 %collective-permute-start.71 = (bf16[512,1152]{1,0:T(8,128)(2,1)}, bf16[512,1152]{1,0:T(8,128)(2,1)}, u32[]{:S(2)}, u32[]{:S(2)}) collective-permute-start(bf16[512,1152]{1,0:T(8,128)(2,1)} %fusion.27), channel_id=1, source_target_pairs={{0,1},{1,0},{2,3},{3,2},{4,5},{5,4},{6,7},{7,6},{8,9},{9,8},{10,11... | collective-permute-start | bytes 3538952 | tf_op jit(solution)/shard_map/ppermute | solution.py:97
  1468.2 97.9 %collective-permute-start.72 = (bf16[4,2,2,80,864]{4,3,2,1,0:T(8,128)(2,1)}, bf16[4,2,2,80,864]{4,3,2,1,0:T(8,128)(2,1)}, u32[]{:S(2)}, u32[]{:S(2)}) collective-permute-start(bf16[4,2,2,80,864]{4,3,2,1,0:T(8,128)(2,1)} %dynamic-slice_bitcast_fusion.2), channel_id=1, source_target_pairs={{0,4},{4,0},{8,12},{12,8},{16,20},{20,16},{24,28},{28,24},{1,5},{5... | collective-permute-start | bytes 6635528 | tf_op jit(solution)/shard_map/ppermute | solution.py:87
  1472.2 78.8 %collective-permute-start.78 = (bf16[4,2,2,64,864]{4,3,0,1,2:T(8,128)(2,1)}, bf16[4,2,2,64,864]{4,3,0,1,2:T(8,128)(2,1)}, u32[]{:S(2)}, u32[]{:S(2)}) collective-permute-start(bf16[4,2,2,64,864]{4,3,0,1,2:T(8,128)(2,1)} %copy.144), channel_id=1, source_target_pairs={{0,4},{4,0},{8,12},{12,8},{16,20},{20,16},{24,28},{28,24},{1,5},{5... | collective-permute-start | bytes 5308424 | tf_op jit(solution)/shard_map/ppermute | solution.py:87
  1495.0 83.2 %collective-permute-start.96 = (bf16[4,2,2,64,1152]{4,3,0,1,2:T(8,128)(2,1)}, bf16[4,2,2,64,1152]{4,3,0,1,2:T(8,128)(2,1)}, u32[]{:S(2)}, u32[]{:S(2)}) collective-permute-start(bf16[4,2,2,64,1152]{4,3,0,1,2:T(8,128)(2,1)} %bitcast.468), channel_id=1, source_target_pairs={{0,4},{4,0},{8,12},{12,8},{16,20},{20,16},{24,28},{28,24},{1,5},{5... | collective-permute-start | bytes 7077896 | tf_op jit(solution)/shard_map/ppermute | solution.py:87
  1551.0 31.6 %collective-permute-start.108 = (bf16[4,2,2,64,1152]{4,3,0,1,2:T(8,128)(2,1)S(1)}, bf16[4,2,2,64,1152]{4,3,0,1,2:T(8,128)(2,1)S(1)}, u32[]{:S(2)}, u32[]{:S(2)}) collective-permute-start(bf16[4,2,2,64,1152]{4,3,0,1,2:T(8,128)(2,1)S(1)} %bitcast.552), channel_id=1, source_target_pairs={{0,4},{4,0},{8,12},{12,8},{16,20},{20,16},{24,28},{28,24},{1,5},{5... | collective-permute-start | bytes 7077896 | tf_op jit(solution)/shard_map/ppermute | solution.py:87
  1565.9 53.5 %collective-permute-start.90 = (bf16[4,2,2,80,1152]{4,3,2,1,0:T(8,128)(2,1)}, bf16[4,2,2,80,1152]{4,3,2,1,0:T(8,128)(2,1)}, u32[]{:S(2)}, u32[]{:S(2)}) collective-permute-start(bf16[4,2,2,80,1152]{4,3,2,1,0:T(8,128)(2,1)} %dynamic-slice_bitcast_fusion.1), channel_id=1, source_target_pairs={{0,4},{4,0},{8,12},{12,8},{16,20},{20,16},{24,28},{28,24},{1,5},{5... | collective-permute-start | bytes 8847368 | tf_op jit(solution)/shard_map/ppermute | solution.py:87
  1577.2 23.3 %collective-permute-start.79 = (bf16[4,2,64,864]{3,2,0,1:T(8,128)(2,1)S(1)}, bf16[4,2,64,864]{3,2,0,1:T(8,128)(2,1)S(1)}, u32[]{:S(2)}, u32[]{:S(2)}) collective-permute-start(bf16[4,2,64,864]{3,2,0,1:T(8,128)(2,1)S(1)} %dynamic-slice_bitcast_fusion.10), channel_id=1, source_target_pairs={{0,8},{4,12},{8,0},{12,4},{16,24},{20,28},{24,16},{28,20},{1,9},{5... | collective-permute-start | bytes 2654216 | tf_op jit(solution)/shard_map/ppermute | solution.py:87
  1578.2 55.9 %collective-permute-start.73 = (bf16[4,2,80,864]{3,2,1,0:T(8,128)(2,1)}, bf16[4,2,80,864]{3,2,1,0:T(8,128)(2,1)}, u32[]{:S(2)}, u32[]{:S(2)}) collective-permute-start(bf16[4,2,80,864]{3,2,1,0:T(8,128)(2,1)} %dynamic-slice_bitcast_fusion.9), channel_id=1, source_target_pairs={{0,16},{4,20},{8,24},{12,28},{16,0},{20,4},{24,8},{28,12},{1,17},{... | collective-permute-start | bytes 3317768 | tf_op jit(solution)/shard_map/ppermute | solution.py:87
  1587.0 54.7 %collective-permute-start.97 = (bf16[4,2,64,1152]{3,2,0,1:T(8,128)(2,1)}, bf16[4,2,64,1152]{3,2,0,1:T(8,128)(2,1)}, u32[]{:S(2)}, u32[]{:S(2)}) collective-permute-start(bf16[4,2,64,1152]{3,2,0,1:T(8,128)(2,1)} %dynamic-slice_bitcast_fusion.8), channel_id=1, source_target_pairs={{0,8},{4,12},{8,0},{12,4},{16,24},{20,28},{24,16},{28,20},{1,9},{5... | collective-permute-start | bytes 3538952 | tf_op jit(solution)/shard_map/ppermute | solution.py:87
  1597.3 53.8 %collective-permute-start.109 = (bf16[4,2,64,1152]{3,2,0,1:T(8,128)(2,1)}, bf16[4,2,64,1152]{3,2,0,1:T(8,128)(2,1)}, u32[]{:S(2)}, u32[]{:S(2)}) collective-permute-start(bf16[4,2,64,1152]{3,2,0,1:T(8,128)(2,1)} %dynamic-slice_bitcast_fusion.7), channel_id=1, source_target_pairs={{0,8},{4,12},{8,0},{12,4},{16,24},{20,28},{24,16},{28,20},{1,9},{5... | collective-permute-start | bytes 3538952 | tf_op jit(solution)/shard_map/ppermute | solution.py:87
  1617.5 45.0 %collective-permute-start.103 = (bf16[4,2,80,1152]{3,2,1,0:T(8,128)(2,1)}, bf16[4,2,80,1152]{3,2,1,0:T(8,128)(2,1)S(1)}, u32[]{:S(2)}, u32[]{:S(2)}) collective-permute-start(bf16[4,2,80,1152]{3,2,1,0:T(8,128)(2,1)} %dynamic-slice_bitcast_fusion.4), channel_id=1, source_target_pairs={{0,16},{4,20},{8,24},{12,28},{16,0},{20,4},{24,8},{28,12},{1,17},{... | collective-permute-start | bytes 4423688 | tf_op jit(solution)/shard_map/ppermute | solution.py:87
  1632.8 108.1 %collective-permute-start.91 = (bf16[4,2,80,1152]{3,2,1,0:T(8,128)(2,1)}, bf16[4,2,80,1152]{3,2,1,0:T(8,128)(2,1)}, u32[]{:S(2)}, u32[]{:S(2)}) collective-permute-start(bf16[4,2,80,1152]{3,2,1,0:T(8,128)(2,1)} %dynamic-slice_bitcast_fusion.5), channel_id=1, source_target_pairs={{0,16},{4,20},{8,24},{12,28},{16,0},{20,4},{24,8},{28,12},{1,17},{... | collective-permute-start | bytes 4423688 | tf_op jit(solution)/shard_map/ppermute | solution.py:87
  1643.4 53.7 %collective-permute-start.98 = (bf16[4,64,1152]{2,1,0:T(8,128)(2,1)S(1)}, bf16[4,64,1152]{2,1,0:T(8,128)(2,1)S(1)}, u32[]{:S(2)}, u32[]{:S(2)}) collective-permute-start(bf16[4,64,1152]{2,1,0:T(8,128)(2,1)S(1)} %dynamic-slice_bitcast_fusion.15), channel_id=1, source_target_pairs={{0,16},{4,20},{8,24},{12,28},{16,0},{20,4},{24,8},{28,12},{1,17},{... | collective-permute-start | bytes 1769480 | tf_op jit(solution)/shard_map/ppermute | solution.py:87
  1652.8 51.7 %collective-permute-start.110 = (bf16[4,64,1152]{2,1,0:T(8,128)(2,1)S(1)}, bf16[4,64,1152]{2,1,0:T(8,128)(2,1)S(1)}, u32[]{:S(2)}, u32[]{:S(2)}) collective-permute-start(bf16[4,64,1152]{2,1,0:T(8,128)(2,1)S(1)} %dynamic-slice_bitcast_fusion.14), channel_id=1, source_target_pairs={{0,16},{4,20},{8,24},{12,28},{16,0},{20,4},{24,8},{28,12},{1,17},{... | collective-permute-start | bytes 1769480 | tf_op jit(solution)/shard_map/ppermute | solution.py:87
  1663.9 83.7 %collective-permute-start.104 = (bf16[4,80,1152]{2,1,0:T(8,128)(2,1)}, bf16[4,80,1152]{2,1,0:T(8,128)(2,1)}, u32[]{:S(2)}, u32[]{:S(2)}) collective-permute-start(bf16[4,80,1152]{2,1,0:T(8,128)(2,1)} %dynamic-slice_bitcast_fusion.11), channel_id=1, source_target_pairs={{0,8},{4,12},{8,0},{12,4},{16,24},{20,28},{24,16},{28,20},{1,9},{5... | collective-permute-start | bytes 2211848 | tf_op jit(solution)/shard_map/ppermute | solution.py:87
  1669.4 35.3 %collective-permute-start.76 = (bf16[80,864]{1,0:T(8,128)(2,1)S(1)}, bf16[80,864]{1,0:T(8,128)(2,1)S(1)}, u32[]{:S(2)}, u32[]{:S(2)}) collective-permute-start(bf16[80,864]{1,0:T(8,128)(2,1)S(1)} %fusion.164), channel_id=1, source_target_pairs={{0,1},{1,2},{2,3},{3,0},{4,5},{5,6},{6,7},{7,4},{8,9},{9,10},{10,1... | collective-permute-start | bytes 414728 | tf_op jit(solution)/shard_map/ppermute | solution.py:92
  1705.6 33.2 %collective-permute-start.100 = (bf16[64,1152]{1,0:T(8,128)(2,1)}, bf16[64,1152]{1,0:T(8,128)(2,1)}, u32[]{:S(2)}, u32[]{:S(2)}) collective-permute-start(bf16[64,1152]{1,0:T(8,128)(2,1)} %fusion.156), channel_id=1, source_target_pairs={{0,1},{1,2},{2,3},{3,0},{4,5},{5,6},{6,7},{7,4},{8,9},{9,10},{10,1... | collective-permute-start | bytes 442376 | tf_op jit(solution)/shard_map/ppermute | solution.py:92
  1712.9 26.9 %collective-permute-start.112 = (bf16[64,1152]{1,0:T(8,128)(2,1)}, bf16[64,1152]{1,0:T(8,128)(2,1)}, u32[]{:S(2)}, u32[]{:S(2)}) collective-permute-start(bf16[64,1152]{1,0:T(8,128)(2,1)} %fusion.154), channel_id=1, source_target_pairs={{0,1},{1,2},{2,3},{3,0},{4,5},{5,6},{6,7},{7,4},{8,9},{9,10},{10,1... | collective-permute-start | bytes 442376 | tf_op jit(solution)/shard_map/ppermute | solution.py:92
  (178 other events, 3568.6 us)

commit v2 on v1

v2 whole, which is shorter than its diff:
```python
from functools import partial
import math

import jax
import jax.numpy as jnp
from jax import lax
from jax.experimental import pallas as pl
from jax.experimental.pallas import tpu as pltpu
from jax.sharding import PartitionSpec as P

HEADS = 16
HEAD_DIM = 72
FF = 4608
LEN = 1024

epsilon = 1e-06
momentum_decay = 0.9
learning_rate = 0.4
HIGHEST = lax.Precision.HIGHEST
bf16 = jnp.bfloat16
f32 = jnp.float32
VMEM_LIMIT = 56 * 1024 * 1024


def layer_norm(values):
    center = values - jnp.mean(values, axis=-1, keepdims=True)
    variance = jnp.mean(center * center, axis=-1, keepdims=True)
    return center * lax.rsqrt(variance + epsilon)


def norm_back(values, gradient):
    center = values - jnp.mean(values, axis=-1, keepdims=True)
    variance = jnp.mean(center * center, axis=-1, keepdims=True)
    inverse = lax.rsqrt(variance + epsilon)
    normed = center * inverse
    mean_grad = jnp.mean(gradient, axis=-1, keepdims=True)
    mean_inner = jnp.mean(gradient * normed, axis=-1, keepdims=True)
    return (gradient - mean_grad - normed * mean_inner) * inverse


def grid_shapes(model_width, block_size, tensor_size):
    row_blocks = model_width // block_size
    split_size = block_size * tensor_size
    return [
        (row_blocks, 3 * model_width // split_size),
        (model_width // split_size, row_blocks),
        (row_blocks, FF // split_size),
        (FF // split_size, row_blocks),
        (row_blocks, 6 * model_width // split_size),
    ]


def to_dense(blocks, col_blocks):
    count, size = blocks.shape[0], blocks.shape[1]
    if count >= col_blocks:
        shaped = blocks.reshape(count // col_blocks, col_blocks, size, size)
        return jnp.transpose(shaped, (0, 2, 1, 3)).reshape(-1, col_blocks * size)
    return jnp.transpose(blocks, (1, 0, 2)).reshape(size, count * size)


def to_blocks(dense, size):
    rows, cols = dense.shape
    shaped = dense.reshape(rows // size, size, cols // size, size)
    return jnp.transpose(shaped, (0, 2, 1, 3)).reshape(-1, size, size)


def whole_from_runs(runs, rows, cols):
    tensor_size, dp_size, r, c = runs.shape
    per = cols // c
    if per == 1:
        return runs.reshape(tensor_size, rows, cols)
    shaped = runs.reshape(tensor_size, dp_size // per, per, r, c)
    return jnp.transpose(shaped, (0, 1, 3, 2, 4)).reshape(tensor_size, rows, cols)


def runs_from_whole(whole, dp_size, r, c):
    tensor_size, rows, cols = whole.shape
    per = cols // c
    if per == 1:
        return whole.reshape(tensor_size, dp_size, r, c)
    shaped = whole.reshape(tensor_size, dp_size // per, r, per, c)
    return jnp.transpose(shaped, (0, 1, 3, 2, 4)).reshape(tensor_size, dp_size, r, c)


def exchange(values, axis):
    return lax.all_to_all(values, axis, split_axis=0, concat_axis=0, tiled=True)


def bit_swap(values, bit):
    size = lax.axis_size("dp")
    return lax.ppermute(values, "dp", [(k, k ^ bit) for k in range(size)])


def ring(values):
    size = lax.axis_size("tensor")
    return lax.ppermute(values, "tensor", [(k, (k + 1) % size) for k in range(size)])


def pair_swap(values):
    size = lax.axis_size("tensor")
    return lax.ppermute(values, "tensor", [(k, k ^ 1) for k in range(size)])


def exchange_t(slots):
    return exchange(slots, "tensor")


def after(values, *earlier):
    return lax.optimization_barrier((values, *earlier))[0]


class Gathering:
    def __init__(self, piece, bits, *earlier):
        self.bits = bits
        size = lax.axis_size("tensor")
        piece = after(piece, *earlier) if earlier else piece
        self.slots = exchange_t(jnp.broadcast_to(piece, (size,) + piece.shape))

    def start(self, *earlier):
        half = self.slots.shape[0] // 2
        slots = after(self.slots, *earlier) if earlier else self.slots
        self.masks = [[0], [0]]
        self.stacks = [slots[None, :half], slots[None, half:]]
        self.orders = [self.bits, self.bits[::-1]]
        return self.send()

    def send(self):
        self.flying = [bit_swap(stack, order[0]) for stack, order in zip(self.stacks, self.orders)]
        return self

    def join(self, *earlier):
        for n, order in enumerate(self.orders):
            got = after(self.flying[n], *earlier) if earlier else self.flying[n]
            self.masks[n] = self.masks[n] + [mask ^ order[0] for mask in self.masks[n]]
            self.stacks[n] = jnp.concatenate([self.stacks[n], got])
        self.orders = [order[1:] for order in self.orders]
        return self.stacks

    def last_send(self):
        while len(self.orders[0]) > 1:
            self.send()
            self.join()
        self.send()
        self.crossed = [bit_swap(stack, 1) for stack in self.stacks]
        return self

    def cross(self, *earlier):
        if earlier:
            self.flying = [after(got, *earlier) for got in self.flying]
        self.last = [bit_swap(got, 1) for got in self.flying]
        return self.flying

    def parts(self):
        half = self.stacks[0].shape[1]
        found = []
        for n, order in enumerate(self.orders):
            near = self.masks[n]
            far = [mask ^ order[0] for mask in near]
            for masks, stack in (
                (near, self.stacks[n]),
                (far, self.flying[n]),
                ([mask ^ 1 for mask in near], self.crossed[n]),
                ([mask ^ 1 for mask in far], self.last[n]),
            ):
                found.append((n * half, masks, stack))
        return found

    def assemble(self, dp_size, where, *earlier):
        found = self.parts()
        if earlier:
            found[0] = found[0][:2] + (after(found[0][2], *earlier),)
        return assemble(found, dp_size, where)


def assemble_kernel(plan, where, *refs):
    count = len(plan)
    stacks, out, held, sems = refs[:count], refs[count], refs[count + 1], refs[count + 2]
    i = where[0]
    loads, stores = [], []
    for number, (first, masks) in enumerate(plan):
        slots = stacks[number].shape[1]
        for m, mask in enumerate(masks):
            for n in range(slots):
                place = (first + n, i ^ mask)
                sem = sems.at[len(loads)]
                loads.append(pltpu.make_async_copy(stacks[number].at[m, n], held.at[place], sem))
                stores.append(pltpu.make_async_copy(held.at[place], out.at[place], sem))
    for copy in loads:
        copy.start()
    for load, store in zip(loads, stores):
        load.wait()
        store.start()
    for copy in stores:
        copy.wait()


def assemble(found, dp_size, where):
    plan = [(first, masks) for first, masks, _ in found]
    stacks = [stack for _, _, stack in found]
    r, c = stacks[0].shape[2:]
    slots = sum(stack.shape[1] * len(masks) for (_, masks), stack in zip(plan, stacks)) // dp_size
    shape = (slots, dp_size, r, c)
    amount = 2 * 2 * math.prod(shape)
    return pl.pallas_call(
        partial(assemble_kernel, plan),
        out_shape=jax.ShapeDtypeStruct(shape, stacks[0].dtype),
        in_specs=[pl.BlockSpec(memory_space=pltpu.SMEM)]
        + [pl.BlockSpec(memory_space=pl.ANY)] * len(stacks),
        out_specs=pl.BlockSpec(memory_space=pl.ANY),
        scratch_shapes=[
            pltpu.VMEM(shape, stacks[0].dtype),
            pltpu.SemaphoreType.DMA((slots * dp_size,)),
        ],
        compiler_params=pltpu.CompilerParams(vmem_limit_bytes=VMEM_LIMIT),
        cost_estimate=pl.CostEstimate(flops=0, bytes_accessed=amount, transcendentals=0),
        name="assemble",
    )(where, *stacks)


def take(values, index, axis):
    return lax.dynamic_index_in_dim(values, index, axis, keepdims=False)


def add(left, right):
    return (left.astype(f32) + right.astype(f32)).astype(bf16)


class Reduction:
    def __init__(self, runs, bits, order, i):
        self.left, self.order, self.i, self.runs = list(bits[::-1]), list(order), i, runs

    def send(self, *earlier):
        bit = self.order[0]
        other = take(self.runs, 1 - (self.i // bit) % 2, 1 + self.left.index(bit))
        self.flying = bit_swap(after(other, *earlier) if earlier else other, bit)
        return self

    def add(self, *earlier):
        bit = self.order.pop(0)
        got = after(self.flying, *earlier) if earlier else self.flying
        self.runs = add(take(self.runs, (self.i // bit) % 2, 1 + self.left.index(bit)), got)
        self.left.remove(bit)
        return self.runs

    def last_add(self, *earlier):
        self.add(*earlier)
        while self.order:
            self.send()
            self.add()
        return self.runs


def total(slots, *earlier):
    if earlier:
        slots = after(slots, *earlier)
    return jnp.sum(slots.astype(f32), axis=0)


def contract(left, right, dims):
    return lax.dot_general(left, right, ((dims[:1], dims[1:]), ((), ())), preferred_element_type=f32)


def attend_kernel(q_ref, k_ref, v_ref, k_other_ref, v_other_ref, out_ref, log_ref):
    factor = HEAD_DIM ** (-0.5) * math.log2(math.e)
    q = q_ref[0, 0]
    scores = [contract(keys[0, 0], q, (0, 0)) for keys in (k_ref, k_other_ref)]
    highest = jnp.max(scores[0], axis=0, keepdims=True)
    for piece in scores[1:]:
        highest = jnp.maximum(highest, jnp.max(piece, axis=0, keepdims=True))
    shift = highest * factor
    amount = jnp.zeros_like(shift)
    attended = jnp.zeros(q.shape, f32)
    for piece, values in zip(scores, (v_ref, v_other_ref)):
        weights = jnp.exp2(piece * factor - shift)
        amount = amount + jnp.sum(weights, axis=0, keepdims=True)
        attended = attended + contract(values[0, 0], weights.astype(bf16), (1, 0))
    size = q.shape[0]
    out_ref[0, :size] = (attended / amount).astype(bf16)
    out_ref[0, size:] = jnp.zeros((out_ref.shape[1] - size, q.shape[1]), bf16)
    log_ref[0] = shift + jnp.log2(amount)


def head_specs(heads, size, rows, start):
    def spec(part, column):
        return pl.BlockSpec(
            (1, 1, size, rows), lambda n: (start + n // heads, part * heads + n % heads, 0, column)
        )

    return [spec(0, 0), spec(1, 0), spec(2, 0), spec(1, 1), spec(2, 1)]


def attend(projected, heads, start, groups):
    _, _, size, columns = projected.shape
    rows = columns // 2
    count = groups * heads
    tall = size + -size % 16
    return pl.pallas_call(
        attend_kernel,
        grid=(count,),
        in_specs=head_specs(heads, size, rows, start),
        out_specs=[
            pl.BlockSpec((1, tall, rows), lambda n: (n, 0, 0)),
            pl.BlockSpec((1, 1, rows), lambda n: (n, 0, 0)),
        ],
        out_shape=[
            jax.ShapeDtypeStruct((count, tall, rows), bf16),
            jax.ShapeDtypeStruct((count, 1, rows), f32),
        ],
        compiler_params=pltpu.CompilerParams(vmem_limit_bytes=VMEM_LIMIT),
        cost_estimate=pl.CostEstimate(
            flops=count * 16 * size * rows * rows,
            bytes_accessed=count * 12 * size * rows,
            transcendentals=count * 2 * rows * rows,
        ),
        name="attend",
    )(*[projected] * 5)


def attend_back_kernel(
    q_ref, k_ref, v_ref, k_other_ref, v_other_ref, grad_ref, log_ref, out_ref
):
    scale = HEAD_DIM ** (-0.5)
    factor = scale * math.log2(math.e)
    rows = q_ref.shape[3]
    q, log = q_ref[0, 0], log_ref[0]
    grad = grad_ref[0, : q.shape[0]]
    keys = [k_ref[0, 0], k_other_ref[0, 0]]
    values = [v_ref[0, 0], v_other_ref[0, 0]]
    weights = [jnp.exp2(contract(k, q, (0, 0)) * factor - log) for k in keys]
    grads = [contract(v, grad, (0, 0)) for v in values]
    inner = jnp.zeros_like(log)
    for w, g in zip(weights, grads):
        inner = inner + jnp.sum(w * g, axis=0, keepdims=True)
    grad_q = jnp.zeros(q.shape, f32)
    for place, (k, w, g) in enumerate(zip(keys, weights, grads)):
        columns = pl.ds(place * rows, rows)
        grad_v = contract(grad, w.astype(bf16), (1, 1))
        grad_scores = (w * (g - inner)).astype(bf16)
        grad_k = contract(q, grad_scores, (1, 1)) * scale
        grad_q = grad_q + contract(k, grad_scores, (1, 0))
        out_ref[0, 1, 0, :, columns] = grad_k.astype(bf16)
        out_ref[0, 2, 0, :, columns] = grad_v.astype(bf16)
    out_ref[0, 0, 0, :, pl.ds(0, rows)] = (grad_q * scale).astype(bf16)
    out_ref[0, 0, 0, :, pl.ds(rows, rows)] = jnp.zeros(q.shape, bf16)


def attend_back(projected, grad, log, heads, start, groups):
    _, _, size, columns = projected.shape
    rows = columns // 2
    count = groups * heads
    at = start * heads
    return pl.pallas_call(
        attend_back_kernel,
        grid=(count,),
        in_specs=head_specs(heads, size, rows, start)
        + [
            pl.BlockSpec((1, grad.shape[1], rows), lambda n: (at + n, 0, 0)),
            pl.BlockSpec((1, 1, rows), lambda n: (n, 0, 0)),
        ],
        out_specs=pl.BlockSpec(
            (1, 3, 1, size, columns), lambda n: (n // heads, 0, n % heads, 0, 0)
        ),
        out_shape=jax.ShapeDtypeStruct((groups, 3, heads, size, columns), bf16),
        compiler_params=pltpu.CompilerParams(vmem_limit_bytes=VMEM_LIMIT),
        cost_estimate=pl.CostEstimate(
            flops=count * 40 * size * rows * rows,
            bytes_accessed=count * 24 * size * rows,
            transcendentals=count * 2 * rows * rows,
        ),
        name="attend_back",
    )(*[projected] * 5, grad, log)


def step_kernel(size, aliased, grads_ref, master_ref, moment_ref, stats_ref, roots_ref, *refs):
    new_master, new_moment, new_stats, held = refs[aliased:]
    n = pl.program_id(0)

    @pl.when(n == 0)
    def _():
        found = grads_ref[0].astype(f32)
        for k in range(1, grads_ref.shape[0]):
            found = found + grads_ref[k].astype(f32)
        held[...] = found

    rows = held[pl.ds(pl.multiple_of(n * size, 8), size), :]
    for b in range(master_ref.shape[0]):
        grad = rows[:, b * size : b * size + size]
        low = grad.astype(bf16)
        new_stats[0, b] = 0.5 * stats_ref[0, b] + 0.5 * contract(low, low, (1, 1))
        new_stats[1, b] = 0.5 * stats_ref[1, b] + 0.5 * contract(low, low, (0, 0))
        moment = momentum_decay * moment_ref[b] + (1.0 - momentum_decay) * grad
        new_moment[b] = moment
        update = contract(roots_ref[0, b].astype(bf16), moment.astype(bf16), (1, 0))
        update = contract(update.astype(bf16), roots_ref[1, b].astype(bf16), (1, 0))
        new_master[b] = master_ref[b] - learning_rate * update


def step(grads, span, state, earlier):
    master, moment, stats, roots = state
    size = master.shape[1]
    r, c = grads.shape[1:]
    steps, count = r // size, (span[1] - span[0]) // (r // size)
    base = span[0] // count
    blocks = pl.BlockSpec((count, size, size), lambda n: (base + n, 0, 0))
    pairs = pl.BlockSpec((2, count, size, size), lambda n: (0, base + n, 0, 0))
    aliased = list(earlier or ())
    amount = 40 * size * 128 * (span[1] - span[0])
    return pl.pallas_call(
        partial(step_kernel, size, len(aliased)),
        grid=(steps,),
        in_specs=[
            pl.BlockSpec(grads.shape, lambda n: (0, 0, 0)),
            blocks,
            blocks,
            pairs,
            pairs,
        ]
        + [pl.BlockSpec(memory_space=pl.ANY)] * len(aliased),
        out_specs=[blocks, blocks, pairs],
        out_shape=[jax.ShapeDtypeStruct(x.shape, f32) for x in (master, moment, stats)],
        scratch_shapes=[pltpu.VMEM((r, c), f32)],
        input_output_aliases={5 + n: n for n in range(len(aliased))},
        compiler_params=pltpu.CompilerParams(vmem_limit_bytes=VMEM_LIMIT),
        cost_estimate=pl.CostEstimate(flops=amount, bytes_accessed=amount, transcendentals=0),
        name="step",
    )(grads, master, moment, stats, roots, *aliased)


def local(tokens, conditioning, master, moment, stats, roots, cotangent):
    dp_size = lax.axis_size("dp")
    tensor_size = lax.axis_size("tensor")
    i, t = lax.axis_index("dp"), lax.axis_index("tensor")
    where = jnp.stack([i, t]).astype(jnp.int32)
    rows, width = tokens.shape
    size = master.shape[1]
    sequences = conditioning.shape[0]
    latents = sequences * dp_size
    heads = HEADS // tensor_size
    shapes = grid_shapes(width, size, tensor_size)
    bits = [1 << b for b in range(1, dp_size.bit_length() - 1)]

    low = master.astype(bf16)
    pieces, spans, offset = [], [], 0
    for row_blocks, col_blocks in shapes:
        count = row_blocks * col_blocks // dp_size
        pieces.append(to_dense(low[offset : offset + count], col_blocks))
        spans.append((offset, offset + count))
        offset += count
    w_ada = pieces[4]

    head_cols = heads * HEAD_DIM
    ro, c_out = pieces[1].shape
    tall = HEAD_DIM + -HEAD_DIM % 16
    per = width // c_out
    pieces_out = jnp.pad(pieces[1], ((0, tall - ro), (0, 0)))
    one = Gathering(pieces[0], bits)

    silu_low = jax.nn.silu(conditioning).astype(bf16)
    ada_cols = 6 * width // tensor_size
    ada_r, ada_c = w_ada.shape
    ada_per = ada_cols // ada_c
    row_at, col_at = (i // ada_per) * ada_r, (i % ada_per) * ada_c
    silu_for = jnp.moveaxis(silu_low.reshape(sequences, dp_size // ada_per, ada_r), 1, 0)
    silu_for = jnp.repeat(silu_for, ada_per, axis=0)
    silu_mine = exchange(silu_for, "dp").reshape(latents, ada_r)
    share = jnp.dot(silu_mine, w_ada, preferred_element_type=f32)
    if ada_per > 1:
        share = lax.dynamic_update_slice(jnp.zeros((latents, ada_cols), f32), share, (0, col_at))
    shares = exchange(share.reshape(dp_size, sequences, ada_cols), "dp")
    own_mods = jnp.sum(shares, axis=0)
    span = LEN // rows
    mods = exchange(jnp.repeat(own_mods, span, axis=0), "tensor").reshape(6, 1, width)
    shift1, scale1, gate1, shift2, scale2, gate2 = (mods[k] for k in range(6))

    one.start().join()
    others = pair_swap(after(tokens, one.slots))
    three = Gathering(pieces[2], bits, one.slots)
    one.last_send()
    two = Gathering(pieces_out, bits, three.slots)
    one.cross()
    three.start(*one.flying)
    two.start().join()
    four = Gathering(pieces[3], bits, two.slots)
    two.last_send().cross()

    inputs = tokens.astype(f32)
    normed_one = layer_norm(inputs)
    h1 = (normed_one * (1.0 + scale1) + shift1).astype(bf16)
    h1_other = (layer_norm(others.astype(f32)) * (1.0 + scale1) + shift1).astype(bf16)
    h1_all = jnp.concatenate([h1, h1_other])
    w_qkv = whole_from_runs(one.assemble(dp_size, where), width, 3 * head_cols)
    projected = jnp.einsum("tdc,rd->tcr", w_qkv, h1_all, preferred_element_type=f32).astype(bf16)
    projected = projected.reshape(tensor_size, 3 * heads, HEAD_DIM, 2 * rows)
    projected = after(projected, *three.join())
    three.last_send()
    cut = tensor_size // 2
    first, first_log = attend(projected, heads, 0, cut)
    three.cross(first)
    four.start(*three.flying)
    second, second_log = attend(after(projected, *three.flying), heads, cut, cut)
    attended = jnp.concatenate([first, second]).reshape(HEADS * tall, rows)
    out_runs = two.assemble(dp_size, where, second).reshape(tensor_size, heads, per, tall, c_out)
    out_runs = jnp.moveaxis(out_runs, 2, 0).reshape(per, HEADS * tall, c_out)
    branch = jnp.concatenate(
        [
            jnp.einsum("er,ed->rd", attended, out_runs[n], preferred_element_type=f32)
            for n in range(per)
        ],
        axis=1,
    )
    middle = inputs + gate1 * branch
    normed_two = layer_norm(middle)
    h2 = (normed_two * (1.0 + scale2) + shift2).astype(bf16)
    w_up = whole_from_runs(three.assemble(dp_size, where, h2), width, FF // tensor_size)
    four.join(w_up)
    four.last_send()
    h2_now = after(h2, *four.stacks)
    pre_gelu = jnp.einsum("rd,tdc->trc", h2_now, w_up, preferred_element_type=f32)
    hidden = jax.nn.gelu(pre_gelu, approximate=True).astype(bf16)

    core = i % 2
    fast = all(pieces[n].shape[1] == shapes[n][1] * size for n in (0, 2, 3))
    lead = (2,) * len(bits)

    def core_part(values, axis, part):
        shape = values.shape
        shaped = values.reshape(shape[:axis] + (dp_size // 2, 2, shape[axis] // dp_size) + shape[axis + 1 :])
        taken = take(shaped, part, axis + 1)
        return taken.reshape(shape[:axis] + (shape[axis] // 2,) + shape[axis + 1 :])

    def both_cores(values, axis, columns=None, *earlier):
        keep = values if columns is None else core_part(values, columns, core)
        send = values if columns is None else core_part(values, columns, 1 - core)
        if earlier:
            send = after(send, *earlier)
        return jnp.concatenate([keep, bit_swap(send, 1)], axis=axis)

    def core_reduced(whole, shape):
        runs = runs_from_whole(whole, dp_size, *shape)
        runs = runs.reshape(runs.shape[:1] + (dp_size // 2, 2) + shape)
        got = bit_swap(take(runs, 1 - core, 2), 1)
        done = add(take(runs, core, 2), got)
        return done.reshape(runs.shape[:1] + lead + shape)

    def row_grads(spec, left, right, number):
        found = jnp.einsum(spec, left, right, preferred_element_type=f32).astype(bf16)
        if fast:
            return found.reshape(found.shape[:1] + lead + pieces[number].shape)
        return core_reduced(found, pieces[number].shape)

    def halves(runs):
        return [
            Reduction(runs[n * cut : n * cut + cut], bits, order, i)
            for n, order in enumerate((bits[::-1], bits))
        ]

    def send_all(*reductions, earlier=()):
        for half in reductions:
            if half.order:
                half.send(*earlier)

    grad_out = cotangent.astype(f32)
    gm = (grad_out * gate2).astype(bf16)
    if fast:
        hidden_all = both_cores(hidden, 1, 2)
        gm_all = both_cores(gm, 0, None, hidden)
    else:
        hidden_all, gm_all = hidden, gm
    grad_down = row_grads("trc,rd->tcd", hidden_all, gm_all, 3)
    red_down = halves(grad_down)
    four.cross(grad_down)
    send_all(*red_down, earlier=four.flying)
    w_down = whole_from_runs(four.assemble(dp_size, where), FF // tensor_size, width)
    gm_later = after(gm, grad_down)
    grad_hidden = jnp.einsum("rd,tcd->trc", gm_later, w_down, preferred_element_type=f32)
    _, gelu_pullback = jax.vjp(partial(jax.nn.gelu, approximate=True), pre_gelu)
    gz = gelu_pullback(grad_hidden)[0].astype(bf16)
    if fast:
        gz_all = both_cores(gz, 1)
        h2_all = both_cores(h2, 0, 1, gz)
    else:
        gz_all, h2_all = gz, h2
    gh2 = jnp.einsum("trc,tdc->rd", gz, w_up, preferred_element_type=f32)
    gx1 = grad_out + norm_back(middle, gh2 * (1.0 + scale2))
    ga = (gx1 * gate1).astype(bf16)
    down_two = [half.add(ga) for half in red_down]
    send_all(*red_down)
    ga = after(ga, *down_two)
    ga_runs = [ga[:, n * c_out : n * c_out + c_out] for n in range(per)]
    go = sum(
        jnp.einsum("ed,rd->er", out_runs[n], ga_runs[n], preferred_element_type=f32)
        for n in range(per)
    ).astype(bf16)
    go = go.reshape(HEADS, tall, rows)

    def out_grad(some):
        return jnp.einsum("er,rd->ed", attended, some, preferred_element_type=f32).astype(bf16)

    if fast:
        stacked = jnp.stack(ga_runs)
        keep, away = out_grad(take(stacked, core, 0)), out_grad(take(stacked, 1 - core, 0))
        grad_wo = add(keep, bit_swap(away, 1))
        grad_wo = grad_wo.reshape((tensor_size,) + lead + (tall, c_out))
    else:
        away = out_grad(ga)
        grad_wo = core_reduced(away.reshape(tensor_size, heads * tall, width), (tall, c_out))
    grad_up = row_grads("rd,trc->tdc", h2_all, after(gz_all, away, go), 2)
    down_one = [half.last_add(grad_up) for half in red_down]
    down_spread = exchange_t(jnp.concatenate(down_one))
    red_up, red_out = halves(grad_up), halves(grad_wo)
    send_all(*red_up, *red_out, earlier=down_one)
    first = attend_back(after(projected, *down_one), go, first_log, heads, 0, cut)
    first = first.reshape(cut, 3 * head_cols, 2 * rows)
    out_two = [half.add(first) for half in red_out]
    send_all(*red_out)
    first_all = both_cores(first, 2) if fast else first
    second = attend_back(after(projected, *out_two), go, second_log, heads, cut, cut)
    second = second.reshape(cut, 3 * head_cols, 2 * rows)
    state = (master, moment, stats, roots)
    done = step(after(down_spread, second), spans[3], state, None)
    up_two = [half.add(*done) for half in red_up]
    send_all(*red_up)
    out_one = [half.last_add(*up_two) for half in red_out]
    out_spread = exchange_t(after(jnp.concatenate(out_one)[:, :ro], *up_two))
    second_all = both_cores(second, 2) if fast else second
    h1_both = both_cores(h1_all, 0, 1, second) if fast else h1_all
    grad_first = row_grads("rd,tcr->tdc", h1_both, after(first_all, *out_one), 0)
    gh1_other = jnp.einsum(
        "tcr,tdc->rd",
        after(jnp.concatenate([first, second]), grad_first)[:, head_cols:, rows:],
        w_qkv[:, :, head_cols:],
        preferred_element_type=f32,
    ).astype(bf16)
    done = step(after(out_spread, gh1_other), spans[1], state, done)
    up_one = [half.last_add(gh1_other) for half in red_up]
    gh1_far = pair_swap(after(gh1_other, *up_one))
    red_first = Reduction(grad_first, bits, bits[::-1], i)
    red_first.send(*up_one)
    grad_second = row_grads("rd,tcr->tdc", h1_both, after(second_all, *up_one), 0)
    red_second = Reduction(grad_second, bits, bits, i)
    red_second.send()
    up_spread = exchange_t(after(jnp.concatenate(up_one), grad_second))
    gh1 = jnp.einsum(
        "tcr,tdc->rd",
        after(jnp.concatenate([first, second])[:, :, :rows], grad_second),
        w_qkv,
        preferred_element_type=f32,
    )
    feed = jnp.einsum(
        "trc,tcd->rd", after(hidden, gh1), w_down, preferred_element_type=f32
    )
    result = (middle + gate2 * feed).astype(bf16)
    first_two = red_first.add(feed)
    second_two = red_second.add(feed)
    send_all(red_first, red_second)
    gh1 = after(gh1, *first_two, *second_two) + gh1_far.astype(f32)
    grad_tokens = gx1 + norm_back(inputs, gh1 * (1.0 + scale1))

    grad_mods = jnp.stack(
        [
            jnp.sum(gh1, axis=0),
            jnp.sum(gh1 * normed_one, axis=0),
            jnp.sum(gx1 * branch, axis=0),
            jnp.sum(gh2, axis=0),
            jnp.sum(gh2 * normed_two, axis=0),
            jnp.sum(grad_out * feed, axis=0),
        ]
    ).reshape(tensor_size, ada_cols)
    grad_mods = exchange_t(grad_mods)
    done = step(after(up_spread, grad_mods), spans[2], state, done)
    qkv_one = [red_first.last_add(*done), red_second.last_add(*done)]
    qkv_spread = exchange_t(jnp.concatenate(qkv_one))
    grad_mods = jnp.sum(grad_mods.reshape(sequences, span, ada_cols), axis=1)
    grad_mods = after(grad_mods, *qkv_one)
    if ada_per > 1:
        parts = jnp.moveaxis(grad_mods.reshape(sequences, ada_per, ada_c), 1, 0)
        grad_mods = jnp.tile(parts, (dp_size // ada_per, 1, 1))
    else:
        grad_mods = jnp.broadcast_to(grad_mods, (dp_size,) + grad_mods.shape)
    grad_mods = exchange(grad_mods, "dp").reshape(latents, ada_c)
    grad_ada = jnp.einsum("sr,sc->rc", silu_mine.astype(f32), grad_mods, precision=HIGHEST)
    grad_silu = jnp.einsum("sc,rc->sr", grad_mods, w_ada.astype(f32), precision=HIGHEST)
    grad_silu = exchange(grad_silu.reshape(dp_size, sequences, ada_r), "dp")
    grad_silu = jnp.sum(grad_silu.reshape(dp_size // ada_per, ada_per, sequences, ada_r), axis=1)
    grad_silu = jnp.moveaxis(grad_silu, 0, 1).reshape(sequences, width)
    done = step(after(grad_ada[None], grad_silu), spans[4], state, done)
    grad_silu = exchange_t(jnp.broadcast_to(grad_silu, (tensor_size,) + grad_silu.shape))
    grad_silu = jnp.sum(grad_silu, axis=0)
    _, silu_pullback = jax.vjp(jax.nn.silu, conditioning)
    grad_conditioning = silu_pullback(grad_silu)[0]
    done = step(after(qkv_spread, *done), spans[0], state, done)
    return (result, grad_tokens, grad_conditioning, *done)


def solution(mesh):
    both = ("dp", "tensor")
    rows, blocks, pairs = P(both, None), P(both, None, None), P(None, both, None, None)
    return jax.shard_map(
        local,
        mesh=mesh,
        in_specs=(rows, P("dp", None), blocks, blocks, pairs, pairs, rows),
        out_specs=(rows, rows, P("dp", None), blocks, blocks, pairs),
        check_vma=False,
    )
```

time: 1850 us -> 692 us (0.37)
  Pallas kernels: 1050 us -> 110 us
  waiting for transfers between devices: 277 us -> 136 us
  matrix products: 188 us -> 133 us
  blocking collectives: 43.7 us -> 0 us
  starting transfers between devices: 65.9 us -> 107 us
  local copies, waits for them, and re-layouts: 123 us -> 92 us
  other arithmetic: 80.8 us -> 102 us
    pallas_call x4, Pallas kernels: 1000 us -> 29 us  [assemble(): pl.pallas_call(partial(assemble_kernel, plan), out_shape=jax.ShapeDtypeSt...]
    ppermute x42 -> x0, waiting for transfers between devices: 157 us -> none  [ring(): lax.ppermute(values, 'tensor', [(k, (k + 1) % size) for k in range(size)])]
    all_to_all x3 -> x15, waiting for transfers between devices: 4.14 us -> 70 us  [exchange(): return lax.all_to_all(values, axis, split_axis=0, concat_axis=0, tiled=True)]
    dot_general x29 -> x16, matrix products: 173 us -> 118 us  [the longest x4 32.8 us: row_grads(): jnp.einsum(spec, left, right, preferred_element_type=f32).astype(bf16)]
    all_to_all x3 -> x15, starting transfers between devices: 10.8 us -> 65.2 us  [exchange(): return lax.all_to_all(values, axis, split_axis=0, concat_axis=0, tiled=True)]
    ppermute x70 -> x56, waiting for transfers between devices: 107 us -> 60.1 us  [bit_swap(): return lax.ppermute(values, 'dp', [(k, k ^ bit) for k in range(size)])]
    concatenate x6 -> x19, other arithmetic: 12.6 us -> 48.2 us  [the longest x3 18.8 us: both_cores(): return jnp.concatenate([keep, bit_swap(send, 1)], axis=axis)]
    all_gather x3 -> x0, blocking collectives: 32.2 us -> none  [the longest x1 14.5 us: local(): all_mods = lax.all_gather(own_mods, 'tensor', axis=0, tiled=False)]
  transfers between devices with their start and end apart: 117 -> 73, of which waited for: 51 -> 21; matrix products, arithmetic and copies ran while one was open for 17% -> 41% of each run, Pallas kernels for 57% -> 15%
where the time goes in v2:
time: 692 us; the launch traced here: 683 us
  waiting for transfers between devices  136 us (20%)
  matrix products  133 us (19%)
  Pallas kernels  110 us (16%)
  starting transfers between devices  107 us (15%)
  other arithmetic  102 us (15%)
  local copies, waits for them, and re-layouts  92 us (13%)
    all_to_all x15, waiting for transfers between devices, exchange(): return lax.all_to_all(values, axis, split_axis=0, concat_axis=0, tiled=True)  70 us
    all_to_all x15, starting transfers between devices, exchange(): return lax.all_to_all(values, axis, split_axis=0, concat_axis=0, tiled=True)  65.2 us
    ppermute x56, waiting for transfers between devices, bit_swap(): return lax.ppermute(values, 'dp', [(k, k ^ bit) for k in range(size)])  60.1 us
    ppermute x56, starting transfers between devices, bit_swap(): return lax.ppermute(values, 'dp', [(k, k ^ bit) for k in range(size)])  38.1 us
    pallas_call x2, Pallas kernels, attend_back(): pl.pallas_call(attend_back_kernel, grid=(count,), in_specs=head_specs(hea...  33.4 us
    dot_general x4, matrix products, row_grads(): jnp.einsum(spec, left, right, preferred_element_type=f32).astype(bf16)  32.8 us
    pallas_call x4, Pallas kernels, assemble(): pl.pallas_call(partial(assemble_kernel, plan), out_shape=jax.ShapeDtypeSt...  29 us
    pallas_call x5, Pallas kernels, step(): pl.pallas_call(partial(step_kernel, size, len(aliased)), grid=(steps,), i...  26.9 us
  transfers between devices with their start and end apart: 73, of which 21 were waited for; matrix products, arithmetic and copies ran while one was open for 41% of the time, Pallas kernels for 15%

profile of v2, /device:TPU:0, one launch (start us, length us, event | category | flops | bytes accessed | tf_op | source)
XLA Modules:
  0.0 682.6 jit_solution(7995680952593763427)
XLA Ops:
  2.1 5.2 all-to-all-start
  19.0 4.8 all-to-all-done.1
  24.8 5.0 all-to-all-start.3
  33.7 21.3 %all-to-all-done.3 = bf16[4,144,864]{2,1,0:T(8,128)(2,1)S(1)} async-done(((bf16[4,144,864]{2,1,0:T(8,128)(2,1)}), bf16[4,144,864]{2,1,0:T(8,128)(2,1)S(1)}, u32[]{:S(2)}, u32[]{:S(2)}) %all-to-all-start.3) | async-done | bytes 995360 | tf_op jit(solution)/shard_map/all_to_all | solution.py:86
  66.8 4.3 all-to-all-start.4
  77.3 6.8 collective-permute-done.4
  97.8 6.0 collective-permute-done.8
  115.7 5.0 all-to-all-start.5
  124.2 7.5 %assemble.4 = bf16[4,8,144,864]{3,2,1,0:T(8,128)(2,1)} custom-call(s32[2]{0:T(128)} %pad_add_fusion.where, bf16[2,2,144,864]{3,2,1,0:T(8,128)(2,1)} %pad_maximum_fusion.13.refs_0_, bf16[2,2,144,864]{3,2,1,0:T(8,128)(2,1)} %collective-permute-done.1.refs_1_, bf16[2,2,144,864]{3,2,1,0:T(8,128)(2,1)} %collective-permute-done.2.refs_2_, ...), custom_call_target="tpu_custom_call" | custom-call | bytes 15925248 | tf_op jit(solution)/shard_map/assemble/pallas_call | solution.py:204
  146.3 15.8 %convolution_convert_fusion = bf16[4,864,1024]{2,1,0:T(8,128)(2,1)} fusion(bf16[4,1152,864]{2,1,0:T(8,128)(2,1)} %bitcast.322, bf16[512,1152]{1,0:T(8,128)(2,1)S(1)} %copy-done.34, bf16[512,1152]{1,0:T(8,128)(2,1)S(1)} %get-tuple-element.228), kind=kOutput, calls=%fused_computation.22 | convolution fusion | flops 8161984512 | bytes 17399808 | tf_op jit(solution)/shard_map/tdc,rd->tcr/dot_general | solution.py:492
  163.2 5.2 all-to-all-start.6
  168.5 11.8 %collective-permute-done.14.refs_1_ = bf16[2,2,80,576]{3,2,1,0:T(8,128)(2,1)} collective-permute-done((bf16[2,2,80,576]{3,2,1,0:T(8,128)(2,1)}, bf16[2,2,80,576]{3,2,1,0:T(8,128)(2,1)}, u32[]{:S(2)}, u32[]{:S(2)}) %collective-permute-start.14) | collective-permute-done | bytes 368672 | tf_op jit(solution)/shard_map/ppermute | solution.py:91
  180.9 10.6 %attend.2 = (bf16[8,80,512]{2,1,0:T(8,128)(2,1)}, f32[8,1,512]{2,1,0:T(1,128)}) custom-call(bf16[4,12,72,1024]{3,2,1,0:T(8,128)(2,1)} %bitcast.278, bf16[4,12,72,1024]{3,2,1,0:T(8,128)(2,1)} %bitcast.279, bf16[4,12,72,1024]{3,2,1,0:T(8,128)(2,1)} %bitcast.280, bf16[4,12,72,1024]{3,2,1,0:T(8,128)(2,1)} %bitcast.281, bf16[4,12,72,1024]{3,2,1,0:T(8,128)(2,1)} %bitcast.282), custom_call_target="tpu_custom_call" | custom-call | flops 2415919104 | bytes 3538944 | tf_op jit(solution)/shard_map/attend/pallas_call | solution.py:297
  191.9 10.6 %attend.3 = (bf16[8,80,512]{2,1,0:T(8,128)(2,1)}, f32[8,1,512]{2,1,0:T(1,128)}) custom-call(bf16[4,12,72,1024]{3,2,1,0:T(8,128)(2,1)} %bitcast.283, bf16[4,12,72,1024]{3,2,1,0:T(8,128)(2,1)} %bitcast.284, bf16[4,12,72,1024]{3,2,1,0:T(8,128)(2,1)} %bitcast.285, bf16[4,12,72,1024]{3,2,1,0:T(8,128)(2,1)} %bitcast.286, bf16[4,12,72,1024]{3,2,1,0:T(8,128)(2,1)} %bitcast.287), custom_call_target="tpu_custom_call" | custom-call | flops 2415919104 | bytes 3538944 | tf_op jit(solution)/shard_map/attend/pallas_call | solution.py:297
  220.7 8.7 %assemble.6 = bf16[4,8,144,1152]{3,2,1,0:T(8,128)(2,1)} custom-call(s32[2]{0:T(128)} %pad_add_fusion.where, bf16[2,2,144,1152]{3,2,1,0:T(8,128)(2,1)} %pad_maximum_fusion.6.refs_0_, bf16[2,2,144,1152]{3,2,1,0:T(8,128)(2,1)} %collective-permute-done.11.refs_1_, bf16[2,2,144,1152]{3,2,1,0:T(8,128)(2,1)} %collective-permute-done.21.refs_2_, ...), custom_call_target="tpu_custom_call" | custom-call | bytes 21233664 | tf_op jit(solution)/shard_map/assemble/pallas_call | solution.py:204
  229.4 5.5 collective-permute-done.26
  237.4 14.7 %fusion.10 = (bf16[4,512,1152]{1,2,0:T(8,128)(2,1)S(1)}, f32[4,1152,512]{2,1,0:T(8,128)}) fusion(bf16[4,1152,1152]{2,1,0:T(8,128)(2,1)} %bitcast.313, bf16[512,1152]{1,0:T(8,128)(2,1)S(1)} %add_convert_fusion.2), kind=kOutput, calls=%fused_computation.16 | convolution fusion | flops 5457051648 | bytes 25952256 | tf_op jit(solution)/shard_map/rd,tdc->trc/dot_general | solution.py:518
  262.4 4.3 copy.235
  267.2 8.8 %convolution_convert_fusion.2 = bf16[4,576,1152]{2,1,0:T(8,128)(2,1)S(1)} fusion(bf16[4,512,576]{1,2,0:T(8,128)(2,1)} %collective-permute-done.27, bf16[4,512,576]{1,2,0:T(8,128)(2,1)} %bitcast.336, bf16[512,1152]{1,0:T(8,128)(2,1)} %collective-permute-done.28, bf16[512,1152]{1,0:T(8,128)(2,1)} %fusion.49), kind=kOutput, calls=%fused_computation.26 | convolution fusion | flops 5452627968 | bytes 12386304 | tf_op jit(solution)/shard_map/trc,rd->tcd/dot_general | solution.py:546
  276.1 12.7 %collective-permute-done.30.refs_5_ = bf16[2,2,144,1152]{3,2,1,0:T(8,128)(2,1)} collective-permute-done((bf16[2,2,144,1152]{3,2,1,0:T(8,128)(2,1)}, bf16[2,2,144,1152]{3,2,1,0:T(8,128)(2,1)}, u32[]{:S(2)}, u32[]{:S(2)}) %collective-permute-start.30) | collective-permute-done | bytes 1327136 | tf_op jit(solution)/shard_map/ppermute | solution.py:91
  298.9 8.8 %assemble.7 = bf16[4,8,144,1152]{3,2,1,0:T(8,128)(2,1)} custom-call(s32[2]{0:T(128)} %pad_add_fusion.where, bf16[2,2,144,1152]{3,2,1,0:T(8,128)(2,1)} %pad_maximum_fusion.8.refs_0_, bf16[2,2,144,1152]{3,2,1,0:T(8,128)(2,1)} %collective-permute-done.29.refs_1_, bf16[2,2,144,1152]{3,2,1,0:T(8,128)(2,1)} %copy-done.53, ...), custom_call_target="tpu_custom_call" | custom-call | bytes 21233664 | tf_op jit(solution)/shard_map/assemble/pallas_call | solution.py:204
  307.7 17.8 %fusion.6 = bf16[4,512,1152]{1,2,0:T(8,128)(2,1)} fusion(f32[4,1152,512]{2,1,0:T(8,128)} %get-tuple-element.231, bf16[4,1152,1152]{2,1,0:T(8,128)(2,1)} %bitcast.309, bf16[512,1152]{1,0:T(8,128)(2,1)} %fusion.49), kind=kOutput, calls=%fused_computation.8 | convolution fusion | flops 5483003904 | bytes 25952256 | tf_op jit(solution)/shard_map/rd,tcd->trc/dot_general | solution.py:575
  325.5 10.7 %multiply_reduce_fusion = (f32[1152]{0:T(1024)}, f32[512]{0:T(512)S(1)}, f32[512]{0:T(512)S(1)}, f32[1152]{0:T(1024)}, f32[512,1152]{1,0:T(8,128)}) fusion(f32[512,1152]{1,0:T(8,128)S(1)} %get-tuple-element.183, f32[512]{0:T(512)S(1)} %copy-done.89, f32[512]{0:T(512)S(1)} %copy-done.83, f32[1152]{0:T(1024)S(1)} %copy-done.74, ...), kind=kOutput, calls=%fused_computation.88 | convolution fusion | flops 5441123328 | bytes 20076032 | tf_op jit(solution)/shard_map/trc,tdc->rd/dot_general | solution.py:583
  373.0 5.4 pad_maximum_fusion
  378.4 7.1 %convolution_convert_fusion.1 = bf16[4,1152,576]{1,2,0:T(8,128)(2,1)S(1)} fusion(bf16[4,1024,1152]{1,2,0:T(8,128)(2,1)S(1)} %pad_maximum_fusion, bf16[512,576]{0,1:T(8,128)(2,1)} %collective-permute-done.39, bf16[512,576]{0,1:T(8,128)(2,1)S(1)} %bitcast.351), kind=kOutput, calls=%fused_computation.25 | convolution fusion | flops 5440831488 | bytes 15925248 | tf_op jit(solution)/shard_map/rd,trc->tdc/dot_general | solution.py:546
  393.6 4.5 all-to-all-start.7
  403.5 16.6 %attend_back.2 = bf16[2,3,4,72,1024]{4,3,2,1,0:T(8,128)(2,1)} custom-call(bf16[4,12,72,1024]{3,2,1,0:T(8,128)(2,1)} %bitcast.288, bf16[4,12,72,1024]{3,2,1,0:T(8,128)(2,1)} %bitcast.289, bf16[4,12,72,1024]{3,2,1,0:T(8,128)(2,1)} %bitcast.290, bf16[4,12,72,1024]{3,2,1,0:T(8,128)(2,1)} %bitcast.291, bf16[4,12,72,1024]{3,2,1,0:T(8,128)(2,1)} %bitcast.292, ...), custom_call_target="tpu_custom_call" | custom-call | flops 6039797760 | bytes 7077888 | tf_op jit(solution)/shard_map/attend_back/pallas_call | solution.py:352
  420.1 12.1 %collective-permute-done.43 = bf16[2,2,80,576]{3,2,0,1:T(8,128)(2,1)S(1)} collective-permute-done((bf16[2,2,80,576]{3,2,0,1:T(8,128)(2,1)S(1)}, bf16[2,2,80,576]{3,2,0,1:T(8,128)(2,1)S(1)}, u32[]{:S(2)}, u32[]{:S(2)}) %collective-permute-start.43) | collective-permute-done | bytes 368672 | tf_op jit(solution)/shard_map/ppermute | solution.py:91
  434.6 16.8 %attend_back.3 = bf16[2,3,4,72,1024]{4,3,2,1,0:T(8,128)(2,1)} custom-call(bf16[4,12,72,1024]{3,2,1,0:T(8,128)(2,1)} %bitcast.293, bf16[4,12,72,1024]{3,2,1,0:T(8,128)(2,1)} %bitcast.294, bf16[4,12,72,1024]{3,2,1,0:T(8,128)(2,1)} %bitcast.295, bf16[4,12,72,1024]{3,2,1,0:T(8,128)(2,1)} %bitcast.296, bf16[4,12,72,1024]{3,2,1,0:T(8,128)(2,1)} %bitcast.297, ...), custom_call_target="tpu_custom_call" | custom-call | flops 6039797760 | bytes 7077888 | tf_op jit(solution)/shard_map/attend_back/pallas_call | solution.py:352
  455.4 5.4 pad_maximum_fusion.1
  460.8 5.9 step.5
  479.8 4.4 all-to-all-start.10
  484.2 7.3 %pad_maximum_fusion.3 = bf16[2,864,2048]{2,1,0:T(8,128)(2,1)} fusion(bf16[2,864,1024]{2,1,0:T(8,128)(2,1)} %collective-permute-done.47, bf16[2,864,1024]{2,1,0:T(8,128)(2,1)} %bitcast.304), kind=kLoop, calls=%fused_computation.21 | loop fusion | flops 14155776 | bytes 14155776 | tf_op jit(solution)/shard_map/concatenate | solution.py:536
  491.6 8.2 %convolution_convert_fusion.6 = bf16[2,864,576]{1,2,0:T(8,128)(2,1)S(1)} fusion(bf16[2,864,2048]{2,1,0:T(8,128)(2,1)} %pad_maximum_fusion.3, bf16[1024,576]{0,1:T(8,128)(2,1)} %collective-permute-done.51, bf16[1024,576]{0,1:T(8,128)(2,1)} %bitcast.349), kind=kOutput, calls=%fused_computation.105 | convolution fusion | flops 4082577408 | bytes 11427840 | tf_op jit(solution)/shard_map/rd,tcr->tdc/dot_general | solution.py:546
  499.8 9.2 %fusion.21 = bf16[512,1152]{1,0:T(8,128)(2,1)} fusion(bf16[4,1152,864]{2,1,0:T(8,128)(2,1)} %bitcast.323, bf16[4,864,1024]{2,1,0:T(8,128)(2,1)S(1)} %bitcast.326), kind=kOutput, calls=%fused_computation.45 | convolution fusion | flops 2718498816 | bytes 9437184 | tf_op jit(solution)/shard_map/tcr,tdc->rd/dot_general | solution.py:628
  519.0 6.0 pad_maximum_fusion.2
  525.0 8.6 %convolution_convert_fusion.5 = bf16[2,864,576]{1,2,0:T(8,128)(2,1)S(1)} fusion(bf16[2,864,2048]{2,1,0:T(8,128)(2,1)} %pad_maximum_fusion.2, bf16[1024,576]{0,1:T(8,128)(2,1)} %collective-permute-done.51, bf16[1024,576]{0,1:T(8,128)(2,1)S(1)} %bitcast.350), kind=kOutput, calls=%fused_computation.104 | convolution fusion | flops 4082577408 | bytes 11427840 | tf_op jit(solution)/shard_map/rd,tcr->tdc/dot_general | solution.py:546
  535.7 7.6 %convolution_bitcast_fusion.1 = f32[512,1152]{1,0:T(8,128)S(1)} fusion(bf16[4,864,512]{2,1,0:T(8,128)(2,1)S(1)} %copy-done.40, bf16[4,1152,864]{2,1,0:T(8,128)(2,1)} %bitcast.324), kind=kOutput, calls=%fused_computation.40 | convolution fusion | flops 4076863488 | bytes 13860864 | tf_op jit(solution)/shard_map/tcr,tdc->rd/dot_general | solution.py:643
  545.6 9.1 %fusion.50 = (f32[1152]{0:T(1024)S(1)}, bf16[512,1152]{1,0:T(8,128)(2,1)}) fusion(bf16[512,1152]{1,0:T(8,128)(2,1)S(1)} %copy-done.28, f32[512,1152]{1,0:T(8,128)S(1)} %copy-done.5, f32[1152]{0:T(1024)S(1)} %copy-done.85, bf16[4,512,1152]{1,2,0:T(8,128)(2,1)} %copy-done.30, bf16[4,1152,1152]{2,1,0:T(8,128)(2,1)S(1)} %bitcast.312), kind=kOutput, calls=%fused_computation.80 | convolution fusion | flops 5439355904 | bytes 20063232 | tf_op jit(solution)/shard_map/trc,tcd->rd/dot_general | solution.py:649
  566.3 4.5 all-to-all-done.8
  588.2 15.0 %all-to-all-done.9.grads_ref = bf16[4,144,1152]{2,1,0:T(8,128)(2,1)S(1)} async-done(((bf16[4,144,1152]{2,1,0:T(8,128)(2,1)}), bf16[4,144,1152]{2,1,0:T(8,128)(2,1)S(1)}, u32[]{:S(2)}, u32[]{:S(2)}) %all-to-all-start.9) | async-done | bytes 1327136 | tf_op jit(solution)/shard_map/all_to_all | solution.py:86
  604.3 5.9 step.7
  619.4 4.8 all-to-all-done.11
  648.8 4.2 all-to-all-start.14
  653.0 4.3 fusion.42
  659.8 7.2 %step.8 = (f32[144,72,72]{2,1,0:T(8,128)}, f32[144,72,72]{2,1,0:T(8,128)}, f32[2,144,72,72]{3,2,1,0:T(8,128)}) custom-call(f32[1,144,1728]{2,1,0:T(8,128)} %convolution_bitcast_fusion.3.grads_ref, f32[144,72,72]{2,1,0:T(8,128)} %master_ref.9, f32[144,72,72]{2,1,0:T(8,128)} %moment_ref.9, ...), custom_call_target="tpu_custom_call", output_to_operand_aliasing={{0}: (5, {}), {1}: (6, {}), {2}: (7, {})} | custom-call | flops 17694720 | bytes 17694720 | tf_op jit(solution)/shard_map/step/pallas_call | solution.py:408
  668.5 9.0 %all-to-all-done.14.grads_ref = bf16[4,144,864]{2,1,0:T(8,128)(2,1)} async-done(((bf16[4,144,864]{2,1,0:T(8,128)(2,1)}), bf16[4,144,864]{2,1,0:T(8,128)(2,1)}, u32[]{:S(2)}, u32[]{:S(2)}) %all-to-all-start.14) | async-done | bytes 995360 | tf_op jit(solution)/shard_map/all_to_all | solution.py:86
  677.5 4.9 step.9
  (484 shorter events, 274.7 us)
Async XLA Ops:
  24.8 30.2 %all-to-all-start.3 = ((bf16[4,144,864]{2,1,0:T(8,128)(2,1)}), bf16[4,144,864]{2,1,0:T(8,128)(2,1)S(1)}, u32[]{:S(2)}, u32[]{:S(2)}) async-start(bf16[4,144,864]{2,1,0:T(8,128)(2,1)} %broadcast_in_dim.63), calls=%async_computation.3 | async-start | bytes 2064384 | tf_op jit(solution)/shard_map/all_to_all | solution.py:86
  60.6 43.2 %collective-permute-start.8 = (bf16[512,1152]{1,0:T(8,128)(2,1)S(1)}, bf16[512,1152]{1,0:T(8,128)(2,1)S(1)}, u32[]{:S(2)}, u32[]{:S(2)}) collective-permute-start(bf16[512,1152]{1,0:T(8,128)(2,1)S(1)} %copy-done.2), channel_id=1, source_target_pairs={{0,1},{1,0},{2,3},{3,2},{4,5},{5,4},{6,7},{7,6},{8,9},{9,8},{10,11... | collective-permute-start | bytes 3538952 | tf_op jit(solution)/shard_map/ppermute | solution.py:101
  66.8 44.2 %all-to-all-start.4 = ((bf16[4,144,1152]{2,1,0:T(8,128)(2,1)}), bf16[4,144,1152]{2,1,0:T(8,128)(2,1)}, u32[]{:S(2)}, u32[]{:S(2)}) async-start(bf16[4,144,1152]{2,1,0:T(8,128)(2,1)} %broadcast_in_dim.66), calls=%async_computation.4 | async-start | bytes 2654208 | tf_op jit(solution)/shard_map/all_to_all | solution.py:86
  85.4 23.8 %collective-permute-start.5 = (bf16[2,2,144,864]{3,2,1,0:T(8,128)(2,1)S(1)}, bf16[2,2,144,864]{3,2,1,0:T(8,128)(2,1)}, u32[]{:S(2)}, u32[]{:S(2)}) collective-permute-start(bf16[2,2,144,864]{3,2,1,0:T(8,128)(2,1)S(1)} %pad_maximum_fusion.14.refs_4_), channel_id=1, source_target_pairs={{0,8},{4,12},{8,0},{12,4},{16,24},{20,28},{24,16},{28,20},{1,9},{5... | collective-permute-start | bytes 2985992 | tf_op jit(solution)/shard_map/ppermute | solution.py:91
  91.0 20.0 %collective-permute-start.1 = (bf16[2,2,144,864]{3,2,1,0:T(8,128)(2,1)}, bf16[2,2,144,864]{3,2,1,0:T(8,128)(2,1)}, u32[]{:S(2)}, u32[]{:S(2)}) collective-permute-start(bf16[2,2,144,864]{3,2,1,0:T(8,128)(2,1)} %pad_maximum_fusion.13.refs_0_), channel_id=1, source_target_pairs={{0,16},{4,20},{8,24},{12,28},{16,0},{20,4},{24,8},{28,12},{1,17},{... | collective-permute-start | bytes 2985992 | tf_op jit(solution)/shard_map/ppermute | solution.py:91
  97.3 23.5 %collective-permute-start.6 = (bf16[2,2,144,864]{3,2,1,0:T(8,128)(2,1)S(1)}, bf16[2,2,144,864]{3,2,1,0:T(8,128)(2,1)}, u32[]{:S(2)}, u32[]{:S(2)}) collective-permute-start(bf16[2,2,144,864]{3,2,1,0:T(8,128)(2,1)S(1)} %pad_maximum_fusion.14.refs_4_), channel_id=1, source_target_pairs={{0,4},{4,0},{8,12},{12,8},{16,20},{20,16},{24,28},{28,24},{1,5},{5... | collective-permute-start | bytes 2985992 | tf_op jit(solution)/shard_map/ppermute | solution.py:91
  97.3 26.9 %collective-permute-start.2 = (bf16[2,2,144,864]{3,2,1,0:T(8,128)(2,1)}, bf16[2,2,144,864]{3,2,1,0:T(8,128)(2,1)}, u32[]{:S(2)}, u32[]{:S(2)}) collective-permute-start(bf16[2,2,144,864]{3,2,1,0:T(8,128)(2,1)} %pad_maximum_fusion.13.refs_0_), channel_id=1, source_target_pairs={{0,4},{4,0},{8,12},{12,8},{16,20},{20,16},{24,28},{28,24},{1,5},{5... | collective-permute-start | bytes 2985992 | tf_op jit(solution)/shard_map/ppermute | solution.py:91
  113.5 22.3 %collective-permute-start.10 = (bf16[1,2,144,1152]{3,2,1,0:T(8,128)(2,1)}, bf16[1,2,144,1152]{3,2,1,0:T(8,128)(2,1)}, u32[]{:S(2)}, u32[]{:S(2)}) collective-permute-start(bf16[1,2,144,1152]{3,2,1,0:T(8,128)(2,1)} %get-tuple-element.214), channel_id=1, source_target_pairs={{0,16},{4,20},{8,24},{12,28},{16,0},{20,4},{24,8},{28,12},{1,17},{... | collective-permute-start | bytes 1990664 | tf_op jit(solution)/shard_map/ppermute | solution.py:91
  120.7 18.8 %collective-permute-start.9 = (bf16[1,2,144,1152]{3,2,1,0:T(8,128)(2,1)}, bf16[1,2,144,1152]{3,2,1,0:T(8,128)(2,1)}, u32[]{:S(2)}, u32[]{:S(2)}) collective-permute-start(bf16[1,2,144,1152]{3,2,1,0:T(8,128)(2,1)} %get-tuple-element.215), channel_id=1, source_target_pairs={{0,8},{4,12},{8,0},{12,4},{16,24},{20,28},{24,16},{28,20},{1,9},{5... | collective-permute-start | bytes 1990664 | tf_op jit(solution)/shard_map/ppermute | solution.py:91
  138.3 42.5 %collective-permute-start.12 = (bf16[2,2,144,1152]{3,2,1,0:T(8,128)(2,1)}, bf16[2,2,144,1152]{3,2,1,0:T(8,128)(2,1)}, u32[]{:S(2)}, u32[]{:S(2)}) collective-permute-start(bf16[2,2,144,1152]{3,2,1,0:T(8,128)(2,1)} %pad_maximum_fusion.7.refs_4_), channel_id=1, source_target_pairs={{0,8},{4,12},{8,0},{12,4},{16,24},{20,28},{24,16},{28,20},{1,9},{5... | collective-permute-start | bytes 3981320 | tf_op jit(solution)/shard_map/ppermute | solution.py:91
  141.9 49.6 %collective-permute-start.11 = (bf16[2,2,144,1152]{3,2,1,0:T(8,128)(2,1)}, bf16[2,2,144,1152]{3,2,1,0:T(8,128)(2,1)}, u32[]{:S(2)}, u32[]{:S(2)}) collective-permute-start(bf16[2,2,144,1152]{3,2,1,0:T(8,128)(2,1)} %pad_maximum_fusion.6.refs_0_), channel_id=1, source_target_pairs={{0,16},{4,20},{8,24},{12,28},{16,0},{20,4},{24,8},{28,12},{1,17},{... | collective-permute-start | bytes 3981320 | tf_op jit(solution)/shard_map/ppermute | solution.py:91
  144.1 36.2 %collective-permute-start.14 = (bf16[2,2,80,576]{3,2,1,0:T(8,128)(2,1)}, bf16[2,2,80,576]{3,2,1,0:T(8,128)(2,1)}, u32[]{:S(2)}, u32[]{:S(2)}) collective-permute-start(bf16[2,2,80,576]{3,2,1,0:T(8,128)(2,1)} %pad_maximum_fusion.16.refs_0_), channel_id=1, source_target_pairs={{0,16},{4,20},{8,24},{12,28},{16,0},{20,4},{24,8},{28,12},{1,17},{... | collective-permute-start | bytes 1105928 | tf_op jit(solution)/shard_map/ppermute | solution.py:91
  145.5 34.8 %collective-permute-start.18 = (bf16[2,2,80,576]{3,2,1,0:T(8,128)(2,1)}, bf16[2,2,80,576]{3,2,1,0:T(8,128)(2,1)}, u32[]{:S(2)}, u32[]{:S(2)}) collective-permute-start(bf16[2,2,80,576]{3,2,1,0:T(8,128)(2,1)} %pad_maximum_fusion.17.refs_4_), channel_id=1, source_target_pairs={{0,8},{4,12},{8,0},{12,4},{16,24},{20,28},{24,16},{28,20},{1,9},{5... | collective-permute-start | bytes 1105928 | tf_op jit(solution)/shard_map/ppermute | solution.py:91
  163.2 52.8 %all-to-all-start.6 = ((bf16[4,144,1152]{2,1,0:T(8,128)(2,1)}), bf16[4,144,1152]{2,1,0:T(8,128)(2,1)}, u32[]{:S(2)}, u32[]{:S(2)}) async-start(bf16[4,144,1152]{2,1,0:T(8,128)(2,1)} %broadcast_in_dim.72), calls=%async_computation.6 | async-start | bytes 2654208 | tf_op jit(solution)/shard_map/all_to_all | solution.py:86
  168.4 34.1 %collective-permute-start.15 = (bf16[2,2,80,576]{3,2,1,0:T(8,128)(2,1)}, bf16[2,2,80,576]{3,2,1,0:T(8,128)(2,1)S(1)}, u32[]{:S(2)}, u32[]{:S(2)}) collective-permute-start(bf16[2,2,80,576]{3,2,1,0:T(8,128)(2,1)} %pad_maximum_fusion.16.refs_0_), channel_id=1, source_target_pairs={{0,4},{4,0},{8,12},{12,8},{16,20},{20,16},{24,28},{28,24},{1,5},{5... | collective-permute-start | bytes 1105928 | tf_op jit(solution)/shard_map/ppermute | solution.py:91
  180.3 22.4 %collective-permute-start.19 = (bf16[2,2,80,576]{3,2,1,0:T(8,128)(2,1)}, bf16[2,2,80,576]{3,2,1,0:T(8,128)(2,1)S(1)}, u32[]{:S(2)}, u32[]{:S(2)}) collective-permute-start(bf16[2,2,80,576]{3,2,1,0:T(8,128)(2,1)} %pad_maximum_fusion.17.refs_4_), channel_id=1, source_target_pairs={{0,4},{4,0},{8,12},{12,8},{16,20},{20,16},{24,28},{28,24},{1,5},{5... | collective-permute-start | bytes 1105928 | tf_op jit(solution)/shard_map/ppermute | solution.py:91
  180.3 22.8 %collective-permute-start.16 = (bf16[2,2,80,576]{3,2,1,0:T(8,128)(2,1)}, bf16[2,2,80,576]{3,2,1,0:T(8,128)(2,1)S(1)}, u32[]{:S(2)}, u32[]{:S(2)}) collective-permute-start(bf16[2,2,80,576]{3,2,1,0:T(8,128)(2,1)} %collective-permute-done.14.refs_1_), channel_id=1, source_target_pairs={{0,4},{4,0},{8,12},{12,8},{16,20},{20,16},{24,28},{28,24},{1,5},{5... | collective-permute-start | bytes 1105928 | tf_op jit(solution)/shard_map/ppermute | solution.py:91
  180.8 22.4 %collective-permute-start.20 = (bf16[2,2,80,576]{3,2,1,0:T(8,128)(2,1)}, bf16[2,2,80,576]{3,2,1,0:T(8,128)(2,1)S(1)}, u32[]{:S(2)}, u32[]{:S(2)}) collective-permute-start(bf16[2,2,80,576]{3,2,1,0:T(8,128)(2,1)} %collective-permute-done.18.refs_5_), channel_id=1, source_target_pairs={{0,4},{4,0},{8,12},{12,8},{16,20},{20,16},{24,28},{28,24},{1,5},{5... | collective-permute-start | bytes 1105928 | tf_op jit(solution)/shard_map/ppermute | solution.py:91
  191.4 28.0 %collective-permute-start.23 = (bf16[2,2,144,1152]{3,2,1,0:T(8,128)(2,1)}, bf16[2,2,144,1152]{3,2,1,0:T(8,128)(2,1)}, u32[]{:S(2)}, u32[]{:S(2)}) collective-permute-start(bf16[2,2,144,1152]{3,2,1,0:T(8,128)(2,1)} %pad_maximum_fusion.7.refs_4_), channel_id=1, source_target_pairs={{0,4},{4,0},{8,12},{12,8},{16,20},{20,16},{24,28},{28,24},{1,5},{5... | collective-permute-start | bytes 3981320 | tf_op jit(solution)/shard_map/ppermute | solution.py:91
  257.4 31.4 %collective-permute-start.30 = (bf16[2,2,144,1152]{3,2,1,0:T(8,128)(2,1)}, bf16[2,2,144,1152]{3,2,1,0:T(8,128)(2,1)}, u32[]{:S(2)}, u32[]{:S(2)}) collective-permute-start(bf16[2,2,144,1152]{3,2,1,0:T(8,128)(2,1)} %pad_maximum_fusion.9.refs_4_), channel_id=1, source_target_pairs={{0,8},{4,12},{8,0},{12,4},{16,24},{20,28},{24,16},{28,20},{1,9},{5... | collective-permute-start | bytes 3981320 | tf_op jit(solution)/shard_map/ppermute | solution.py:91
  258.1 31.1 %collective-permute-start.29 = (bf16[2,2,144,1152]{3,2,1,0:T(8,128)(2,1)}, bf16[2,2,144,1152]{3,2,1,0:T(8,128)(2,1)}, u32[]{:S(2)}, u32[]{:S(2)}) collective-permute-start(bf16[2,2,144,1152]{3,2,1,0:T(8,128)(2,1)} %pad_maximum_fusion.8.refs_0_), channel_id=1, source_target_pairs={{0,16},{4,20},{8,24},{12,28},{16,0},{20,4},{24,8},{28,12},{1,17},{... | collective-permute-start | bytes 3981320 | tf_op jit(solution)/shard_map/ppermute | solution.py:91
  266.7 29.2 %collective-permute-start.34 = (bf16[2,2,144,1152]{3,2,1,0:T(8,128)(2,1)}, bf16[2,2,144,1152]{3,2,1,0:T(8,128)(2,1)S(1)}, u32[]{:S(2)}, u32[]{:S(2)}) collective-permute-start(bf16[2,2,144,1152]{3,2,1,0:T(8,128)(2,1)} %pad_maximum_fusion.9.refs_4_), channel_id=1, source_target_pairs={{0,4},{4,0},{8,12},{12,8},{16,20},{20,16},{24,28},{28,24},{1,5},{5... | collective-permute-start | bytes 3981320 | tf_op jit(solution)/shard_map/ppermute | solution.py:91
  266.7 30.6 %collective-permute-start.32 = (bf16[2,2,144,1152]{3,2,1,0:T(8,128)(2,1)}, bf16[2,2,144,1152]{3,2,1,0:T(8,128)(2,1)S(1)}, u32[]{:S(2)}, u32[]{:S(2)}) collective-permute-start(bf16[2,2,144,1152]{3,2,1,0:T(8,128)(2,1)} %pad_maximum_fusion.8.refs_0_), channel_id=1, source_target_pairs={{0,4},{4,0},{8,12},{12,8},{16,20},{20,16},{24,28},{28,24},{1,5},{5... | collective-permute-start | bytes 3981320 | tf_op jit(solution)/shard_map/ppermute | solution.py:91
  292.1 47.9 %collective-permute-start.38 = (bf16[2,2,144,1152]{3,2,0,1:T(8,128)(2,1)}, bf16[2,2,144,1152]{3,2,0,1:T(8,128)(2,1)}, u32[]{:S(2)}, u32[]{:S(2)}) collective-permute-start(bf16[2,2,144,1152]{3,2,0,1:T(8,128)(2,1)} %bitcast.270), channel_id=1, source_target_pairs={{0,8},{4,12},{8,0},{12,4},{16,24},{20,28},{24,16},{28,20},{1,9},{5... | collective-permute-start | bytes 3981320 | tf_op jit(solution)/shard_map/ppermute | solution.py:91
  295.9 44.2 %collective-permute-start.31 = (bf16[2,2,144,1152]{3,2,0,1:T(8,128)(2,1)}, bf16[2,2,144,1152]{3,2,0,1:T(8,128)(2,1)}, u32[]{:S(2)}, u32[]{:S(2)}) collective-permute-start(bf16[2,2,144,1152]{3,2,0,1:T(8,128)(2,1)} %bitcast.271), channel_id=1, source_target_pairs={{0,16},{4,20},{8,24},{12,28},{16,0},{20,4},{24,8},{28,12},{1,17},{... | collective-permute-start | bytes 3981320 | tf_op jit(solution)/shard_map/ppermute | solution.py:91
  336.2 36.7 %collective-permute-start.37 = (bf16[4,512,1152]{1,2,0:T(8,128)(2,1)}, bf16[4,512,1152]{1,2,0:T(8,128)(2,1)}, u32[]{:S(2)}, u32[]{:S(2)}) collective-permute-start(bf16[4,512,1152]{1,2,0:T(8,128)(2,1)} %fusion.6), channel_id=1, source_target_pairs={{0,4},{4,0},{8,12},{12,8},{16,20},{20,16},{24,28},{28,24},{1,5},{5... | collective-permute-start | bytes 14155784 | tf_op jit(solution)/shard_map/ppermute | solution.py:91
  356.3 22.1 %collective-permute-start.39 = (bf16[512,576]{0,1:T(8,128)(2,1)}, bf16[512,576]{0,1:T(8,128)(2,1)}, u32[]{:S(2)}, u32[]{:S(2)}) collective-permute-start(bf16[512,576]{0,1:T(8,128)(2,1)} %bitcast.55), channel_id=1, source_target_pairs={{0,4},{4,0},{8,12},{12,8},{16,20},{20,16},{24,28},{28,24},{1,5},{5... | collective-permute-start | bytes 1769480 | tf_op jit(solution)/shard_map/ppermute | solution.py:91
  357.3 28.3 %collective-permute-start.40 = (bf16[2,144,1152]{2,1,0:T(8,128)(2,1)}, bf16[2,144,1152]{2,1,0:T(8,128)(2,1)}, u32[]{:S(2)}, u32[]{:S(2)}) collective-permute-start(bf16[2,144,1152]{2,1,0:T(8,128)(2,1)} %dynamic-slice_bitcast_fusion.2), channel_id=1, source_target_pairs={{0,16},{4,20},{8,24},{12,28},{16,0},{20,4},{24,8},{28,12},{1,17},{... | collective-permute-start | bytes 1990664 | tf_op jit(solution)/shard_map/ppermute | solution.py:91
  358.9 28.0 %collective-permute-start.36 = (bf16[2,144,1152]{2,1,0:T(8,128)(2,1)}, bf16[2,144,1152]{2,1,0:T(8,128)(2,1)}, u32[]{:S(2)}, u32[]{:S(2)}) collective-permute-start(bf16[2,144,1152]{2,1,0:T(8,128)(2,1)} %dynamic-slice_bitcast_fusion.3), channel_id=1, source_target_pairs={{0,8},{4,12},{8,0},{12,4},{16,24},{20,28},{24,16},{28,20},{1,9},{5... | collective-permute-start | bytes 1990664 | tf_op jit(solution)/shard_map/ppermute | solution.py:91
  392.2 74.5 %collective-permute-start.49 = (bf16[2,2,144,1152]{3,2,0,1:T(8,128)(2,1)}, bf16[2,2,144,1152]{3,2,0,1:T(8,128)(2,1)}, u32[]{:S(2)}, u32[]{:S(2)}) collective-permute-start(bf16[2,2,144,1152]{3,2,0,1:T(8,128)(2,1)} %bitcast.268), channel_id=1, source_target_pairs={{0,8},{4,12},{8,0},{12,4},{16,24},{20,28},{24,16},{28,20},{1,9},{5... | collective-permute-start | bytes 3981320 | tf_op jit(solution)/shard_map/ppermute | solution.py:91
  393.6 67.2 %all-to-all-start.7 = ((bf16[4,144,1152]{2,1,0:T(8,128)(2,1)}), bf16[4,144,1152]{2,1,0:T(8,128)(2,1)}, u32[]{:S(2)}, u32[]{:S(2)}) async-start(bf16[4,144,1152]{2,1,0:T(8,128)(2,1)} %pad_maximum_fusion.10), calls=%async_computation.7 | async-start | bytes 2654208 | tf_op jit(solution)/shard_map/all_to_all | solution.py:86
  398.1 34.0 %collective-permute-start.43 = (bf16[2,2,80,576]{3,2,0,1:T(8,128)(2,1)S(1)}, bf16[2,2,80,576]{3,2,0,1:T(8,128)(2,1)S(1)}, u32[]{:S(2)}, u32[]{:S(2)}) collective-permute-start(bf16[2,2,80,576]{3,2,0,1:T(8,128)(2,1)S(1)} %bitcast.352), channel_id=1, source_target_pairs={{0,8},{4,12},{8,0},{12,4},{16,24},{20,28},{24,16},{28,20},{1,9},{5... | collective-permute-start | bytes 1105928 | tf_op jit(solution)/shard_map/ppermute | solution.py:91
  398.9 33.2 %collective-permute-start.42 = (bf16[2,2,80,576]{3,2,0,1:T(8,128)(2,1)}, bf16[2,2,80,576]{3,2,0,1:T(8,128)(2,1)S(1)}, u32[]{:S(2)}, u32[]{:S(2)}) collective-permute-start(bf16[2,2,80,576]{3,2,0,1:T(8,128)(2,1)} %bitcast.353), channel_id=1, source_target_pairs={{0,16},{4,20},{8,24},{12,28},{16,0},{20,4},{24,8},{28,12},{1,17},{... | collective-permute-start | bytes 1105928 | tf_op jit(solution)/shard_map/ppermute | solution.py:91
  402.8 65.3 %collective-permute-start.45 = (bf16[2,2,144,1152]{3,2,0,1:T(8,128)(2,1)}, bf16[2,2,144,1152]{3,2,0,1:T(8,128)(2,1)}, u32[]{:S(2)}, u32[]{:S(2)}) collective-permute-start(bf16[2,2,144,1152]{3,2,0,1:T(8,128)(2,1)} %bitcast.269), channel_id=1, source_target_pairs={{0,16},{4,20},{8,24},{12,28},{16,0},{20,4},{24,8},{28,12},{1,17},{... | collective-permute-start | bytes 3981320 | tf_op jit(solution)/shard_map/ppermute | solution.py:91
  420.1 64.1 %collective-permute-start.47 = (bf16[2,864,1024]{2,1,0:T(8,128)(2,1)}, bf16[2,864,1024]{2,1,0:T(8,128)(2,1)}, u32[]{:S(2)}, u32[]{:S(2)}) collective-permute-start(bf16[2,864,1024]{2,1,0:T(8,128)(2,1)} %bitcast.302), channel_id=1, source_target_pairs={{0,4},{4,0},{8,12},{12,8},{16,20},{20,16},{24,28},{28,24},{1,5},{5... | collective-permute-start | bytes 10616840 | tf_op jit(solution)/shard_map/ppermute | solution.py:91
  433.2 39.0 %collective-permute-start.50 = (bf16[2,80,576]{2,1,0:T(8,128)(2,1)}, bf16[2,80,576]{2,1,0:T(8,128)(2,1)}, u32[]{:S(2)}, u32[]{:S(2)}) collective-permute-start(bf16[2,80,576]{2,1,0:T(8,128)(2,1)} %dynamic-slice_bitcast_fusion.6), channel_id=1, source_target_pairs={{0,16},{4,20},{8,24},{12,28},{16,0},{20,4},{24,8},{28,12},{1,17},{... | collective-permute-start | bytes 552968 | tf_op jit(solution)/shard_map/ppermute | solution.py:91
  451.4 67.7 %collective-permute-start.44 = (bf16[2,864,1024]{2,1,0:T(8,128)(2,1)}, bf16[2,864,1024]{2,1,0:T(8,128)(2,1)}, u32[]{:S(2)}, u32[]{:S(2)}) collective-permute-start(bf16[2,864,1024]{2,1,0:T(8,128)(2,1)} %bitcast.298), channel_id=1, source_target_pairs={{0,4},{4,0},{8,12},{12,8},{16,20},{20,16},{24,28},{28,24},{1,5},{5... | collective-permute-start | bytes 10616840 | tf_op jit(solution)/shard_map/ppermute | solution.py:91
  468.1 23.4 %collective-permute-start.51 = (bf16[1024,576]{0,1:T(8,128)(2,1)}, bf16[1024,576]{0,1:T(8,128)(2,1)}, u32[]{:S(2)}, u32[]{:S(2)}) collective-permute-start(bf16[1024,576]{0,1:T(8,128)(2,1)} %bitcast.85), channel_id=1, source_target_pairs={{0,4},{4,0},{8,12},{12,8},{16,20},{20,16},{24,28},{28,24},{1,5},{5... | collective-permute-start | bytes 3538952 | tf_op jit(solution)/shard_map/ppermute | solution.py:91
  475.2 33.9 %collective-permute-start.52 = (bf16[2,144,1152]{2,1,0:T(8,128)(2,1)}, bf16[2,144,1152]{2,1,0:T(8,128)(2,1)}, u32[]{:S(2)}, u32[]{:S(2)}) collective-permute-start(bf16[2,144,1152]{2,1,0:T(8,128)(2,1)} %dynamic-slice_bitcast_fusion), channel_id=1, source_target_pairs={{0,16},{4,20},{8,24},{12,28},{16,0},{20,4},{24,8},{28,12},{1,17},{... | collective-permute-start | bytes 1990664 | tf_op jit(solution)/shard_map/ppermute | solution.py:91
  476.7 32.4 %collective-permute-start.46 = (bf16[2,144,1152]{2,1,0:T(8,128)(2,1)}, bf16[2,144,1152]{2,1,0:T(8,128)(2,1)}, u32[]{:S(2)}, u32[]{:S(2)}) collective-permute-start(bf16[2,144,1152]{2,1,0:T(8,128)(2,1)} %dynamic-slice_bitcast_fusion.1), channel_id=1, source_target_pairs={{0,8},{4,12},{8,0},{12,4},{16,24},{20,28},{24,16},{28,20},{1,9},{5... | collective-permute-start | bytes 1990664 | tf_op jit(solution)/shard_map/ppermute | solution.py:91
  479.8 81.4 %all-to-all-start.10 = ((bf16[4,72,576]{2,1,0:T(8,128)(2,1)}), bf16[4,72,576]{2,1,0:T(8,128)(2,1)}, u32[]{:S(2)}, u32[]{:S(2)}) async-start(bf16[4,72,576]{2,1,0:T(8,128)(2,1)} %pad_maximum_fusion.18), calls=%async_computation.10 | async-start | bytes 737280 | tf_op jit(solution)/shard_map/all_to_all | solution.py:86
  515.6 59.0 %collective-permute-start.54 = (bf16[2,2,144,864]{3,2,0,1:T(8,128)(2,1)}, bf16[2,2,144,864]{3,2,0,1:T(8,128)(2,1)}, u32[]{:S(2)}, u32[]{:S(2)}) collective-permute-start(bf16[2,2,144,864]{3,2,0,1:T(8,128)(2,1)} %bitcast.273), channel_id=1, source_target_pairs={{0,16},{4,20},{8,24},{12,28},{16,0},{20,4},{24,8},{28,12},{1,17},{... | collective-permute-start | bytes 2985992 | tf_op jit(solution)/shard_map/ppermute | solution.py:91
  517.0 38.3 %collective-permute-start.53 = (bf16[512,1152]{1,0:T(8,128)(2,1)}, bf16[512,1152]{1,0:T(8,128)(2,1)S(1)}, u32[]{:S(2)}, u32[]{:S(2)}) collective-permute-start(bf16[512,1152]{1,0:T(8,128)(2,1)} %fusion.21), channel_id=1, source_target_pairs={{0,1},{1,0},{2,3},{3,2},{4,5},{5,4},{6,7},{7,6},{8,9},{9,8},{10,11... | collective-permute-start | bytes 3538952 | tf_op jit(solution)/shard_map/ppermute | solution.py:101
  544.5 30.1 %collective-permute-start.56 = (bf16[2,2,144,864]{3,2,0,1:T(8,128)(2,1)}, bf16[2,2,144,864]{3,2,0,1:T(8,128)(2,1)}, u32[]{:S(2)}, u32[]{:S(2)}) collective-permute-start(bf16[2,2,144,864]{3,2,0,1:T(8,128)(2,1)} %bitcast.272), channel_id=1, source_target_pairs={{0,8},{4,12},{8,0},{12,4},{16,24},{20,28},{24,16},{28,20},{1,9},{5... | collective-permute-start | bytes 2985992 | tf_op jit(solution)/shard_map/ppermute | solution.py:91
  570.8 32.4 %all-to-all-start.9 = ((bf16[4,144,1152]{2,1,0:T(8,128)(2,1)}), bf16[4,144,1152]{2,1,0:T(8,128)(2,1)S(1)}, u32[]{:S(2)}, u32[]{:S(2)}) async-start(bf16[4,144,1152]{2,1,0:T(8,128)(2,1)} %pad_maximum_fusion.11), calls=%async_computation.9 | async-start | bytes 2654208 | tf_op jit(solution)/shard_map/all_to_all | solution.py:86
  577.1 33.1 %collective-permute-start.57 = (bf16[2,144,864]{2,1,0:T(8,128)(2,1)}, bf16[2,144,864]{2,1,0:T(8,128)(2,1)}, u32[]{:S(2)}, u32[]{:S(2)}) collective-permute-start(bf16[2,144,864]{2,1,0:T(8,128)(2,1)} %dynamic-slice_bitcast_fusion.4), channel_id=1, source_target_pairs={{0,16},{4,20},{8,24},{12,28},{16,0},{20,4},{24,8},{28,12},{1,17},{... | collective-permute-start | bytes 1493000 | tf_op jit(solution)/shard_map/ppermute | solution.py:91
  580.0 32.2 %collective-permute-start.55 = (bf16[2,144,864]{2,1,0:T(8,128)(2,1)}, bf16[2,144,864]{2,1,0:T(8,128)(2,1)}, u32[]{:S(2)}, u32[]{:S(2)}) collective-permute-start(bf16[2,144,864]{2,1,0:T(8,128)(2,1)} %dynamic-slice_bitcast_fusion.5), channel_id=1, source_target_pairs={{0,8},{4,12},{8,0},{12,4},{16,24},{20,28},{24,16},{28,20},{1,9},{5... | collective-permute-start | bytes 1493000 | tf_op jit(solution)/shard_map/ppermute | solution.py:91
  648.8 28.7 %all-to-all-start.14 = ((bf16[4,144,864]{2,1,0:T(8,128)(2,1)}), bf16[4,144,864]{2,1,0:T(8,128)(2,1)}, u32[]{:S(2)}, u32[]{:S(2)}) async-start(bf16[4,144,864]{2,1,0:T(8,128)(2,1)} %pad_maximum_fusion.15), calls=%async_computation.14 | async-start | bytes 2064384 | tf_op jit(solution)/shard_map/all_to_all | solution.py:86
  (127 other events, 1258.3 us)

commit v3 on v2

--- a/solution.py
+++ b/solution.py
@@ -20,6 +20,16 @@
 bf16 = jnp.bfloat16
 f32 = jnp.float32
 VMEM_LIMIT = 56 * 1024 * 1024
+SCALE = 0.001
+TIMES = dict(
+    first=6, middle=8, up=15, down=13, down_back=12, up_back=16, out_back=9, weight_grads=11, qkv_back=16, last=6
+)
+
+
+def cost(microseconds):
+    return pl.CostEstimate(
+        flops=int(SCALE * microseconds * 1.15e9), bytes_accessed=1024, transcendentals=0
+    )
 
 
 def layer_norm(values):
@@ -105,22 +115,36 @@
     return exchange(slots, "tensor")
 
 
+def shift_t(values, k):
+    size = lax.axis_size("tensor")
+    return lax.ppermute(values, "tensor", [(n, (n + k) % size) for n in range(size)])
+
+
 def after(values, *earlier):
     return lax.optimization_barrier((values, *earlier))[0]
 
 
 class Gathering:
-    def __init__(self, piece, bits, *earlier):
+    def __init__(self, piece, bits, *earlier, relative=False):
         self.bits = bits
         size = lax.axis_size("tensor")
         piece = after(piece, *earlier) if earlier else piece
-        self.slots = exchange_t(jnp.broadcast_to(piece, (size,) + piece.shape))
+        if relative:
+            self.slots = [piece] + [shift_t(piece, k) for k in range(1, size)]
+        else:
+            self.slots = exchange_t(jnp.broadcast_to(piece, (size,) + piece.shape))
 
     def start(self, *earlier):
-        half = self.slots.shape[0] // 2
-        slots = after(self.slots, *earlier) if earlier else self.slots
+        size = lax.axis_size("tensor")
+        half = size // 2
+        slots = self.slots
+        if isinstance(slots, list):
+            self.stacks = [jnp.stack(slots[n : n + half])[None] for n in (0, half)]
+        else:
+            self.stacks = [slots[None, :half], slots[None, half:]]
+        if earlier:
+            self.stacks = [after(stack, *earlier) for stack in self.stacks]
         self.masks = [[0], [0]]
-        self.stacks = [slots[None, :half], slots[None, half:]]
         self.orders = [self.bits, self.bits[::-1]]
         return self.send()
 
@@ -129,8 +153,9 @@
         return self
 
     def join(self, *earlier):
+        landed = lax.optimization_barrier((*self.flying, *earlier))
         for n, order in enumerate(self.orders):
-            got = after(self.flying[n], *earlier) if earlier else self.flying[n]
+            got = landed[n]
             self.masks[n] = self.masks[n] + [mask ^ order[0] for mask in self.masks[n]]
             self.stacks[n] = jnp.concatenate([self.stacks[n], got])
         self.orders = [order[1:] for order in self.orders]
@@ -145,8 +170,7 @@
         return self
 
     def cross(self, *earlier):
-        if earlier:
-            self.flying = [after(got, *earlier) for got in self.flying]
+        self.flying = list(lax.optimization_barrier((*self.flying, *earlier))[:2])
         self.last = [bit_swap(got, 1) for got in self.flying]
         return self.flying
 
@@ -172,16 +196,44 @@
         return assemble(found, dp_size, where)
 
 
-def assemble_kernel(plan, where, *refs):
+class WholeGathering:
+    def __init__(self, piece, bits, *earlier):
+        size = lax.axis_size("tensor")
+        piece = after(piece, *earlier)
+        self.stack = exchange_t(jnp.broadcast_to(piece, (size,) + piece.shape))[None]
+        self.masks, self.order = [0], list(bits) + [1]
+
+    def send(self, *earlier):
+        if earlier:
+            self.stack = after(self.stack, *earlier)
+        self.flying = bit_swap(self.stack, self.order[0])
+
+    def join(self, *earlier):
+        got = after(self.flying, *earlier) if earlier else self.flying
+        self.stack = jnp.concatenate([self.stack, got])
+        self.masks = self.masks + [mask ^ self.order[0] for mask in self.masks]
+        self.order = self.order[1:]
+        return self.stack
+
+    def middle(self):
+        while len(self.order) > 2:
+            self.send()
+            self.join()
+
+
+def assemble_kernel(plan, relative, per, where, *refs):
     count = len(plan)
     stacks, out, held, sems = refs[:count], refs[count], refs[count + 1], refs[count + 2]
-    i = where[0]
+    i, t = where[0], where[1]
+    size = out.shape[1 if per > 1 else 0]
     loads, stores = [], []
     for number, (first, masks) in enumerate(plan):
         slots = stacks[number].shape[1]
         for m, mask in enumerate(masks):
             for n in range(slots):
-                place = (first + n, i ^ mask)
+                slot = lax.rem(t + size - (first + n), size) if relative else first + n
+                owner = i ^ mask
+                place = (owner % per, slot, owner // per) if per > 1 else (slot, owner)
                 sem = sems.at[len(loads)]
                 loads.append(pltpu.make_async_copy(stacks[number].at[m, n], held.at[place], sem))
                 stores.append(pltpu.make_async_copy(held.at[place], out.at[place], sem))
@@ -194,15 +246,15 @@
         copy.wait()
 
 
-def assemble(found, dp_size, where):
+def assemble(found, dp_size, where, relative=False, per=1):
     plan = [(first, masks) for first, masks, _ in found]
     stacks = [stack for _, _, stack in found]
     r, c = stacks[0].shape[2:]
     slots = sum(stack.shape[1] * len(masks) for (_, masks), stack in zip(plan, stacks)) // dp_size
-    shape = (slots, dp_size, r, c)
+    shape = (per, slots, dp_size // per, r, c) if per > 1 else (slots, dp_size, r, c)
     amount = 2 * 2 * math.prod(shape)
     return pl.pallas_call(
-        partial(assemble_kernel, plan),
+        partial(assemble_kernel, plan, relative, per),
         out_shape=jax.ShapeDtypeStruct(shape, stacks[0].dtype),
         in_specs=[pl.BlockSpec(memory_space=pltpu.SMEM)]
         + [pl.BlockSpec(memory_space=pl.ANY)] * len(stacks),
@@ -212,7 +264,7 @@
             pltpu.SemaphoreType.DMA((slots * dp_size,)),
         ],
         compiler_params=pltpu.CompilerParams(vmem_limit_bytes=VMEM_LIMIT),
-        cost_estimate=pl.CostEstimate(flops=0, bytes_accessed=amount, transcendentals=0),
+        cost_estimate=cost(8.7),
         name="assemble",
     )(where, *stacks)
 
@@ -307,11 +359,7 @@
             jax.ShapeDtypeStruct((count, 1, rows), f32),
         ],
         compiler_params=pltpu.CompilerParams(vmem_limit_bytes=VMEM_LIMIT),
-        cost_estimate=pl.CostEstimate(
-            flops=count * 16 * size * rows * rows,
-            bytes_accessed=count * 12 * size * rows,
-            transcendentals=count * 2 * rows * rows,
-        ),
+        cost_estimate=cost(10.6),
         name="attend",
     )(*[projected] * 5)
 
@@ -362,11 +410,7 @@
         ),
         out_shape=jax.ShapeDtypeStruct((groups, 3, heads, size, columns), bf16),
         compiler_params=pltpu.CompilerParams(vmem_limit_bytes=VMEM_LIMIT),
-        cost_estimate=pl.CostEstimate(
-            flops=count * 40 * size * rows * rows,
-            bytes_accessed=count * 24 * size * rows,
-            transcendentals=count * 2 * rows * rows,
-        ),
+        cost_estimate=cost(16.6),
         name="attend_back",
     )(*[projected] * 5, grad, log)
 
@@ -421,12 +465,515 @@
         scratch_shapes=[pltpu.VMEM((r, c), f32)],
         input_output_aliases={5 + n: n for n in range(len(aliased))},
         compiler_params=pltpu.CompilerParams(vmem_limit_bytes=VMEM_LIMIT),
-        cost_estimate=pl.CostEstimate(flops=amount, bytes_accessed=amount, transcendentals=0),
+        cost_estimate=cost(6.0),
         name="step",
     )(grads, master, moment, stats, roots, *aliased)
 
 
-def local(tokens, conditioning, master, moment, stats, roots, cotangent):
+def call(kernel, name, grid, inputs, outputs, scratch=(), flops=0):
+    amount = sum(math.prod(x.shape) * x.dtype.itemsize for x, _, _ in inputs)
+    amount += sum(math.prod(shape) * jnp.dtype(kind).itemsize for shape, kind, _, _ in outputs)
+    in_specs = []
+    for x, block, index in inputs:
+        if block is None and x.dtype == jnp.int32:
+            in_specs.append(pl.BlockSpec(memory_space=pltpu.SMEM))
+        elif block is None:
+            in_specs.append(pl.BlockSpec(x.shape, lambda *_, rank=len(x.shape): (0,) * rank))
+        else:
+            in_specs.append(pl.BlockSpec(block, index))
+    return pl.pallas_call(
+        kernel,
+        grid=grid,
+        in_specs=in_specs,
+        out_specs=[pl.BlockSpec(block, index) for _, _, block, index in outputs],
+        out_shape=[jax.ShapeDtypeStruct(shape, kind) for shape, kind, _, _ in outputs],
+        scratch_shapes=list(scratch),
+        compiler_params=pltpu.CompilerParams(vmem_limit_bytes=VMEM_LIMIT),
+        cost_estimate=cost(TIMES[name]),
+        name=name,
+    )(*[x for x, _, _ in inputs])
+
+
+def split_rows(where, held, keep, send):
+    rows = held.shape[0] // 8
+    i = where[0]
+    chip, core = i // 2, lax.rem(i, 2)
+    for rel in range(4):
+        for part, out in ((core, keep), (1 - core, send)):
+            at = pl.multiple_of((2 * (chip ^ rel) + part) * rows, 16)
+            out(rel * rows, held[pl.ds(at, rows), :])
+
+
+def norm_parts(values):
+    center = values - jnp.mean(values, axis=-1, keepdims=True)
+    variance = jnp.mean(center * center, axis=-1, keepdims=True)
+    inverse = lax.rsqrt(variance + epsilon)
+    return center * inverse, inverse
+
+
+def first_kernel(where, tokens, others, mods, h_ref, keep_ref, send_ref, held):
+    rows = tokens.shape[0]
+    for part, source in enumerate((tokens, others)):
+        normed, _ = norm_parts(source[...].astype(f32))
+        h = normed * (1.0 + mods[1:2]) + mods[0:1]
+        h_ref[part] = h.astype(bf16)
+        held[...] = h.T.astype(bf16)
+
+        columns = pl.ds(part * rows, rows)
+
+        def keep(at, values, columns=columns):
+            keep_ref[pl.ds(at, values.shape[0]), columns] = values
+
+        def send(at, values, columns=columns):
+            send_ref[pl.ds(at, values.shape[0]), columns] = values
+
+        split_rows(where, held, keep, send)
+
+
+def first(where, tokens, others, mods):
+    rows, width = tokens.shape
+    half = (width // 2, 2 * rows)
+    return call(
+        first_kernel,
+        "first",
+        (1,),
+        [(where, None, None), (tokens, None, None), (others, None, None), (mods, None, None)],
+        [
+            ((2, rows, width), bf16, (2, rows, width), lambda n: (0, 0, 0)),
+            (half, bf16, half, lambda n: (0, 0)),
+            (half, bf16, half, lambda n: (0, 0)),
+        ],
+        [pltpu.VMEM((width, rows), bf16)],
+    )
+
+
+def middle_kernel(
+    where, one, two, w, tokens, mods, branch_ref, middle_ref, h_ref, keep_ref, send_ref, held
+):
+    count = one.shape[0] * one.shape[1]
+    columns = one.shape[2]
+    c = w.shape[2]
+    for n in range(w.shape[0]):
+        part = contract(one[...].reshape(count, columns), w[n, :count], (0, 0))
+        part = part + contract(two[...].reshape(count, columns), w[n, count:], (0, 0))
+        branch_ref[:, n * c : n * c + c] = part
+    values = tokens[...].astype(f32) + mods[2:3] * branch_ref[...]
+    middle_ref[...] = values
+    normed, _ = norm_parts(values)
+    h = normed * (1.0 + mods[4:5]) + mods[3:4]
+    h_ref[...] = h.astype(bf16)
+    held[...] = h.T.astype(bf16)
+
+    def keep(at, values):
+        keep_ref[pl.ds(at, values.shape[0]), :] = values
+
+    def send(at, values):
+        send_ref[pl.ds(at, values.shape[0]), :] = values
+
+    split_rows(where, held, keep, send)
+
+
+def middle_part(where, one, two, w, tokens, mods):
+    rows, width = tokens.shape
+    part = rows // 2
+    heads, tall, _ = one.shape
+    row = lambda n: (n, 0)
+    column = lambda n: (0, n)
+    return call(
+        middle_kernel,
+        "middle",
+        (2,),
+        [
+            (where, None, None),
+            (one, (heads, tall, part), lambda n: (0, 0, n)),
+            (two, (heads, tall, part), lambda n: (0, 0, n)),
+            (w, None, None),
+            (tokens, (part, width), row),
+            (mods, None, None),
+        ],
+        [
+            ((rows, width), f32, (part, width), row),
+            ((rows, width), f32, (part, width), row),
+            ((rows, width), bf16, (part, width), row),
+            ((width // 2, rows), bf16, (width // 2, part), column),
+            ((width // 2, rows), bf16, (width // 2, part), column),
+        ],
+        [pltpu.VMEM((width, part), bf16)],
+        flops=4 * rows * width * heads * tall,
+    )
+
+
+def up_kernel(where, h, w, u_ref, slope_ref, keep_ref, send_ref, held):
+    root = math.sqrt(2.0 / math.pi)
+    z = contract(h[...], w[0], (1, 0))
+    square = z * z
+    bent = jnp.tanh(root * z * (1.0 + 0.044715 * square))
+    side = 0.5 * (1.0 + bent)
+    u = z * side
+    slope = side + 0.5 * z * (1.0 - bent * bent) * (root * (1.0 + 3 * 0.044715 * square))
+    u_ref[0] = u.astype(bf16)
+    slope_ref[0] = slope.astype(bf16)
+    held[...] = u.T.astype(bf16)
+
+    def keep(at, values):
+        keep_ref[0, pl.ds(at, values.shape[0]), :] = values
+
+    def send(at, values):
+        send_ref[0, pl.ds(at, values.shape[0]), :] = values
+
+    split_rows(where, held, keep, send)
+
+
+def up_part(where, h, w):
+    rows, width = h.shape
+    slots, _, c = w.shape
+    block = lambda n: (n, 0, 0)
+    return call(
+        up_kernel,
+        "up",
+        (slots,),
+        [(where, None, None), (h, None, None), (w, (1, width, c), block)],
+        [
+            ((slots, rows, c), bf16, (1, rows, c), block),
+            ((slots, rows, c), bf16, (1, rows, c), block),
+            ((slots, c // 2, rows), bf16, (1, c // 2, rows), block),
+            ((slots, c // 2, rows), bf16, (1, c // 2, rows), block),
+        ],
+        [pltpu.VMEM((c, rows), bf16)],
+        flops=2 * rows * width * c * slots,
+    )
+
+
+def down_kernel(u, w, middle, grad, mods, out_ref, sums_ref, total):
+    n = pl.program_id(0)
+    part = contract(u[0], w[0], (1, 0))
+
+    @pl.when(n == 0)
+    def _():
+        total[...] = part
+
+    @pl.when(n > 0)
+    def _():
+        total[...] += part
+
+    @pl.when(n == pl.num_programs(0) - 1)
+    def _():
+        feed = total[...]
+        out_ref[...] = (middle[...] + mods[5:6] * feed).astype(bf16)
+        sums_ref[...] = jnp.broadcast_to(
+            jnp.sum(grad[...].astype(f32) * feed, axis=0, keepdims=True), sums_ref.shape
+        )
+
+
+def down_part(u, w, middle, grad, mods):
+    slots, rows, c = u.shape
+    width = w.shape[2]
+    block = lambda n: (n, 0, 0)
+    return call(
+        down_kernel,
+        "down",
+        (slots,),
+        [
+            (u, (1, rows, c), block),
+            (w, (1, c, width), block),
+            (middle, None, None),
+            (grad, None, None),
+            (mods, None, None),
+        ],
+        [
+            ((rows, width), bf16, (rows, width), lambda n: (0, 0)),
+            ((8, width), f32, (8, width), lambda n: (0, 0)),
+        ],
+        [pltpu.VMEM((rows, width), f32)],
+        flops=2 * rows * width * c * slots,
+    )
+
+
+def down_back_kernel(gm, w, slope, gz_ref):
+    gz_ref[0] = (contract(gm[...], w[0], (1, 1)) * slope[0].astype(f32)).astype(bf16)
+
+
+def down_back(gm, w, slope):
+    slots, rows, c = slope.shape
+    width = w.shape[2]
+    block = lambda n: (n, 0, 0)
+    return call(
+        down_back_kernel,
+        "down_back",
+        (slots,),
+        [(gm, None, None), (w, (1, c, width), block), (slope, (1, rows, c), block)],
+        [((slots, rows, c), bf16, (1, rows, c), block)],
+        flops=2 * rows * width * c * slots,
+    )[0]
+
+
+def up_back_kernel(gz, w, middle, grad, branch, mods, gx_ref, ga_ref, sums_ref, total):
+    n = pl.program_id(0)
+    part = contract(gz[0], w[0], (1, 1))
+
+    @pl.when(n == 0)
+    def _():
+        total[...] = part
+
+    @pl.when(n > 0)
+    def _():
+        total[...] += part
+
+    @pl.when(n == pl.num_programs(0) - 1)
+    def _():
+        gh = total[...]
+        normed, inverse = norm_parts(middle[...])
+        slope = gh * (1.0 + mods[4:5])
+        mean_grad = jnp.mean(slope, axis=-1, keepdims=True)
+        mean_inner = jnp.mean(slope * normed, axis=-1, keepdims=True)
+        gx = grad[...].astype(f32) + (slope - mean_grad - normed * mean_inner) * inverse
+        gx_ref[...] = gx
+        ga_ref[...] = (gx * mods[2:3]).astype(bf16)
+        sums_ref[0:1] = jnp.sum(gx * branch[...], axis=0, keepdims=True)
+        sums_ref[1:2] = jnp.sum(gh, axis=0, keepdims=True)
+        sums_ref[2:3] = jnp.sum(gh * normed, axis=0, keepdims=True)
+        sums_ref[3:8] = jnp.zeros((5, gh.shape[1]), f32)
+
+
+def up_back(gz, w, middle, grad, branch, mods):
+    slots, rows, c = gz.shape
+    width = w.shape[1]
+    block = lambda n: (n, 0, 0)
+    whole = lambda n: (0, 0)
+    return call(
+        up_back_kernel,
+        "up_back",
+        (slots,),
+        [
+            (gz, (1, rows, c), block),
+            (w, (1, width, c), block),
+            (middle, None, None),
+            (grad, None, None),
+            (branch, None, None),
+            (mods, None, None),
+        ],
+        [
+            ((rows, width), f32, (rows, width), whole),
+            ((rows, width), bf16, (rows, width), whole),
+            ((8, width), f32, (8, width), whole),
+        ],
+        [pltpu.VMEM((rows, width), f32)],
+        flops=2 * rows * width * c * slots,
+    )
+
+
+def out_back_kernel(where, one, two, w, ga, go_ref, keep_ref, away_ref, held):
+    heads, tall, rows = one.shape
+    count = heads * tall
+    c = w.shape[2]
+    i = where[0]
+    chip, core = i // 2, lax.rem(i, 2)
+    groups = keep_ref.shape[1]
+    for half, some in enumerate((one, two)):
+        flat = some[...].reshape(count, rows)
+        found = jnp.zeros((count, rows), f32)
+        for n in range(w.shape[0]):
+            some_ga = ga[:, n * c : n * c + c]
+            found = found + contract(w[n, half * count : half * count + count], some_ga, (1, 1))
+            grad = contract(flat, some_ga, (1, 0)).astype(bf16)
+            held[n, half * heads : half * heads + heads] = grad.reshape(heads, tall, c)
+        go_ref[half * heads : half * heads + heads] = found.astype(bf16).reshape(heads, tall, rows)
+    for slot in range(keep_ref.shape[0]):
+        for group in range(groups):
+            keep_ref[slot, group] = held[core, slot * groups + (chip ^ group)]
+            away_ref[slot, group] = held[1 - core, slot * groups + (chip ^ group)]
+
+
+def out_back(where, one, two, w, ga):
+    heads, tall, rows = one.shape
+    c = w.shape[2]
+    shape = (heads // 2, 4, tall, c)
+    zeros = lambda n: (0, 0, 0, 0)
+    return call(
+        out_back_kernel,
+        "out_back",
+        (1,),
+        [
+            (where, None, None),
+            (one, None, None),
+            (two, None, None),
+            (w, None, None),
+            (ga, None, None),
+        ],
+        [
+            ((2 * heads, tall, rows), bf16, (2 * heads, tall, rows), lambda n: (0, 0, 0)),
+            (shape, bf16, shape, zeros),
+            (shape, bf16, shape, zeros),
+        ],
+        [pltpu.VMEM((2, 2 * heads, tall, c), bf16)],
+    )
+
+
+def weight_kernel(kinds, turned, *refs):
+    left, left_far, right, right_far = refs[:4]
+    outs = {}
+    at = 4
+    for kind in sorted(set(kinds)):
+        outs[kind] = refs[at : at + 2]
+        at += 2
+    n = pl.program_id(0)
+
+    def read(ref):
+        return ref[0] if len(ref.shape) == 3 else ref[...]
+
+    dims = (1, 1) if turned else (1, 0)
+    found = contract(read(left), read(right), dims)
+    found = (found + contract(read(left_far), read(right_far), dims)).astype(bf16)
+    r = found.shape[0] // 4
+    for kind, (send, keep) in outs.items():
+
+        @pl.when((n >= kinds.index(kind)) & (n < kinds.index(kind) + kinds.count(kind)))
+        def _():
+            for m in range(2):
+                for near, out in ((1, send), (0, keep)):
+                    rel = (2 * near + m) if kind == 0 else (2 * m + near)
+                    out[0, m] = found[rel * r : rel * r + r]
+
+
+def weight_grads(left, left_far, right, right_far, kinds, turned=False):
+    slots = len(kinds)
+    r = left.shape[-2] // 4
+    c = right.shape[-2] if turned else right.shape[-1]
+
+    def spec(x):
+        if len(x.shape) == 2:
+            return (x, None, None)
+        return (x, (1,) + x.shape[1:], lambda n: (n, 0, 0))
+
+    outputs, order = [], sorted(set(kinds))
+    for kind in order:
+        low, count = kinds.index(kind), kinds.count(kind)
+        index = lambda n, low=low, count=count: (jnp.clip(n - low, 0, count - 1), 0, 0, 0)
+        outputs += [((count, 2, r, c), bf16, (1, 2, r, c), index)] * 2
+    found = call(
+        partial(weight_kernel, kinds, turned),
+        "weight_grads",
+        (slots,),
+        [spec(left), spec(left_far), spec(right), spec(right_far)],
+        outputs,
+        flops=4 * slots * 4 * r * c * left.shape[-1],
+    )
+    return {kind: found[2 * n : 2 * n + 2] for n, kind in enumerate(order)}
+
+
+def qkv_back_kernel(one, two, w, own_ref, other_ref, total):
+    n = pl.program_id(0)
+    half = pl.num_programs(0) // 2
+    rows = own_ref.shape[0]
+
+    @pl.when(n == 0)
+    def _():
+        total[...] = contract(w[0], one[0], (1, 0))
+
+    @pl.when((n > 0) & (n < half))
+    def _():
+        total[...] += contract(w[0], one[0], (1, 0))
+
+    @pl.when(n >= half)
+    def _():
+        total[...] += contract(w[0], two[0], (1, 0))
+
+    @pl.when(n == pl.num_programs(0) - 1)
+    def _():
+        own_ref[...] = total[:, :rows].T
+        other_ref[...] = total[:, rows:].T.astype(bf16)
+
+
+def qkv_back(one, two, w):
+    half, c, columns = one.shape
+    slots, width, _ = w.shape
+    rows = columns // 2
+    return call(
+        qkv_back_kernel,
+        "qkv_back",
+        (slots,),
+        [
+            (one, (1, c, columns), lambda n: (jnp.minimum(n, half - 1), 0, 0)),
+            (two, (1, c, columns), lambda n: (jnp.maximum(n - half, 0), 0, 0)),
+            (w, (1, width, c), lambda n: (n, 0, 0)),
+        ],
+        [
+            ((rows, width), f32, (rows, width), lambda n: (0, 0)),
+            ((rows, width), bf16, (rows, width), lambda n: (0, 0)),
+        ],
+        [pltpu.VMEM((width, columns), f32)],
+        flops=2 * slots * c * columns * width,
+    )
+
+
+def last_kernel(own, far, tokens, gx, mods, out_ref, sums_ref):
+    n = pl.program_id(0)
+    gh = own[...] + far[...].astype(f32)
+    normed, inverse = norm_parts(tokens[...].astype(f32))
+    slope = gh * (1.0 + mods[1:2])
+    mean_grad = jnp.mean(slope, axis=-1, keepdims=True)
+    mean_inner = jnp.mean(slope * normed, axis=-1, keepdims=True)
+    out_ref[...] = gx[...] + (slope - mean_grad - normed * mean_inner) * inverse
+
+    @pl.when(n == 0)
+    def _():
+        sums_ref[...] = jnp.zeros(sums_ref.shape, f32)
+
+    sums_ref[0:1] += jnp.sum(gh, axis=0, keepdims=True)
+    sums_ref[1:2] += jnp.sum(gh * normed, axis=0, keepdims=True)
+
+
+def last_part(own, far, tokens, gx, mods):
+    rows, width = tokens.shape
+    part = rows // 4
+    row = lambda n: (n, 0)
+    return call(
+        last_kernel,
+        "last",
+        (4,),
+        [
+            (own, (part, width), row),
+            (far, (part, width), row),
+            (tokens, (part, width), row),
+            (gx, (part, width), row),
+            (mods, None, None),
+        ],
+        [
+            ((rows, width), f32, (part, width), row),
+            ((8, width), f32, (8, width), lambda n: (0, 0)),
+        ],
+    )
+
+
+def land(halves, *earlier):
+    landed = lax.optimization_barrier((*[half.flying for half in halves], *earlier))
+    for half, got in zip(halves, landed):
+        half.flying = got
+    return [half.add() for half in halves]
+
+
+class Relative:
+    def __init__(self, parts, kind, bits):
+        self.order = bits[::-1] if kind == 0 else list(bits)
+        send, self.keep = parts
+        self.send_part = send
+
+    def send(self, *earlier):
+        part = after(self.send_part, *earlier) if earlier else self.send_part
+        self.flying = bit_swap(part, self.order[0])
+        return self
+
+    def add(self, *earlier):
+        got = after(self.flying, *earlier) if earlier else self.flying
+        self.order = self.order[1:]
+        if self.order:
+            self.send_part, self.keep = add(self.keep[:, 1], got[:, 1]), add(self.keep[:, 0], got[:, 0])
+            return self.send_part
+        self.keep = add(self.keep, got)
+        return self.keep
+
+
+def local_any(tokens, conditioning, master, moment, stats, roots, cotangent):
     dp_size = lax.axis_size("dp")
     tensor_size = lax.axis_size("tensor")
     i, t = lax.axis_index("dp"), lax.axis_index("tensor")
@@ -453,7 +1000,7 @@
     tall = HEAD_DIM + -HEAD_DIM % 16
     per = width // c_out
     pieces_out = jnp.pad(pieces[1], ((0, tall - ro), (0, 0)))
-    one = Gathering(pieces[0], bits)
+    one = Gathering(pieces[0], bits, relative=True)
 
     silu_low = jax.nn.silu(conditioning).astype(bf16)
     ada_cols = 6 * width // tensor_size
@@ -472,34 +1019,44 @@
     mods = exchange(jnp.repeat(own_mods, span, axis=0), "tensor").reshape(6, 1, width)
     shift1, scale1, gate1, shift2, scale2, gate2 = (mods[k] for k in range(6))
 
-    one.start().join()
-    others = pair_swap(after(tokens, one.slots))
-    three = Gathering(pieces[2], bits, one.slots)
+    two = WholeGathering(pieces_out, bits, *one.slots[1:])
+    one.start()
+    others = pair_swap(after(tokens, two.stack))
+    three = Gathering(pieces[2], bits, two.stack)
+    one.join(mods)
     one.last_send()
-    two = Gathering(pieces_out, bits, three.slots)
     one.cross()
-    three.start(*one.flying)
-    two.start().join()
-    four = Gathering(pieces[3], bits, two.slots)
-    two.last_send().cross()
+    two.send(*one.flying)
 
     inputs = tokens.astype(f32)
     normed_one = layer_norm(inputs)
     h1 = (normed_one * (1.0 + scale1) + shift1).astype(bf16)
     h1_other = (layer_norm(others.astype(f32)) * (1.0 + scale1) + shift1).astype(bf16)
     h1_all = jnp.concatenate([h1, h1_other])
-    w_qkv = whole_from_runs(one.assemble(dp_size, where), width, 3 * head_cols)
-    projected = jnp.einsum("tdc,rd->tcr", w_qkv, h1_all, preferred_element_type=f32).astype(bf16)
+    two.join(h1_all)
+    two.middle()
+    two.send()
+    w_qkv = whole_from_runs(one.assemble(dp_size, where, two.stack), width, 3 * head_cols)
+    three.start()
+    four = Gathering(pieces[3], bits, three.slots)
+    h1_now = after(h1_all, *three.stacks)
+    projected = jnp.einsum("tdc,rd->tcr", w_qkv, h1_now, preferred_element_type=f32).astype(bf16)
     projected = projected.reshape(tensor_size, 3 * heads, HEAD_DIM, 2 * rows)
-    projected = after(projected, *three.join())
+    three.join(projected)
     three.last_send()
+    two.join(projected)
+    two.send()
+    projected = after(projected, *three.stacks, two.stack)
     cut = tensor_size // 2
     first, first_log = attend(projected, heads, 0, cut)
-    three.cross(first)
-    four.start(*three.flying)
-    second, second_log = attend(after(projected, *three.flying), heads, cut, cut)
+    two.join(first)
+    second, second_log = attend(
+        after(projected, first, two.stack, *three.crossed), heads, cut, cut
+    )
     attended = jnp.concatenate([first, second]).reshape(HEADS * tall, rows)
-    out_runs = two.assemble(dp_size, where, second).reshape(tensor_size, heads, per, tall, c_out)
+    out_parts = [(0, two.masks, after(two.stack, second, four.slots))]
+    out_runs = assemble(out_parts, dp_size, where, relative=True)
+    out_runs = out_runs.reshape(tensor_size, heads, per, tall, c_out)
     out_runs = jnp.moveaxis(out_runs, 2, 0).reshape(per, HEADS * tall, c_out)
     branch = jnp.concatenate(
         [
@@ -511,7 +1068,9 @@
     middle = inputs + gate1 * branch
     normed_two = layer_norm(middle)
     h2 = (normed_two * (1.0 + scale2) + shift2).astype(bf16)
-    w_up = whole_from_runs(three.assemble(dp_size, where, h2), width, FF // tensor_size)
+    three.cross(h2)
+    four.start(*three.flying)
+    w_up = whole_from_runs(three.assemble(dp_size, where, *four.stacks), width, FF // tensor_size)
     four.join(w_up)
     four.last_send()
     h2_now = after(h2, *four.stacks)
@@ -566,11 +1125,13 @@
         gm_all = both_cores(gm, 0, None, hidden)
     else:
         hidden_all, gm_all = hidden, gm
-    grad_down = row_grads("trc,rd->tcd", hidden_all, gm_all, 3)
+    four.cross(hidden_all)
+    grad_down = row_grads("trc,rd->tcd", after(hidden_all, *four.flying, *four.crossed), gm_all, 3)
     red_down = halves(grad_down)
-    four.cross(grad_down)
-    send_all(*red_down, earlier=four.flying)
-    w_down = whole_from_runs(four.assemble(dp_size, where), FF // tensor_size, width)
+    send_all(*red_down)
+    w_down = whole_from_runs(
+        four.assemble(dp_size, where, grad_down), FF // tensor_size, width
+    )
     gm_later = after(gm, grad_down)
     grad_hidden = jnp.einsum("rd,tcd->trc", gm_later, w_down, preferred_element_type=f32)
     _, gelu_pullback = jax.vjp(partial(jax.nn.gelu, approximate=True), pre_gelu)
@@ -604,45 +1165,48 @@
     else:
         away = out_grad(ga)
         grad_wo = core_reduced(away.reshape(tensor_size, heads * tall, width), (tall, c_out))
-    grad_up = row_grads("rd,trc->tdc", h2_all, after(gz_all, away, go), 2)
+    red_out = Reduction(grad_wo, bits, bits[::-1], i).send()
+    grad_up = row_grads("rd,trc->tdc", h2_all, after(gz_all, grad_wo, go), 2)
     down_one = [half.last_add(grad_up) for half in red_down]
     down_spread = exchange_t(jnp.concatenate(down_one))
-    red_up, red_out = halves(grad_up), halves(grad_wo)
-    send_all(*red_up, *red_out, earlier=down_one)
-    first = attend_back(after(projected, *down_one), go, first_log, heads, 0, cut)
+    red_up = halves(grad_up)
+    send_all(*red_up, earlier=down_one)
+    out_two = red_out.add(*down_one)
+    send_all(red_out)
+    first = attend_back(after(projected, out_two), go, first_log, heads, 0, cut)
     first = first.reshape(cut, 3 * head_cols, 2 * rows)
-    out_two = [half.add(first) for half in red_out]
-    send_all(*red_out)
+    out_one = red_out.last_add(first)
     first_all = both_cores(first, 2) if fast else first
-    second = attend_back(after(projected, *out_two), go, second_log, heads, cut, cut)
+    second = attend_back(after(projected, out_one), go, second_log, heads, cut, cut)
     second = second.reshape(cut, 3 * head_cols, 2 * rows)
+    up_two = [half.add(second) for half in red_up]
+    send_all(*red_up)
+    second_all = both_cores(second, 2, None, first_all, *up_two) if fast else second
     state = (master, moment, stats, roots)
-    done = step(after(down_spread, second), spans[3], state, None)
-    up_two = [half.add(*done) for half in red_up]
-    send_all(*red_up)
-    out_one = [half.last_add(*up_two) for half in red_out]
-    out_spread = exchange_t(after(jnp.concatenate(out_one)[:, :ro], *up_two))
-    second_all = both_cores(second, 2) if fast else second
+    done = step(after(down_spread, *up_two), spans[3], state, None)
+    out_one = after(out_one[:, :ro], down_spread)
+    out_slots = [take(out_one, (t + tensor_size - k) % tensor_size, 0) for k in range(tensor_size)]
+    out_spread = exchange_t(jnp.stack(out_slots))
     h1_both = both_cores(h1_all, 0, 1, second) if fast else h1_all
-    grad_first = row_grads("rd,tcr->tdc", h1_both, after(first_all, *out_one), 0)
+    grad_first = row_grads("rd,tcr->tdc", h1_both, after(first_all, *done), 0)
+    up_one = [half.last_add(grad_first) for half in red_up]
+    red_first = Reduction(grad_first, bits, bits[::-1], i)
+    red_first.send(*up_one)
+    up_spread = exchange_t(after(jnp.concatenate(up_one), out_spread))
     gh1_other = jnp.einsum(
         "tcr,tdc->rd",
-        after(jnp.concatenate([first, second]), grad_first)[:, head_cols:, rows:],
+        after(jnp.concatenate([first, second]), *up_one, out_spread)[:, head_cols:, rows:],
         w_qkv[:, :, head_cols:],
         preferred_element_type=f32,
     ).astype(bf16)
-    done = step(after(out_spread, gh1_other), spans[1], state, done)
-    up_one = [half.last_add(gh1_other) for half in red_up]
-    gh1_far = pair_swap(after(gh1_other, *up_one))
-    red_first = Reduction(grad_first, bits, bits[::-1], i)
-    red_first.send(*up_one)
-    grad_second = row_grads("rd,tcr->tdc", h1_both, after(second_all, *up_one), 0)
+    gh1_far = pair_swap(gh1_other)
+    grad_second = row_grads("rd,tcr->tdc", h1_both, after(second_all, gh1_other), 0)
     red_second = Reduction(grad_second, bits, bits, i)
     red_second.send()
-    up_spread = exchange_t(after(jnp.concatenate(up_one), grad_second))
+    done = step(after(out_spread, grad_second), spans[1], state, done)
     gh1 = jnp.einsum(
         "tcr,tdc->rd",
-        after(jnp.concatenate([first, second])[:, :, :rows], grad_second),
+        after(jnp.concatenate([first, second])[:, :, :rows], *done),
         w_qkv,
         preferred_element_type=f32,
     )
@@ -669,7 +1233,10 @@
     grad_mods = exchange_t(grad_mods)
     done = step(after(up_spread, grad_mods), spans[2], state, done)
     qkv_one = [red_first.last_add(*done), red_second.last_add(*done)]
-    qkv_spread = exchange_t(jnp.concatenate(qkv_one))
+    qkv_slots = [half[n] for half in qkv_one for n in range(cut)]
+    qkv_spread = [qkv_slots[0]] + [
+        shift_t(qkv_slots[k], tensor_size - k) for k in range(1, tensor_size)
+    ]
     grad_mods = jnp.sum(grad_mods.reshape(sequences, span, ada_cols), axis=1)
     grad_mods = after(grad_mods, *qkv_one)
     if ada_per > 1:
@@ -688,7 +1255,181 @@
     grad_silu = jnp.sum(grad_silu, axis=0)
     _, silu_pullback = jax.vjp(jax.nn.silu, conditioning)
     grad_conditioning = silu_pullback(grad_silu)[0]
-    done = step(after(qkv_spread, *done), spans[0], state, done)
+    done = step(after(jnp.stack(qkv_spread), *done), spans[0], state, done)
+    return (result, grad_tokens, grad_conditioning, *done)
+
+
+def local(tokens, conditioning, master, moment, stats, roots, cotangent):
+    dp_size = lax.axis_size("dp")
+    tensor_size = lax.axis_size("tensor")
+    rows, width = tokens.shape
+    size = master.shape[1]
+    shapes = grid_shapes(width, size, tensor_size)
+    counts = [row_blocks * col_blocks // dp_size for row_blocks, col_blocks in shapes]
+    if dp_size != 8 or any(counts[n] % shapes[n][1] for n in (0, 2, 3, 4)):
+        return local_any(tokens, conditioning, master, moment, stats, roots, cotangent)
+    i, t = lax.axis_index("dp"), lax.axis_index("tensor")
+    where = jnp.stack([i, t]).astype(jnp.int32)
+    sequences = conditioning.shape[0]
+    latents = sequences * dp_size
+    heads = HEADS // tensor_size
+    bits = [2, 4]
+    low = master.astype(bf16)
+    pieces, spans, offset = [], [], 0
+    for count, (_, col_blocks) in zip(counts, shapes):
+        pieces.append(to_dense(low[offset : offset + count], col_blocks))
+        spans.append((offset, offset + count))
+        offset += count
+    w_ada = pieces[4]
+    head_cols = heads * HEAD_DIM
+    ro, c_out = pieces[1].shape
+    tall = HEAD_DIM + -HEAD_DIM % 16
+    per = width // c_out
+    pieces_out = jnp.pad(pieces[1], ((0, tall - ro), (0, 0)))
+    one = Gathering(pieces[0], bits, relative=True)
+
+    silu_low = jax.nn.silu(conditioning).astype(bf16)
+    ada_r, ada_c = w_ada.shape
+    silu_for = jnp.moveaxis(silu_low.reshape(sequences, dp_size, ada_r), 1, 0)
+    silu_mine = exchange(silu_for, "dp").reshape(latents, ada_r)
+    share = jnp.dot(silu_mine, w_ada, preferred_element_type=f32)
+    span = LEN // rows
+    everyone = ("dp", "tensor")
+    shares = exchange(jnp.repeat(share, span, axis=0), everyone)
+    mods = jnp.sum(shares.reshape(dp_size, tensor_size, ada_c), axis=0).reshape(6, width)
+    one.start()
+
+    others = pair_swap(after(tokens, *one.slots[1:]))
+    three = Gathering(pieces[2], bits, mods, *one.stacks)
+    one.join()
+    one.last_send()
+    one.cross(mods)
+    h1, h1_keep, h1_send = first(where, tokens, after(others, *one.flying), mods)
+    two = WholeGathering(pieces_out, bits, three.slots)
+    three.start(h1)
+    w_qkv = whole_from_runs(
+        one.assemble(dp_size, where, *three.stacks), width, 3 * head_cols
+    )
+    two.send(w_qkv)
+    four = Gathering(pieces[3], bits, two.stack)
+    h1_now = after(h1, two.stack).reshape(2 * rows, width)
+    projected = jnp.einsum("tdc,rd->tcr", w_qkv, h1_now, preferred_element_type=f32).astype(bf16)
+    projected = projected.reshape(tensor_size, 3 * heads, HEAD_DIM, 2 * rows)
+    three.join(projected)
+    three.last_send()
+    two.join(projected)
+    two.middle()
+    two.send()
+    projected = after(projected, *three.stacks, two.stack)
+    cut = tensor_size // 2
+    att_one, log_one = attend(projected, heads, 0, cut)
+    two.join(att_one)
+    two.send()
+    att_two, log_two = attend(
+        after(projected, att_one, two.stack, *three.crossed), heads, cut, cut
+    )
+    two.join(att_two)
+    out_parts = [(0, two.masks, after(two.stack, four.slots))]
+    w_out = assemble(out_parts, dp_size, where, relative=True, per=per)
+    w_out = w_out.reshape(per, HEADS * tall, c_out)
+    branch, middle, h2, h2_keep, h2_send = middle_part(
+        where, att_one, att_two, w_out, tokens, mods
+    )
+    three.cross(h2)
+    four.start(*three.flying)
+    w_up = whole_from_runs(three.assemble(dp_size, where, *four.stacks), width, FF // tensor_size)
+    four.join(w_up)
+    four.last_send()
+    hidden, slope, u_keep, u_send = up_part(where, after(h2, *four.stacks), w_up)
+
+    gm = (cotangent.astype(f32) * mods[5]).astype(bf16)
+    gm_far = bit_swap(after(gm, w_up), 1)
+    four.cross(hidden)
+    u_far = bit_swap(after(u_send, *four.flying), 1)
+    grads = weight_grads(
+        after(u_keep, *four.flying, *four.crossed), u_far, gm, gm_far, (0,) * cut + (1,) * cut
+    )
+    red_down = [Relative(grads[kind], kind, bits).send() for kind in range(2)]
+    keeps = [half.keep for half in red_down]
+    w_down = whole_from_runs(
+        four.assemble(dp_size, where, *keeps), FF // tensor_size, width
+    )
+    gz = down_back(gm, w_down, slope)
+    gx, ga, sums_two = up_back(gz, w_up, middle, cotangent, branch, mods)
+    down_two = land(red_down, ga)
+    for half in red_down:
+        half.send()
+    h2_far = bit_swap(after(h2_send, *down_two), 1)
+    gz_far = bit_swap(after(gz, *down_two), 1)
+    go, wo_keep, wo_away = out_back(where, att_one, att_two, w_out, after(ga, *down_two))
+    wo_got = bit_swap(wo_away, 1)
+    grads = weight_grads(
+        h2_keep, h2_far, after(gz, go), gz_far, (0,) * cut + (1,) * cut
+    )
+    red_up = [Relative(grads[kind], kind, bits) for kind in range(2)]
+    keeps = [half.keep for half in red_up]
+    down_one = land(red_down, *keeps)
+    down_spread = exchange_t(jnp.concatenate(down_one))
+    for half in red_up:
+        half.send(*down_one)
+    wo_got = after(wo_got, *keeps)
+    red_out = Relative((add(wo_keep[:, 2:], wo_got[:, 2:]), add(wo_keep[:, :2], wo_got[:, :2])), 0, bits)
+    g_one = attend_back(after(projected, red_out.keep, *down_one), go, log_one, heads, 0, cut)
+    g_one = g_one.reshape(cut, 3 * head_cols, 2 * rows)
+    g_two = attend_back(after(projected, g_one), go, log_two, heads, cut, cut)
+    g_two = g_two.reshape(cut, 3 * head_cols, 2 * rows)
+    up_two = land(red_up, g_two, down_spread)
+    for half in red_up:
+        half.send()
+    g_one_far = bit_swap(after(g_one, *up_two), 1)
+    h1_far = bit_swap(after(h1_send, *up_two), 1)
+    g_two_far = bit_swap(after(g_two, *up_two), 1)
+    gh_own, gh_other = qkv_back(after(g_one, *up_two), g_two, w_qkv)
+    up_one = land(red_up, gh_own)
+    gh_far = pair_swap(after(gh_other, *up_one))
+    up_spread = exchange_t(jnp.concatenate(up_one))
+    grads = weight_grads(h1_keep, h1_far, after(g_one, *up_one), g_one_far, (0,) * cut, True)
+    red_one = Relative(grads[0], 0, bits).send()
+    red_out.send(red_one.keep)
+    grads = weight_grads(
+        h1_keep, h1_far, after(g_two, red_one.keep), g_two_far, (1,) * cut, True
+    )
+    red_two = Relative(grads[1], 1, bits).send()
+    state = (master, moment, stats, roots)
+    done = step(after(down_spread, red_two.keep), spans[3], state, None)
+    result, sums_three = down_part(after(hidden, *done), w_down, middle, cotangent, mods)
+    grad_tokens, sums_one = last_part(after(gh_own, result, up_spread), gh_far, tokens, gx, mods)
+    one_two, two_two, out_two = land([red_one, red_two, red_out], grad_tokens)
+    red_one.send()
+    red_two.send()
+    red_out.send()
+
+    grad_mods = jnp.concatenate([sums_one[:2], sums_two[:3], sums_three[:1]])
+    grad_mods = after(grad_mods.reshape(tensor_size, ada_c), one_two, two_two)
+    grad_mods = jnp.broadcast_to(grad_mods, (dp_size,) + grad_mods.shape)
+    grad_mods = exchange(grad_mods.reshape(-1, ada_c), everyone)
+    grad_mods = jnp.sum(grad_mods.reshape(latents, span, ada_c), axis=1)
+    grad_ada = jnp.einsum("sr,sc->rc", silu_mine.astype(f32), grad_mods, precision=HIGHEST)
+    grad_silu = jnp.einsum("sc,rc->sr", grad_mods, w_ada.astype(f32), precision=HIGHEST)
+    *qkv_one, out_one = land([red_one, red_two, red_out], grad_ada, grad_silu)
+    qkv_slots = [half[n] for half in qkv_one for n in range(cut)]
+    qkv_spread = [qkv_slots[0]] + [
+        shift_t(qkv_slots[k], tensor_size - k) for k in range(1, tensor_size)
+    ]
+    grad_silu = after(grad_silu, *qkv_one).reshape(dp_size, 1, sequences, ada_r)
+    grad_silu = jnp.broadcast_to(grad_silu, (dp_size, tensor_size, sequences, ada_r))
+    grad_silu = exchange(grad_silu.reshape(-1, sequences, ada_r), everyone)
+    done = step(after(up_spread, *qkv_one), spans[2], state, done)
+    done = step(after(grad_ada[None], *done), spans[4], state, done)
+    grad_silu = jnp.sum(grad_silu.reshape(dp_size, tensor_size, sequences, ada_r), axis=1)
+    grad_silu = jnp.moveaxis(grad_silu, 0, 1).reshape(sequences, width)
+    _, silu_pullback = jax.vjp(jax.nn.silu, conditioning)
+    grad_conditioning = silu_pullback(grad_silu)[0]
+    out_one = out_one[:, :ro]
+    out_slots = [take(out_one, (t + tensor_size - k) % tensor_size, 0) for k in range(tensor_size)]
+    out_spread = exchange_t(after(jnp.stack(out_slots), grad_silu))
+    done = step(after(out_spread, *done), spans[1], state, done)
+    done = step(after(jnp.stack(qkv_spread), *done), spans[0], state, done)
     return (result, grad_tokens, grad_conditioning, *done)
 
 

time: 692 us -> 582 us (0.84)
  Pallas kernels: 110 us -> 251 us
  matrix products: 133 us -> 18.4 us
  other arithmetic: 102 us -> 41.5 us
  local copies, waits for them, and re-layouts: 92 us -> 51.4 us
  waiting for transfers between devices: 136 us -> 109 us
  starting transfers between devices: 107 us -> 98.6 us
    pallas_call x4 -> x17, Pallas kernels: 29 us -> 170 us  [the longest x13 141 us: call(): pl.pallas_call(kernel, grid=grid, in_specs=in_specs, out_specs=[pl.BlockS...]
    dot_general x17 -> x1, matrix products: 128 us -> 16.2 us  [local(): jnp.einsum('tdc,rd->tcr', w_qkv, h1_now, preferred_element_type=f32)]
    all_to_all x15 -> x10, waiting for transfers between devices: 70 us -> 13.3 us  [exchange(): return lax.all_to_all(values, axis, split_axis=0, concat_axis=0, tiled=True)]
    concatenate x10 -> x3, other arithmetic: 34.7 us -> 3.21 us  [the longest x1 2 us: join(): self.stack = jnp.concatenate([self.stack, got])]
    dynamic_slice x19 -> x1, local copies, waits for them, and re-layouts: 22.8 us -> 0.05 us  [take(): return lax.dynamic_index_in_dim(values, index, axis, keepdims=False)]
    all_to_all x15 -> x10, starting transfers between devices: 65.2 us -> 47.1 us  [exchange(): return lax.all_to_all(values, axis, split_axis=0, concat_axis=0, tiled=True)]
    ppermute x56 -> x49, waiting for transfers between devices: 60.1 us -> 72.8 us  [bit_swap(): return lax.ppermute(values, 'dp', [(k, k ^ bit) for k in range(size)])]
    ppermute x0 -> x6, starting transfers between devices: none -> 11.7 us  [shift_t(): lax.ppermute(values, 'tensor', [(n, (n + k) % size) for n in range(size)])]
  transfers between devices with their start and end apart: 73 -> 67, of which waited for: 21 -> 22; matrix products, arithmetic and copies ran while one was open for 41% -> 13% of each run, Pallas kernels for 15% -> 43%
where the time goes in v3:
time: 582 us; the launch traced here: 572 us
  Pallas kernels  251 us (43%)
  waiting for transfers between devices  109 us (19%)
  starting transfers between devices  98.6 us (17%)
  local copies, waits for them, and re-layouts  51.4 us (9%)
  other arithmetic  41.5 us (7%)
  matrix products  18.4 us (3%)
    pallas_call x13, Pallas kernels, call(): pl.pallas_call(kernel, grid=grid, in_specs=in_specs, out_specs=[pl.BlockS...  141 us
    ppermute x49, waiting for transfers between devices, bit_swap(): return lax.ppermute(values, 'dp', [(k, k ^ bit) for k in range(size)])  72.8 us
    all_to_all x10, starting transfers between devices, exchange(): return lax.all_to_all(values, axis, split_axis=0, concat_axis=0, tiled=True)  47.1 us
    ppermute x49, starting transfers between devices, bit_swap(): return lax.ppermute(values, 'dp', [(k, k ^ bit) for k in range(size)])  36.8 us
    pallas_call x2, Pallas kernels, attend_back(): pl.pallas_call(attend_back_kernel, grid=(count,), in_specs=head_specs(hea...  33.2 us
    pallas_call x4, Pallas kernels, assemble(): pl.pallas_call(partial(assemble_kernel, plan, relative, per), out_shape=j...  28.9 us
    pallas_call x5, Pallas kernels, step(): pl.pallas_call(partial(step_kernel, size, len(aliased)), grid=(steps,), i...  26.8 us
    pallas_call x2, Pallas kernels, attend(): pl.pallas_call(attend_kernel, grid=(count,), in_specs=head_specs(heads, s...  21.6 us
  transfers between devices with their start and end apart: 67, of which 22 were waited for; matrix products, arithmetic and copies ran while one was open for 13% of the time, Pallas kernels for 43%

profile of v3, /device:TPU:0, one launch (start us, length us, event | category | flops | bytes accessed | tf_op | source)
XLA Modules:
  0.0 571.7 jit_solution(13078437568246387007)
XLA Ops:
  8.6 3.7 all-to-all-start
  21.8 5.0 all-to-all-start.1
  30.3 5.9 %collective-permute-done.2 = bf16[144,864]{1,0:T(8,128)(2,1)} collective-permute-done((bf16[144,864]{1,0:T(8,128)(2,1)}, bf16[144,864]{1,0:T(8,128)(2,1)}, u32[]{:S(2)}, u32[]{:S(2)}) %collective-permute-start.2) | collective-permute-done | bytes 248864 | tf_op jit(solution)/shard_map/ppermute | solution.py:120
  46.0 4.3 all-to-all-start.2
  60.1 17.0 %collective-permute-done.6.refs_1_ = bf16[2,2,144,864]{3,2,1,0:T(8,128)(2,1)} collective-permute-done((bf16[2,2,144,864]{3,2,1,0:T(8,128)(2,1)}, bf16[2,2,144,864]{3,2,1,0:T(8,128)(2,1)}, u32[]{:S(2)}, u32[]{:S(2)}) %collective-permute-start.6) | collective-permute-done | bytes 995360 | tf_op jit(solution)/shard_map/ppermute | solution.py:101
  81.7 16.8 %collective-permute-done.5.others = bf16[512,1152]{1,0:T(8,128)(2,1)} collective-permute-done((bf16[512,1152]{1,0:T(8,128)(2,1)}, bf16[512,1152]{1,0:T(8,128)(2,1)}, u32[]{:S(2)}, u32[]{:S(2)}) %collective-permute-start.5) | collective-permute-done | bytes 1179680 | tf_op jit(solution)/shard_map/ppermute | solution.py:111
  98.5 5.8 %first.1 = (bf16[2,512,1152]{2,1,0:T(8,128)(2,1)}, bf16[576,1024]{1,0:T(8,128)(2,1)}, bf16[576,1024]{1,0:T(8,128)(2,1)}) custom-call(s32[2]{0:T(128)} %pad_add_fusion.where, bf16[512,1152]{1,0:T(8,128)(2,1)} %tokens.5, bf16[512,1152]{1,0:T(8,128)(2,1)} %collective-permute-done.5.others, f32[6,1152]{1,0:T(8,128)} %reshape.181.mods), custom_call_target="tpu_custom_call" | custom-call | flops 6900000 | bytes 1024 | tf_op jit(solution)/shard_map/first/pallas_call | solution.py:484
  105.1 4.2 all-to-all-start.3
  115.6 7.5 %assemble.4 = bf16[4,8,144,864]{3,2,1,0:T(8,128)(2,1)} custom-call(s32[2]{0:T(128)} %pad_add_fusion.where, bf16[2,2,144,864]{3,2,1,0:T(8,128)(2,1)} %pad_maximum_fusion.3.refs_0_, bf16[2,2,144,864]{3,2,1,0:T(8,128)(2,1)} %collective-permute-done.6.refs_1_, bf16[2,2,144,864]{3,2,1,0:T(8,128)(2,1)} %collective-permute-done.8.refs_2_, ...), custom_call_target="tpu_custom_call" | custom-call | flops 10005000 | bytes 1024 | tf_op jit(solution)/shard_map/assemble/pallas_call | solution.py:256
  123.6 16.2 %convolution_convert_fusion = bf16[4,864,1024]{2,1,0:T(8,128)(2,1)} fusion(bf16[4,1152,864]{2,1,0:T(8,128)(2,1)} %bitcast.148, bf16[1024,1152,1]{1,0,2:T(8,128)(2,1)} %bitcast.173), kind=kOutput, calls=%fused_computation | convolution fusion | flops 8157265920 | bytes 17399808 | tf_op jit(solution)/shard_map/tdc,rd->tcr/dot_general | solution.py:1316
  145.5 5.3 all-to-all-start.4
  154.8 10.6 %attend.2 = (bf16[8,80,512]{2,1,0:T(8,128)(2,1)}, f32[8,1,512]{2,1,0:T(1,128)}) custom-call(bf16[4,12,72,1024]{3,2,1,0:T(8,128)(2,1)} %bitcast.124, bf16[4,12,72,1024]{3,2,1,0:T(8,128)(2,1)} %bitcast.125, bf16[4,12,72,1024]{3,2,1,0:T(8,128)(2,1)} %bitcast.126, bf16[4,12,72,1024]{3,2,1,0:T(8,128)(2,1)} %bitcast.127, bf16[4,12,72,1024]{3,2,1,0:T(8,128)(2,1)} %bitcast.128), custom_call_target="tpu_custom_call" | custom-call | flops 12190000 | bytes 1024 | tf_op jit(solution)/shard_map/attend/pallas_call | solution.py:349
  168.9 3.1 collective-permute-done.16.refs_2_
  173.9 11.0 %attend.3 = (bf16[8,80,512]{2,1,0:T(8,128)(2,1)}, f32[8,1,512]{2,1,0:T(1,128)}) custom-call(bf16[4,12,72,1024]{3,2,1,0:T(8,128)(2,1)} %bitcast.129, bf16[4,12,72,1024]{3,2,1,0:T(8,128)(2,1)} %bitcast.130, bf16[4,12,72,1024]{3,2,1,0:T(8,128)(2,1)} %bitcast.131, bf16[4,12,72,1024]{3,2,1,0:T(8,128)(2,1)} %bitcast.132, bf16[4,12,72,1024]{3,2,1,0:T(8,128)(2,1)} %bitcast.133), custom_call_target="tpu_custom_call" | custom-call | flops 12190000 | bytes 1024 | tf_op jit(solution)/shard_map/attend/pallas_call | solution.py:349
  186.9 4.0 assemble.5
  191.0 7.9 %middle.1 = (f32[512,1152]{1,0:T(8,128)}, f32[512,1152]{1,0:T(8,128)}, bf16[512,1152]{1,0:T(8,128)(2,1)}, bf16[576,512]{1,0:T(8,128)(2,1)}, bf16[576,512]{1,0:T(8,128)(2,1)}) custom-call(s32[2]{0:T(128)} %pad_add_fusion.where, bf16[8,80,512]{2,1,0:T(8,128)(2,1)} %get-tuple-element.155.one, bf16[8,80,512]{2,1,0:T(8,128)(2,1)} %get-tuple-element.158.two, ...), custom_call_target="tpu_custom_call" | custom-call | flops 9200000 | bytes 1024 | tf_op jit(solution)/shard_map/middle/pallas_call | solution.py:484
  204.3 8.7 %assemble.6 = bf16[4,8,144,1152]{3,2,1,0:T(8,128)(2,1)} custom-call(s32[2]{0:T(128)} %pad_add_fusion.where, bf16[2,2,144,1152]{3,2,1,0:T(8,128)(2,1)} %constant_dynamic-update-slice_fusion.refs_0_, bf16[2,2,144,1152]{3,2,1,0:T(8,128)(2,1)} %collective-permute-done.19.refs_1_, bf16[2,2,144,1152]{3,2,1,0:T(8,128)(2,1)} %copy-done.31, ...), custom_call_target="tpu_custom_call" | custom-call | flops 10005000 | bytes 1024 | tf_op jit(solution)/shard_map/assemble/pallas_call | solution.py:256
  213.0 3.5 collective-permute-done.21
  220.0 14.8 %up.1 = (bf16[4,512,1152]{2,1,0:T(8,128)(2,1)}, bf16[4,512,1152]{2,1,0:T(8,128)(2,1)}, bf16[4,576,512]{2,1,0:T(8,128)(2,1)}, bf16[4,576,512]{2,1,0:T(8,128)(2,1)}) custom-call(s32[2]{0:T(128)} %pad_add_fusion.where, bf16[512,1152]{1,0:T(8,128)(2,1)} %get-tuple-element.170.h, bf16[4,1152,1152]{2,1,0:T(8,128)(2,1)} %bitcast.146), custom_call_target="tpu_custom_call" | custom-call | flops 17250000 | bytes 1024 | tf_op jit(solution)/shard_map/up/pallas_call | solution.py:484
  234.8 13.0 %collective-permute-done.25.refs_1_ = bf16[2,2,144,1152]{3,2,1,0:T(8,128)(2,1)} collective-permute-done((bf16[2,2,144,1152]{3,2,1,0:T(8,128)(2,1)S(1)}, bf16[2,2,144,1152]{3,2,1,0:T(8,128)(2,1)}, u32[]{:S(2)}, u32[]{:S(2)}) %collective-permute-start.25) | collective-permute-done | bytes 1327136 | tf_op jit(solution)/shard_map/ppermute | solution.py:101
  251.4 6.1 %collective-permute-done.27.refs_2_ = bf16[2,2,144,1152]{3,2,1,0:T(8,128)(2,1)S(1)} collective-permute-done((bf16[2,2,144,1152]{3,2,1,0:T(8,128)(2,1)S(1)}, bf16[2,2,144,1152]{3,2,1,0:T(8,128)(2,1)S(1)}, u32[]{:S(2)}, u32[]{:S(2)}) %collective-permute-start.27) | collective-permute-done | bytes 1327136 | tf_op jit(solution)/shard_map/ppermute | solution.py:101
  259.4 3.4 collective-permute-done.30.refs_3_
  265.2 11.0 %weight_grads.4 = (bf16[2,2,144,1152]{3,2,1,0:T(8,128)(2,1)}, bf16[2,2,144,1152]{3,2,1,0:T(8,128)(2,1)}, bf16[2,2,144,1152]{3,2,1,0:T(8,128)(2,1)}, bf16[2,2,144,1152]{3,2,1,0:T(8,128)(2,1)}) custom-call(bf16[4,576,512]{2,1,0:T(8,128)(2,1)} %get-tuple-element.175.refs_0_, bf16[4,576,512]{2,1,0:T(8,128)(2,1)} %copy-done.11, bf16[512,1152]{1,0:T(8,128)(2,1)} %copy-done.3, ...), custom_call_target="tpu_custom_call" | custom-call | flops 12650000 | bytes 1024 | tf_op jit(solution)/shard_map/weight_grads/pallas_call | solution.py:484
  279.2 8.7 %assemble.7 = bf16[4,8,144,1152]{3,2,1,0:T(8,128)(2,1)} custom-call(s32[2]{0:T(128)} %pad_add_fusion.where, bf16[2,2,144,1152]{3,2,1,0:T(8,128)(2,1)} %copy-done.10, bf16[2,2,144,1152]{3,2,1,0:T(8,128)(2,1)} %collective-permute-done.25.refs_1_, bf16[2,2,144,1152]{3,2,1,0:T(8,128)(2,1)} %copy-done.33, ...), custom_call_target="tpu_custom_call" | custom-call | flops 10005000 | bytes 1024 | tf_op jit(solution)/shard_map/assemble/pallas_call | solution.py:256
  287.9 11.9 %down_back.1.gz.refs_2_ = bf16[4,512,1152]{2,1,0:T(8,128)(2,1)} custom-call(bf16[512,1152]{1,0:T(8,128)(2,1)} %copy-done.3, bf16[4,1152,1152]{2,1,0:T(8,128)(2,1)} %bitcast.144, bf16[4,512,1152]{2,1,0:T(8,128)(2,1)} %get-tuple-element.184.slope), custom_call_target="tpu_custom_call" | custom-call | flops 13800000 | bytes 1024 | tf_op jit(solution)/shard_map/down_back/pallas_call | solution.py:484
  299.8 16.2 %up_back.1 = (f32[512,1152]{1,0:T(8,128)}, bf16[512,1152]{1,0:T(8,128)(2,1)}, f32[8,1152]{1,0:T(8,128)}) custom-call(bf16[4,512,1152]{2,1,0:T(8,128)(2,1)} %down_back.1.gz.refs_2_, bf16[4,1152,1152]{2,1,0:T(8,128)(2,1)} %bitcast.147, f32[512,1152]{1,0:T(8,128)} %get-tuple-element.185.middle, bf16[512,1152]{1,0:T(8,128)(2,1)} %grad.3, ...), custom_call_target="tpu_custom_call" | custom-call | flops 18400000 | bytes 1024 | tf_op jit(solution)/shard_map/up_back/pallas_call | solution.py:484
  321.9 8.7 %out_back.1 = (bf16[16,80,512]{2,1,0:T(8,128)(2,1)}, bf16[4,4,80,576]{3,2,1,0:T(8,128)(2,1)}, bf16[4,4,80,576]{3,2,1,0:T(8,128)(2,1)}) custom-call(s32[2]{0:T(128)} %pad_add_fusion.where, bf16[8,80,512]{2,1,0:T(8,128)(2,1)} %get-tuple-element.155.one, bf16[8,80,512]{2,1,0:T(8,128)(2,1)} %get-tuple-element.158.two, bf16[2,1280,576]{2,1,0:T(8,128)(2,1)} %bitcast.157, ...), custom_call_target="tpu_custom_call" | custom-call | flops 10350000 | bytes 1024 | tf_op jit(solution)/shard_map/out_back/pallas_call | solution.py:484
  331.4 11.3 %weight_grads.5 = (bf16[2,2,144,1152]{3,2,1,0:T(8,128)(2,1)}, bf16[2,2,144,1152]{3,2,1,0:T(8,128)(2,1)}, bf16[2,2,144,1152]{3,2,1,0:T(8,128)(2,1)}, bf16[2,2,144,1152]{3,2,1,0:T(8,128)(2,1)}) custom-call(bf16[576,512]{1,0:T(8,128)(2,1)} %get-tuple-element.190.refs_0_, bf16[576,512]{1,0:T(8,128)(2,1)} %copy-done.41, ...), custom_call_target="tpu_custom_call" | custom-call | flops 12650000 | bytes 1024 | tf_op jit(solution)/shard_map/weight_grads/pallas_call | solution.py:484
  345.8 5.6 all-to-all-start.5
  357.1 16.5 %attend_back.2 = bf16[2,3,4,72,1024]{4,3,2,1,0:T(8,128)(2,1)} custom-call(bf16[4,12,72,1024]{3,2,1,0:T(8,128)(2,1)} %bitcast.134, bf16[4,12,72,1024]{3,2,1,0:T(8,128)(2,1)} %bitcast.135, bf16[4,12,72,1024]{3,2,1,0:T(8,128)(2,1)} %bitcast.136, bf16[4,12,72,1024]{3,2,1,0:T(8,128)(2,1)} %bitcast.137, bf16[4,12,72,1024]{3,2,1,0:T(8,128)(2,1)} %bitcast.138, ...), custom_call_target="tpu_custom_call" | custom-call | flops 19090000 | bytes 1024 | tf_op jit(solution)/shard_map/attend_back/pallas_call | solution.py:400
  373.6 16.7 %attend_back.3 = bf16[2,3,4,72,1024]{4,3,2,1,0:T(8,128)(2,1)} custom-call(bf16[4,12,72,1024]{3,2,1,0:T(8,128)(2,1)} %bitcast.139, bf16[4,12,72,1024]{3,2,1,0:T(8,128)(2,1)} %bitcast.140, bf16[4,12,72,1024]{3,2,1,0:T(8,128)(2,1)} %bitcast.141, bf16[4,12,72,1024]{3,2,1,0:T(8,128)(2,1)} %bitcast.142, bf16[4,12,72,1024]{3,2,1,0:T(8,128)(2,1)} %bitcast.143, ...), custom_call_target="tpu_custom_call" | custom-call | flops 19090000 | bytes 1024 | tf_op jit(solution)/shard_map/attend_back/pallas_call | solution.py:400
  398.8 16.0 %qkv_back.1 = (f32[512,1152]{1,0:T(8,128)}, bf16[512,1152]{1,0:T(8,128)(2,1)}) custom-call(bf16[2,864,1024]{2,1,0:T(8,128)(2,1)} %bitcast.154, bf16[2,864,1024]{2,1,0:T(8,128)(2,1)} %bitcast.150, bf16[4,1152,864]{2,1,0:T(8,128)(2,1)} %bitcast.149), custom_call_target="tpu_custom_call" | custom-call | flops 18400000 | bytes 1024 | tf_op jit(solution)/shard_map/qkv_back/pallas_call | solution.py:484
  419.1 5.3 all-to-all-start.6
  428.5 9.2 %weight_grads.6 = (bf16[2,2,144,864]{3,2,1,0:T(8,128)(2,1)}, bf16[2,2,144,864]{3,2,1,0:T(8,128)(2,1)}) custom-call(bf16[576,1024]{1,0:T(8,128)(2,1)} %get-tuple-element.201.refs_0_, bf16[576,1024]{1,0:T(8,128)(2,1)} %copy-done.5, bf16[2,864,1024]{2,1,0:T(8,128)(2,1)} %bitcast.155, bf16[2,864,1024]{2,1,0:T(8,128)(2,1)} %collective-permute-done.45.refs_3_), custom_call_target="tpu_custom_call" | custom-call | flops 12650000 | bytes 1024 | tf_op jit(solution)/shard_map/weight_grads/pallas_call | solution.py:484
  441.1 9.2 %weight_grads.7 = (bf16[2,2,144,864]{3,2,1,0:T(8,128)(2,1)}, bf16[2,2,144,864]{3,2,1,0:T(8,128)(2,1)}) custom-call(bf16[576,1024]{1,0:T(8,128)(2,1)} %get-tuple-element.201.refs_0_, bf16[576,1024]{1,0:T(8,128)(2,1)} %copy-done.5, bf16[2,864,1024]{2,1,0:T(8,128)(2,1)} %bitcast.151, bf16[2,864,1024]{2,1,0:T(8,128)(2,1)} %collective-permute-done.46.refs_3_), custom_call_target="tpu_custom_call" | custom-call | flops 12650000 | bytes 1024 | tf_op jit(solution)/shard_map/weight_grads/pallas_call | solution.py:484
  454.7 5.8 %step.5 = (f32[144,72,72]{2,1,0:T(8,128)}, f32[144,72,72]{2,1,0:T(8,128)}, f32[2,144,72,72]{3,2,1,0:T(8,128)}) custom-call(bf16[4,144,1152]{2,1,0:T(8,128)(2,1)} %copy-done.4, f32[144,72,72]{2,1,0:T(8,128)} %master_ref.9, f32[144,72,72]{2,1,0:T(8,128)} %moment_ref.9, f32[2,144,72,72]{3,2,1,0:T(8,128)} %stats_ref.9, f32[2,144,72,72]{3,2,1,0:T(8,128)} %roots_ref.9), custom_call_target="tpu_custom_call" | custom-call | flops 6900000 | bytes 1024 | tf_op jit(solution)/shard_map/step/pallas_call | solution.py:452
  460.5 13.0 %down.1 = (bf16[512,1152]{1,0:T(8,128)(2,1)}, f32[8,1152]{1,0:T(8,128)}) custom-call(bf16[4,512,1152]{2,1,0:T(8,128)(2,1)} %get-tuple-element.230.u, bf16[4,1152,1152]{2,1,0:T(8,128)(2,1)} %bitcast.145, f32[512,1152]{1,0:T(8,128)} %get-tuple-element.185.middle, bf16[512,1152]{1,0:T(8,128)(2,1)} %grad.3, f32[6,1152]{1,0:T(8,128)} %reshape.181.mods), custom_call_target="tpu_custom_call" | custom-call | flops 14950000 | bytes 1024 | tf_op jit(solution)/shard_map/down/pallas_call | solution.py:484
  474.3 5.8 %last.1 = (f32[512,1152]{1,0:T(8,128)}, f32[8,1152]{1,0:T(8,128)}) custom-call(f32[512,1152]{1,0:T(8,128)} %get-tuple-element.232.own, bf16[512,1152]{1,0:T(8,128)(2,1)} %collective-permute-done.47.far, bf16[512,1152]{1,0:T(8,128)(2,1)} %tokens.5, f32[512,1152]{1,0:T(8,128)} %get-tuple-element.235.gx, f32[6,1152]{1,0:T(8,128)} %reshape.181.mods), custom_call_target="tpu_custom_call" | custom-call | flops 6900000 | bytes 1024 | tf_op jit(solution)/shard_map/last/pallas_call | solution.py:484
  488.1 5.7 all-to-all-start.7
  499.9 3.7 all-to-all-done.7
  506.8 12.4 %collective-permute-done.53 = bf16[4,80,576]{2,1,0:T(8,128)(2,1)} collective-permute-done((bf16[4,80,576]{2,1,0:T(8,128)(2,1)}, bf16[4,80,576]{2,1,0:T(8,128)(2,1)}, u32[]{:S(2)}, u32[]{:S(2)}) %collective-permute-start.53) | collective-permute-done | bytes 368672 | tf_op jit(solution)/shard_map/ppermute | solution.py:101
  522.6 4.5 all-to-all-start.8
  532.8 5.8 %step.6 = (f32[144,72,72]{2,1,0:T(8,128)}, f32[144,72,72]{2,1,0:T(8,128)}, f32[2,144,72,72]{3,2,1,0:T(8,128)}) custom-call(bf16[4,144,1152]{2,1,0:T(8,128)(2,1)} %all-to-all-done.6.grads_ref, f32[144,72,72]{2,1,0:T(8,128)} %master_ref.9, f32[144,72,72]{2,1,0:T(8,128)} %moment_ref.9, ...), custom_call_target="tpu_custom_call", output_to_operand_aliasing={{0}: (5, {}), {1}: (6, {}), {2}: (7, {})} | custom-call | flops 6900000 | bytes 1024 | tf_op jit(solution)/shard_map/step/pallas_call | solution.py:452
  538.6 7.2 %step.7 = (f32[144,72,72]{2,1,0:T(8,128)}, f32[144,72,72]{2,1,0:T(8,128)}, f32[2,144,72,72]{3,2,1,0:T(8,128)}) custom-call(f32[1,144,1728]{2,1,0:T(8,128)} %bitcast.160, f32[144,72,72]{2,1,0:T(8,128)} %master_ref.9, f32[144,72,72]{2,1,0:T(8,128)} %moment_ref.9, ...), custom_call_target="tpu_custom_call", output_to_operand_aliasing={{0}: (5, {}), {1}: (6, {}), {2}: (7, {})} | custom-call | flops 6900000 | bytes 1024 | tf_op jit(solution)/shard_map/step/pallas_call | solution.py:452
  547.9 3.5 all-to-all-start.9
  553.2 9.6 %all-to-all-done.9.grads_ref = bf16[4,72,576]{2,1,0:T(8,128)(2,1)S(1)} async-done(((bf16[4,72,576]{2,1,0:T(8,128)(2,1)}), bf16[4,72,576]{2,1,0:T(8,128)(2,1)S(1)}, u32[]{:S(2)}, u32[]{:S(2)}) %all-to-all-start.9) | async-done | bytes 331808 | tf_op jit(solution)/shard_map/all_to_all | solution.py:96
  563.5 3.1 step.8
  566.6 4.9 step.9
  (305 shorter events, 161.0 us)
Async XLA Ops:
  4.8 22.0 %collective-permute-start = (bf16[144,864]{1,0:T(8,128)(2,1)}, bf16[144,864]{1,0:T(8,128)(2,1)}, u32[]{:S(2)}, u32[]{:S(2)}) collective-permute-start(bf16[144,864]{1,0:T(8,128)(2,1)} %reshape.173), channel_id=1, source_target_pairs={{0,1},{1,2},{2,3},{3,0},{4,5},{5,6},{6,7},{7,4},{8,9},{9,10},{10,1... | collective-permute-start | bytes 746504 | tf_op jit(solution)/shard_map/ppermute | solution.py:120
  12.3 18.0 %collective-permute-start.3 = (bf16[144,864]{1,0:T(8,128)(2,1)}, bf16[144,864]{1,0:T(8,128)(2,1)}, u32[]{:S(2)}, u32[]{:S(2)}) collective-permute-start(bf16[144,864]{1,0:T(8,128)(2,1)} %reshape.173), channel_id=1, source_target_pairs={{0,3},{1,0},{2,1},{3,2},{4,7},{5,4},{6,5},{7,6},{8,11},{9,8},{10,9... | collective-permute-start | bytes 746504 | tf_op jit(solution)/shard_map/ppermute | solution.py:120
  14.5 21.7 %collective-permute-start.2 = (bf16[144,864]{1,0:T(8,128)(2,1)}, bf16[144,864]{1,0:T(8,128)(2,1)}, u32[]{:S(2)}, u32[]{:S(2)}) collective-permute-start(bf16[144,864]{1,0:T(8,128)(2,1)} %reshape.173), channel_id=1, source_target_pairs={{0,2},{1,3},{2,0},{3,1},{4,6},{5,7},{6,4},{7,5},{8,10},{9,11},{10,... | collective-permute-start | bytes 746504 | tf_op jit(solution)/shard_map/ppermute | solution.py:120
  21.8 20.7 %all-to-all-start.1 = ((f32[32,1,1728]{2,1,0:T(1,128)}), f32[32,1,1728]{2,1,0:T(1,128)}, u32[]{:S(2)}, u32[]{:S(2)}) async-start(f32[32,1,1728]{2,1,0:T(1,128)} %all_to_all.37), calls=%async_computation.1 | async-start | bytes 458752 | tf_op jit(solution)/shard_map/all_to_all | solution.py:96
  28.6 21.8 %collective-permute-start.1 = (bf16[1,2,144,864]{3,2,1,0:T(8,128)(2,1)}, bf16[1,2,144,864]{3,2,1,0:T(8,128)(2,1)}, u32[]{:S(2)}, u32[]{:S(2)}) collective-permute-start(bf16[1,2,144,864]{3,2,1,0:T(8,128)(2,1)} %maximum_bitcast_fusion), channel_id=1, source_target_pairs={{0,8},{4,12},{8,0},{12,4},{16,24},{20,28},{24,16},{28,20},{1,9},{5... | collective-permute-start | bytes 1493000 | tf_op jit(solution)/shard_map/ppermute | solution.py:101
  46.0 58.3 %all-to-all-start.2 = ((bf16[4,144,1152]{2,1,0:T(8,128)(2,1)}), bf16[4,144,1152]{2,1,0:T(8,128)(2,1)}, u32[]{:S(2)}, u32[]{:S(2)}) async-start(bf16[4,144,1152]{2,1,0:T(8,128)(2,1)} %broadcast_in_dim.49), calls=%async_computation.2 | async-start | bytes 2654208 | tf_op jit(solution)/shard_map/all_to_all | solution.py:96
  53.7 23.4 %collective-permute-start.6 = (bf16[2,2,144,864]{3,2,1,0:T(8,128)(2,1)}, bf16[2,2,144,864]{3,2,1,0:T(8,128)(2,1)}, u32[]{:S(2)}, u32[]{:S(2)}) collective-permute-start(bf16[2,2,144,864]{3,2,1,0:T(8,128)(2,1)} %pad_maximum_fusion.3.refs_0_), channel_id=1, source_target_pairs={{0,16},{4,20},{8,24},{12,28},{16,0},{20,4},{24,8},{28,12},{1,17},{... | collective-permute-start | bytes 2985992 | tf_op jit(solution)/shard_map/ppermute | solution.py:101
  57.3 22.4 %collective-permute-start.7 = (bf16[2,2,144,864]{3,2,1,0:T(8,128)(2,1)}, bf16[2,2,144,864]{3,2,1,0:T(8,128)(2,1)}, u32[]{:S(2)}, u32[]{:S(2)}) collective-permute-start(bf16[2,2,144,864]{3,2,1,0:T(8,128)(2,1)} %pad_maximum_fusion.4.refs_4_), channel_id=1, source_target_pairs={{0,8},{4,12},{8,0},{12,4},{16,24},{20,28},{24,16},{28,20},{1,9},{5... | collective-permute-start | bytes 2985992 | tf_op jit(solution)/shard_map/ppermute | solution.py:101
  58.7 39.8 %collective-permute-start.5 = (bf16[512,1152]{1,0:T(8,128)(2,1)}, bf16[512,1152]{1,0:T(8,128)(2,1)}, u32[]{:S(2)}, u32[]{:S(2)}) collective-permute-start(bf16[512,1152]{1,0:T(8,128)(2,1)} %tokens.5), channel_id=1, source_target_pairs={{0,1},{1,0},{2,3},{3,2},{4,5},{5,4},{6,7},{7,6},{8,9},{9,8},{10,11... | collective-permute-start | bytes 3538952 | tf_op jit(solution)/shard_map/ppermute | solution.py:111
  59.6 55.5 %collective-permute-start.8 = (bf16[2,2,144,864]{3,2,1,0:T(8,128)(2,1)}, bf16[2,2,144,864]{3,2,1,0:T(8,128)(2,1)}, u32[]{:S(2)}, u32[]{:S(2)}) collective-permute-start(bf16[2,2,144,864]{3,2,1,0:T(8,128)(2,1)} %pad_maximum_fusion.3.refs_0_), channel_id=1, source_target_pairs={{0,4},{4,0},{8,12},{12,8},{16,20},{20,16},{24,28},{28,24},{1,5},{5... | collective-permute-start | bytes 2985992 | tf_op jit(solution)/shard_map/ppermute | solution.py:101
  59.6 56.0 %collective-permute-start.10 = (bf16[2,2,144,864]{3,2,1,0:T(8,128)(2,1)}, bf16[2,2,144,864]{3,2,1,0:T(8,128)(2,1)}, u32[]{:S(2)}, u32[]{:S(2)}) collective-permute-start(bf16[2,2,144,864]{3,2,1,0:T(8,128)(2,1)} %pad_maximum_fusion.4.refs_4_), channel_id=1, source_target_pairs={{0,4},{4,0},{8,12},{12,8},{16,20},{20,16},{24,28},{28,24},{1,5},{5... | collective-permute-start | bytes 2985992 | tf_op jit(solution)/shard_map/ppermute | solution.py:101
  79.6 36.0 %collective-permute-start.9 = (bf16[2,2,144,864]{3,2,1,0:T(8,128)(2,1)}, bf16[2,2,144,864]{3,2,1,0:T(8,128)(2,1)}, u32[]{:S(2)}, u32[]{:S(2)}) collective-permute-start(bf16[2,2,144,864]{3,2,1,0:T(8,128)(2,1)} %collective-permute-done.6.refs_1_), channel_id=1, source_target_pairs={{0,4},{4,0},{8,12},{12,8},{16,20},{20,16},{24,28},{28,24},{1,5},{5... | collective-permute-start | bytes 2985992 | tf_op jit(solution)/shard_map/ppermute | solution.py:101
  79.6 36.0 %collective-permute-start.11 = (bf16[2,2,144,864]{3,2,1,0:T(8,128)(2,1)}, bf16[2,2,144,864]{3,2,1,0:T(8,128)(2,1)}, u32[]{:S(2)}, u32[]{:S(2)}) collective-permute-start(bf16[2,2,144,864]{3,2,1,0:T(8,128)(2,1)} %collective-permute-done.7.refs_5_), channel_id=1, source_target_pairs={{0,4},{4,0},{8,12},{12,8},{16,20},{20,16},{24,28},{28,24},{1,5},{5... | collective-permute-start | bytes 2985992 | tf_op jit(solution)/shard_map/ppermute | solution.py:101
  105.1 18.1 %all-to-all-start.3 = ((bf16[4,80,576]{2,1,0:T(8,128)(2,1)}), bf16[4,80,576]{2,1,0:T(8,128)(2,1)S(1)}, u32[]{:S(2)}, u32[]{:S(2)}) async-start(bf16[4,80,576]{2,1,0:T(8,128)(2,1)} %broadcast_in_dim.52), calls=%async_computation.3 | async-start | bytes 819200 | tf_op jit(solution)/shard_map/all_to_all | solution.py:96
  111.6 39.2 %collective-permute-start.12 = (bf16[1,2,144,1152]{3,2,1,0:T(8,128)(2,1)}, bf16[1,2,144,1152]{3,2,1,0:T(8,128)(2,1)}, u32[]{:S(2)}, u32[]{:S(2)}) collective-permute-start(bf16[1,2,144,1152]{3,2,1,0:T(8,128)(2,1)} %get-tuple-element.145), channel_id=1, source_target_pairs={{0,8},{4,12},{8,0},{12,4},{16,24},{20,28},{24,16},{28,20},{1,9},{5... | collective-permute-start | bytes 1990664 | tf_op jit(solution)/shard_map/ppermute | solution.py:101
  115.1 35.7 %collective-permute-start.13 = (bf16[1,2,144,1152]{3,2,1,0:T(8,128)(2,1)S(1)}, bf16[1,2,144,1152]{3,2,1,0:T(8,128)(2,1)}, u32[]{:S(2)}, u32[]{:S(2)}) collective-permute-start(bf16[1,2,144,1152]{3,2,1,0:T(8,128)(2,1)S(1)} %get-tuple-element.146), channel_id=1, source_target_pairs={{0,16},{4,20},{8,24},{12,28},{16,0},{20,4},{24,8},{28,12},{1,17},{... | collective-permute-start | bytes 1990664 | tf_op jit(solution)/shard_map/ppermute | solution.py:101
  123.2 17.6 %collective-permute-start.14 = (bf16[1,4,80,576]{3,2,1,0:T(8,128)(2,1)S(1)}, bf16[1,4,80,576]{3,2,1,0:T(8,128)(2,1)S(1)}, u32[]{:S(2)}, u32[]{:S(2)}) collective-permute-start(bf16[1,4,80,576]{3,2,1,0:T(8,128)(2,1)S(1)} %bitcast.161), channel_id=1, source_target_pairs={{0,8},{4,12},{8,0},{12,4},{16,24},{20,28},{24,16},{28,20},{1,9},{5... | collective-permute-start | bytes 1105928 | tf_op jit(solution)/shard_map/ppermute | solution.py:101
  141.8 23.6 %collective-permute-start.15 = (bf16[2,4,80,576]{3,2,1,0:T(8,128)(2,1)}, bf16[2,4,80,576]{3,2,1,0:T(8,128)(2,1)S(1)}, u32[]{:S(2)}, u32[]{:S(2)}) collective-permute-start(bf16[2,4,80,576]{3,2,1,0:T(8,128)(2,1)} %get-tuple-element.283), channel_id=1, source_target_pairs={{0,16},{4,20},{8,24},{12,28},{16,0},{20,4},{24,8},{28,12},{1,17},{... | collective-permute-start | bytes 2211848 | tf_op jit(solution)/shard_map/ppermute | solution.py:101
  145.5 41.4 %all-to-all-start.4 = ((bf16[4,144,1152]{2,1,0:T(8,128)(2,1)}), bf16[4,144,1152]{2,1,0:T(8,128)(2,1)S(1)}, u32[]{:S(2)}, u32[]{:S(2)}) async-start(bf16[4,144,1152]{2,1,0:T(8,128)(2,1)} %broadcast_in_dim.54), calls=%async_computation.4 | async-start | bytes 2654208 | tf_op jit(solution)/shard_map/all_to_all | solution.py:96
  166.3 18.6 %collective-permute-start.18 = (bf16[4,4,80,576]{3,2,1,0:T(8,128)(2,1)}, bf16[4,4,80,576]{3,2,1,0:T(8,128)(2,1)S(1)}, u32[]{:S(2)}, u32[]{:S(2)}) collective-permute-start(bf16[4,4,80,576]{3,2,1,0:T(8,128)(2,1)} %constant_dynamic-update-slice_fusion.6), channel_id=1, source_target_pairs={{0,4},{4,0},{8,12},{12,8},{16,20},{20,16},{24,28},{28,24},{1,5},{5... | collective-permute-start | bytes 4423688 | tf_op jit(solution)/shard_map/ppermute | solution.py:101
  166.9 32.0 %collective-permute-start.19 = (bf16[2,2,144,1152]{3,2,1,0:T(8,128)(2,1)}, bf16[2,2,144,1152]{3,2,1,0:T(8,128)(2,1)}, u32[]{:S(2)}, u32[]{:S(2)}) collective-permute-start(bf16[2,2,144,1152]{3,2,1,0:T(8,128)(2,1)} %constant_dynamic-update-slice_fusion.refs_0_), channel_id=1, source_target_pairs={{0,16},{4,20},{8,24},{12,28},{16,0},{20,4},{24,8},{28,12},{1,17},{... | collective-permute-start | bytes 3981320 | tf_op jit(solution)/shard_map/ppermute | solution.py:101
  167.2 31.6 %collective-permute-start.20 = (bf16[2,2,144,1152]{3,2,1,0:T(8,128)(2,1)}, bf16[2,2,144,1152]{3,2,1,0:T(8,128)(2,1)}, u32[]{:S(2)}, u32[]{:S(2)}) collective-permute-start(bf16[2,2,144,1152]{3,2,1,0:T(8,128)(2,1)} %constant_dynamic-update-slice_fusion.2.refs_4_), channel_id=1, source_target_pairs={{0,8},{4,12},{8,0},{12,4},{16,24},{20,28},{24,16},{28,20},{1,9},{5... | collective-permute-start | bytes 3981320 | tf_op jit(solution)/shard_map/ppermute | solution.py:101
  217.8 30.1 %collective-permute-start.25 = (bf16[2,2,144,1152]{3,2,1,0:T(8,128)(2,1)S(1)}, bf16[2,2,144,1152]{3,2,1,0:T(8,128)(2,1)}, u32[]{:S(2)}, u32[]{:S(2)}) collective-permute-start(bf16[2,2,144,1152]{3,2,1,0:T(8,128)(2,1)S(1)} %constant_dynamic-update-slice_fusion.9.refs_0_), channel_id=1, source_target_pairs={{0,16},{4,20},{8,24},{12,28},{16,0},{20,4},{24,8},{28,12},{1,17},{... | collective-permute-start | bytes 3981320 | tf_op jit(solution)/shard_map/ppermute | solution.py:101
  219.4 29.8 %collective-permute-start.26 = (bf16[2,2,144,1152]{3,2,1,0:T(8,128)(2,1)S(1)}, bf16[2,2,144,1152]{3,2,1,0:T(8,128)(2,1)}, u32[]{:S(2)}, u32[]{:S(2)}) collective-permute-start(bf16[2,2,144,1152]{3,2,1,0:T(8,128)(2,1)S(1)} %constant_dynamic-update-slice_fusion.11.refs_4_), channel_id=1, source_target_pairs={{0,8},{4,12},{8,0},{12,4},{16,24},{20,28},{24,16},{28,20},{1,9},{5... | collective-permute-start | bytes 3981320 | tf_op jit(solution)/shard_map/ppermute | solution.py:101
  251.3 27.9 %collective-permute-start.33 = (bf16[2,2,144,1152]{3,2,1,0:T(8,128)(2,1)}, bf16[2,2,144,1152]{3,2,1,0:T(8,128)(2,1)}, u32[]{:S(2)}, u32[]{:S(2)}) collective-permute-start(bf16[2,2,144,1152]{3,2,1,0:T(8,128)(2,1)} %collective-permute-done.25.refs_1_), channel_id=1, source_target_pairs={{0,4},{4,0},{8,12},{12,8},{16,20},{20,16},{24,28},{28,24},{1,5},{5... | collective-permute-start | bytes 3981320 | tf_op jit(solution)/shard_map/ppermute | solution.py:101
  257.5 21.7 %collective-permute-start.34 = (bf16[2,2,144,1152]{3,2,1,0:T(8,128)(2,1)}, bf16[2,2,144,1152]{3,2,1,0:T(8,128)(2,1)}, u32[]{:S(2)}, u32[]{:S(2)}) collective-permute-start(bf16[2,2,144,1152]{3,2,1,0:T(8,128)(2,1)} %collective-permute-done.26.refs_5_), channel_id=1, source_target_pairs={{0,4},{4,0},{8,12},{12,8},{16,20},{20,16},{24,28},{28,24},{1,5},{5... | collective-permute-start | bytes 3981320 | tf_op jit(solution)/shard_map/ppermute | solution.py:101
  277.7 38.3 %collective-permute-start.31 = (bf16[2,2,144,1152]{3,2,0,1:T(8,128)(2,1)S(1)}, bf16[2,2,144,1152]{3,2,0,1:T(8,128)(2,1)}, u32[]{:S(2)}, u32[]{:S(2)}) collective-permute-start(bf16[2,2,144,1152]{3,2,0,1:T(8,128)(2,1)S(1)} %copy.142), channel_id=1, source_target_pairs={{0,16},{4,20},{8,24},{12,28},{16,0},{20,4},{24,8},{28,12},{1,17},{... | collective-permute-start | bytes 3981320 | tf_op jit(solution)/shard_map/ppermute | solution.py:101
  278.5 37.5 %collective-permute-start.32 = (bf16[2,2,144,1152]{3,2,0,1:T(8,128)(2,1)S(1)}, bf16[2,2,144,1152]{3,2,0,1:T(8,128)(2,1)}, u32[]{:S(2)}, u32[]{:S(2)}) collective-permute-start(bf16[2,2,144,1152]{3,2,0,1:T(8,128)(2,1)S(1)} %copy.143), channel_id=1, source_target_pairs={{0,8},{4,12},{8,0},{12,4},{16,24},{20,28},{24,16},{28,20},{1,9},{5... | collective-permute-start | bytes 3981320 | tf_op jit(solution)/shard_map/ppermute | solution.py:101
  319.0 23.7 %collective-permute-start.35 = (bf16[2,144,1152]{2,1,0:T(8,128)(2,1)S(1)}, bf16[2,144,1152]{2,1,0:T(8,128)(2,1)S(1)}, u32[]{:S(2)}, u32[]{:S(2)}) collective-permute-start(bf16[2,144,1152]{2,1,0:T(8,128)(2,1)S(1)} %fusion.8), channel_id=1, source_target_pairs={{0,8},{4,12},{8,0},{12,4},{16,24},{20,28},{24,16},{28,20},{1,9},{5... | collective-permute-start | bytes 1990664 | tf_op jit(solution)/shard_map/ppermute | solution.py:101
  320.5 22.2 %collective-permute-start.36 = (bf16[2,144,1152]{2,1,0:T(8,128)(2,1)S(1)}, bf16[2,144,1152]{2,1,0:T(8,128)(2,1)S(1)}, u32[]{:S(2)}, u32[]{:S(2)}) collective-permute-start(bf16[2,144,1152]{2,1,0:T(8,128)(2,1)S(1)} %fusion.9), channel_id=1, source_target_pairs={{0,16},{4,20},{8,24},{12,28},{16,0},{20,4},{24,8},{28,12},{1,17},{... | collective-permute-start | bytes 1990664 | tf_op jit(solution)/shard_map/ppermute | solution.py:101
  345.8 45.6 %all-to-all-start.5 = ((bf16[4,144,1152]{2,1,0:T(8,128)(2,1)}), bf16[4,144,1152]{2,1,0:T(8,128)(2,1)S(1)}, u32[]{:S(2)}, u32[]{:S(2)}) async-start(bf16[4,144,1152]{2,1,0:T(8,128)(2,1)} %pad_maximum_fusion.1), calls=%async_computation.5 | async-start | bytes 2654208 | tf_op jit(solution)/shard_map/all_to_all | solution.py:96
  352.9 37.4 %collective-permute-start.39 = (bf16[2,2,144,1152]{3,2,0,1:T(8,128)(2,1)S(1)}, bf16[2,2,144,1152]{3,2,0,1:T(8,128)(2,1)S(1)}, u32[]{:S(2)}, u32[]{:S(2)}) collective-permute-start(bf16[2,2,144,1152]{3,2,0,1:T(8,128)(2,1)S(1)} %copy.148), channel_id=1, source_target_pairs={{0,16},{4,20},{8,24},{12,28},{16,0},{20,4},{24,8},{28,12},{1,17},{... | collective-permute-start | bytes 3981320 | tf_op jit(solution)/shard_map/ppermute | solution.py:101
  354.2 37.2 %collective-permute-start.40 = (bf16[2,2,144,1152]{3,2,0,1:T(8,128)(2,1)S(1)}, bf16[2,2,144,1152]{3,2,0,1:T(8,128)(2,1)S(1)}, u32[]{:S(2)}, u32[]{:S(2)}) collective-permute-start(bf16[2,2,144,1152]{3,2,0,1:T(8,128)(2,1)S(1)} %copy.149), channel_id=1, source_target_pairs={{0,8},{4,12},{8,0},{12,4},{16,24},{20,28},{24,16},{28,20},{1,9},{5... | collective-permute-start | bytes 3981320 | tf_op jit(solution)/shard_map/ppermute | solution.py:101
  396.6 30.9 %collective-permute-start.45 = (bf16[2,864,1024]{2,1,0:T(8,128)(2,1)}, bf16[2,864,1024]{2,1,0:T(8,128)(2,1)}, u32[]{:S(2)}, u32[]{:S(2)}) collective-permute-start(bf16[2,864,1024]{2,1,0:T(8,128)(2,1)} %bitcast.153), channel_id=1, source_target_pairs={{0,4},{4,0},{8,12},{12,8},{16,20},{20,16},{24,28},{28,24},{1,5},{5... | collective-permute-start | bytes 10616840 | tf_op jit(solution)/shard_map/ppermute | solution.py:101
  396.9 44.2 %collective-permute-start.46 = (bf16[2,864,1024]{2,1,0:T(8,128)(2,1)S(1)}, bf16[2,864,1024]{2,1,0:T(8,128)(2,1)}, u32[]{:S(2)}, u32[]{:S(2)}) collective-permute-start(bf16[2,864,1024]{2,1,0:T(8,128)(2,1)S(1)} %bitcast.152), channel_id=1, source_target_pairs={{0,4},{4,0},{8,12},{12,8},{16,20},{20,16},{24,28},{28,24},{1,5},{5... | collective-permute-start | bytes 10616840 | tf_op jit(solution)/shard_map/ppermute | solution.py:101
  397.2 17.7 %collective-permute-start.43 = (bf16[2,144,1152]{2,1,0:T(8,128)(2,1)S(1)}, bf16[2,144,1152]{2,1,0:T(8,128)(2,1)S(1)}, u32[]{:S(2)}, u32[]{:S(2)}) collective-permute-start(bf16[2,144,1152]{2,1,0:T(8,128)(2,1)S(1)} %fusion.11), channel_id=1, source_target_pairs={{0,8},{4,12},{8,0},{12,4},{16,24},{20,28},{24,16},{28,20},{1,9},{5... | collective-permute-start | bytes 1990664 | tf_op jit(solution)/shard_map/ppermute | solution.py:101
  419.1 54.4 %all-to-all-start.6 = ((bf16[4,144,1152]{2,1,0:T(8,128)(2,1)}), bf16[4,144,1152]{2,1,0:T(8,128)(2,1)}, u32[]{:S(2)}, u32[]{:S(2)}) async-start(bf16[4,144,1152]{2,1,0:T(8,128)(2,1)} %pad_maximum_fusion.2), calls=%async_computation.6 | async-start | bytes 2654208 | tf_op jit(solution)/shard_map/all_to_all | solution.py:96
  424.4 49.8 %collective-permute-start.47 = (bf16[512,1152]{1,0:T(8,128)(2,1)}, bf16[512,1152]{1,0:T(8,128)(2,1)}, u32[]{:S(2)}, u32[]{:S(2)}) collective-permute-start(bf16[512,1152]{1,0:T(8,128)(2,1)} %get-tuple-element.234), channel_id=1, source_target_pairs={{0,1},{1,0},{2,3},{3,2},{4,5},{5,4},{6,7},{7,6},{8,9},{9,8},{10,11... | collective-permute-start | bytes 3538952 | tf_op jit(solution)/shard_map/ppermute | solution.py:111
  440.0 42.7 %collective-permute-start.48 = (bf16[2,2,144,864]{3,2,0,1:T(8,128)(2,1)}, bf16[2,2,144,864]{3,2,0,1:T(8,128)(2,1)}, u32[]{:S(2)}, u32[]{:S(2)}) collective-permute-start(bf16[2,2,144,864]{3,2,0,1:T(8,128)(2,1)} %copy.156), channel_id=1, source_target_pairs={{0,16},{4,20},{8,24},{12,28},{16,0},{20,4},{24,8},{28,12},{1,17},{... | collective-permute-start | bytes 2985992 | tf_op jit(solution)/shard_map/ppermute | solution.py:101
  452.6 30.1 %collective-permute-start.49 = (bf16[2,2,144,864]{3,2,0,1:T(8,128)(2,1)}, bf16[2,2,144,864]{3,2,0,1:T(8,128)(2,1)S(1)}, u32[]{:S(2)}, u32[]{:S(2)}) collective-permute-start(bf16[2,2,144,864]{3,2,0,1:T(8,128)(2,1)} %copy.157), channel_id=1, source_target_pairs={{0,8},{4,12},{8,0},{12,4},{16,24},{20,28},{24,16},{28,20},{1,9},{5... | collective-permute-start | bytes 2985992 | tf_op jit(solution)/shard_map/ppermute | solution.py:101
  453.9 28.8 %collective-permute-start.50 = (bf16[4,2,80,576]{3,2,0,1:T(8,128)(2,1)}, bf16[4,2,80,576]{3,2,0,1:T(8,128)(2,1)}, u32[]{:S(2)}, u32[]{:S(2)}) collective-permute-start(bf16[4,2,80,576]{3,2,0,1:T(8,128)(2,1)} %get-tuple-element.242), channel_id=1, source_target_pairs={{0,16},{4,20},{8,24},{12,28},{16,0},{20,4},{24,8},{28,12},{1,17},{... | collective-permute-start | bytes 2211848 | tf_op jit(solution)/shard_map/ppermute | solution.py:101
  493.8 25.3 %collective-permute-start.51 = (bf16[2,144,864]{2,1,0:T(8,128)(2,1)}, bf16[2,144,864]{2,1,0:T(8,128)(2,1)}, u32[]{:S(2)}, u32[]{:S(2)}) collective-permute-start(bf16[2,144,864]{2,1,0:T(8,128)(2,1)} %fusion.15), channel_id=1, source_target_pairs={{0,8},{4,12},{8,0},{12,4},{16,24},{20,28},{24,16},{28,20},{1,9},{5... | collective-permute-start | bytes 1493000 | tf_op jit(solution)/shard_map/ppermute | solution.py:101
  495.8 23.4 %collective-permute-start.52 = (bf16[2,144,864]{2,1,0:T(8,128)(2,1)S(1)}, bf16[2,144,864]{2,1,0:T(8,128)(2,1)}, u32[]{:S(2)}, u32[]{:S(2)}) collective-permute-start(bf16[2,144,864]{2,1,0:T(8,128)(2,1)S(1)} %fusion.16), channel_id=1, source_target_pairs={{0,16},{4,20},{8,24},{12,28},{16,0},{20,4},{24,8},{28,12},{1,17},{... | collective-permute-start | bytes 1493000 | tf_op jit(solution)/shard_map/ppermute | solution.py:101
  499.3 19.8 %collective-permute-start.53 = (bf16[4,80,576]{2,1,0:T(8,128)(2,1)}, bf16[4,80,576]{2,1,0:T(8,128)(2,1)}, u32[]{:S(2)}, u32[]{:S(2)}) collective-permute-start(bf16[4,80,576]{2,1,0:T(8,128)(2,1)} %get-tuple-element.273), channel_id=1, source_target_pairs={{0,8},{4,12},{8,0},{12,4},{16,24},{20,28},{24,16},{28,20},{1,9},{5... | collective-permute-start | bytes 1105928 | tf_op jit(solution)/shard_map/ppermute | solution.py:101
  522.6 25.2 %all-to-all-start.8 = ((f32[32,2,144]{2,1,0:T(2,128)}), f32[32,2,144]{2,1,0:T(2,128)S(1)}, u32[]{:S(2)}, u32[]{:S(2)}) async-start(f32[32,2,144]{2,1,0:T(2,128)} %bitcast.44), calls=%async_computation.8 | async-start | bytes 131072 | tf_op jit(solution)/shard_map/all_to_all | solution.py:96
  527.1 24.9 %collective-permute-start.56 = (bf16[144,864]{1,0:T(8,128)(2,1)S(1)}, bf16[144,864]{1,0:T(8,128)(2,1)S(1)}, u32[]{:S(2)}, u32[]{:S(2)}) collective-permute-start(bf16[144,864]{1,0:T(8,128)(2,1)S(1)} %get-tuple-element.281), channel_id=1, source_target_pairs={{0,1},{1,2},{2,3},{3,0},{4,5},{5,6},{6,7},{7,4},{8,9},{9,10},{10,1... | collective-permute-start | bytes 746504 | tf_op jit(solution)/shard_map/ppermute | solution.py:120
  528.9 23.1 %collective-permute-start.55 = (bf16[144,864]{1,0:T(8,128)(2,1)S(1)}, bf16[144,864]{1,0:T(8,128)(2,1)S(1)}, u32[]{:S(2)}, u32[]{:S(2)}) collective-permute-start(bf16[144,864]{1,0:T(8,128)(2,1)S(1)} %get-tuple-element.280), channel_id=1, source_target_pairs={{0,2},{1,3},{2,0},{3,1},{4,6},{5,7},{6,4},{7,5},{8,10},{9,11},{10,... | collective-permute-start | bytes 746504 | tf_op jit(solution)/shard_map/ppermute | solution.py:120
  531.4 20.6 %collective-permute-start.54 = (bf16[144,864]{1,0:T(8,128)(2,1)S(1)}, bf16[144,864]{1,0:T(8,128)(2,1)S(1)}, u32[]{:S(2)}, u32[]{:S(2)}) collective-permute-start(bf16[144,864]{1,0:T(8,128)(2,1)S(1)} %get-tuple-element.279), channel_id=1, source_target_pairs={{0,3},{1,0},{2,1},{3,2},{4,7},{5,4},{6,5},{7,6},{8,11},{9,8},{10,9... | collective-permute-start | bytes 746504 | tf_op jit(solution)/shard_map/ppermute | solution.py:120
  (66 other events, 593.1 us)

commit v4 on v3

--- a/solution.py
+++ b/solution.py
@@ -1370,39 +1370,41 @@
     keeps = [half.keep for half in red_up]
     down_one = land(red_down, *keeps)
     down_spread = exchange_t(jnp.concatenate(down_one))
+    wo_got = after(wo_got, *keeps)
+    red_out = Relative((add(wo_keep[:, 2:], wo_got[:, 2:]), add(wo_keep[:, :2], wo_got[:, :2])), 0, bits)
     for half in red_up:
         half.send(*down_one)
-    wo_got = after(wo_got, *keeps)
-    red_out = Relative((add(wo_keep[:, 2:], wo_got[:, 2:]), add(wo_keep[:, :2], wo_got[:, :2])), 0, bits)
+    h1_far = bit_swap(after(h1_send, *down_one), 1)
     g_one = attend_back(after(projected, red_out.keep, *down_one), go, log_one, heads, 0, cut)
     g_one = g_one.reshape(cut, 3 * head_cols, 2 * rows)
-    g_two = attend_back(after(projected, g_one), go, log_two, heads, cut, cut)
+    g_one_far = bit_swap(g_one, 1)
+    g_two = attend_back(after(projected, g_one, h1_far), go, log_two, heads, cut, cut)
     g_two = g_two.reshape(cut, 3 * head_cols, 2 * rows)
     up_two = land(red_up, g_two, down_spread)
     for half in red_up:
         half.send()
-    g_one_far = bit_swap(after(g_one, *up_two), 1)
-    h1_far = bit_swap(after(h1_send, *up_two), 1)
+    red_out.send(*up_two)
     g_two_far = bit_swap(after(g_two, *up_two), 1)
     gh_own, gh_other = qkv_back(after(g_one, *up_two), g_two, w_qkv)
     up_one = land(red_up, gh_own)
     gh_far = pair_swap(after(gh_other, *up_one))
-    up_spread = exchange_t(jnp.concatenate(up_one))
     grads = weight_grads(h1_keep, h1_far, after(g_one, *up_one), g_one_far, (0,) * cut, True)
     red_one = Relative(grads[0], 0, bits).send()
-    red_out.send(red_one.keep)
     grads = weight_grads(
         h1_keep, h1_far, after(g_two, red_one.keep), g_two_far, (1,) * cut, True
     )
     red_two = Relative(grads[1], 1, bits).send()
-    state = (master, moment, stats, roots)
-    done = step(after(down_spread, red_two.keep), spans[3], state, None)
-    result, sums_three = down_part(after(hidden, *done), w_down, middle, cotangent, mods)
-    grad_tokens, sums_one = last_part(after(gh_own, result, up_spread), gh_far, tokens, gx, mods)
-    one_two, two_two, out_two = land([red_one, red_two, red_out], grad_tokens)
+    red_out.add(red_two.keep)
+    red_out.send()
+    grad_tokens, sums_one = last_part(after(gh_own, red_two.keep), gh_far, tokens, gx, mods)
+    up_one = after(jnp.concatenate(up_one), gh_far)
+    up_spread = [take(up_one, t, 0)] + [
+        shift_t(take(up_one, (t + k) % tensor_size, 0), k) for k in range(1, tensor_size)
+    ]
+    result, sums_three = down_part(after(hidden, grad_tokens), w_down, middle, cotangent, mods)
+    one_two, two_two, out_one = land([red_one, red_two, red_out], result)
     red_one.send()
     red_two.send()
-    red_out.send()
 
     grad_mods = jnp.concatenate([sums_one[:2], sums_two[:3], sums_three[:1]])
     grad_mods = after(grad_mods.reshape(tensor_size, ada_c), one_two, two_two)
@@ -1411,23 +1413,25 @@
     grad_mods = jnp.sum(grad_mods.reshape(latents, span, ada_c), axis=1)
     grad_ada = jnp.einsum("sr,sc->rc", silu_mine.astype(f32), grad_mods, precision=HIGHEST)
     grad_silu = jnp.einsum("sc,rc->sr", grad_mods, w_ada.astype(f32), precision=HIGHEST)
-    *qkv_one, out_one = land([red_one, red_two, red_out], grad_ada, grad_silu)
+    state = (master, moment, stats, roots)
+    qkv_one = land([red_one, red_two], grad_ada, grad_silu)
     qkv_slots = [half[n] for half in qkv_one for n in range(cut)]
     qkv_spread = [qkv_slots[0]] + [
         shift_t(qkv_slots[k], tensor_size - k) for k in range(1, tensor_size)
     ]
-    grad_silu = after(grad_silu, *qkv_one).reshape(dp_size, 1, sequences, ada_r)
+    out_one = out_one[:, :ro]
+    out_slots = [take(out_one, (t + tensor_size - k) % tensor_size, 0) for k in range(tensor_size)]
+    out_spread = exchange_t(after(jnp.stack(out_slots), *qkv_one))
+    done = step(after(down_spread, *qkv_one), spans[3], state, None)
+    done = step(after(jnp.stack(up_spread), *qkv_one), spans[2], state, done)
+    done = step(after(grad_ada[None], *done), spans[4], state, done)
+    grad_silu = after(grad_silu, out_spread).reshape(dp_size, 1, sequences, ada_r)
     grad_silu = jnp.broadcast_to(grad_silu, (dp_size, tensor_size, sequences, ada_r))
     grad_silu = exchange(grad_silu.reshape(-1, sequences, ada_r), everyone)
-    done = step(after(up_spread, *qkv_one), spans[2], state, done)
-    done = step(after(grad_ada[None], *done), spans[4], state, done)
     grad_silu = jnp.sum(grad_silu.reshape(dp_size, tensor_size, sequences, ada_r), axis=1)
     grad_silu = jnp.moveaxis(grad_silu, 0, 1).reshape(sequences, width)
     _, silu_pullback = jax.vjp(jax.nn.silu, conditioning)
     grad_conditioning = silu_pullback(grad_silu)[0]
-    out_one = out_one[:, :ro]
-    out_slots = [take(out_one, (t + tensor_size - k) % tensor_size, 0) for k in range(tensor_size)]
-    out_spread = exchange_t(after(jnp.stack(out_slots), grad_silu))
     done = step(after(out_spread, *done), spans[1], state, done)
     done = step(after(jnp.stack(qkv_spread), *done), spans[0], state, done)
     return (result, grad_tokens, grad_conditioning, *done)

time: 582 us -> 561 us (0.964)
  waiting for transfers between devices: 109 us -> 83.7 us
    ppermute x49, waiting for transfers between devices: 72.8 us -> 57.5 us  [bit_swap(): return lax.ppermute(values, 'dp', [(k, k ^ bit) for k in range(size)])]
    ppermute x6 -> x9, starting transfers between devices: 11.7 us -> 18.3 us  [shift_t(): lax.ppermute(values, 'tensor', [(n, (n + k) % size) for n in range(size)])]
    ppermute x6 -> x9, waiting for transfers between devices: 5.9 us -> 0.02 us  [shift_t(): lax.ppermute(values, 'tensor', [(n, (n + k) % size) for n in range(size)])]
    all_to_all x10 -> x9, starting transfers between devices: 47.1 us -> 41.4 us  [exchange(): return lax.all_to_all(values, axis, split_axis=0, concat_axis=0, tiled=True)]
    unnamed x101 -> x97, local copies, waits for them, and re-layouts: 17.7 us -> 12.8 us
    all_to_all x10 -> x9, waiting for transfers between devices: 13.3 us -> 8.97 us  [exchange(): return lax.all_to_all(values, axis, split_axis=0, concat_axis=0, tiled=True)]
  transfers between devices with their start and end apart: 67 -> 69, of which waited for: 22 -> 20; matrix products, arithmetic and copies ran while one was open for 13% -> 17% of each run, Pallas kernels for 43% -> 46%
where the time goes in v4:
time: 561 us; the launch traced here: 552 us
  Pallas kernels  252 us (45%)
  starting transfers between devices  101 us (18%)
  waiting for transfers between devices  83.7 us (15%)
  local copies, waits for them, and re-layouts  49.6 us (9%)
  other arithmetic  45.4 us (8%)
  matrix products  18.4 us (3%)
    pallas_call x13, Pallas kernels, call(): pl.pallas_call(kernel, grid=grid, in_specs=in_specs, out_specs=[pl.BlockS...  141 us
    ppermute x49, waiting for transfers between devices, bit_swap(): return lax.ppermute(values, 'dp', [(k, k ^ bit) for k in range(size)])  57.5 us
    all_to_all x9, starting transfers between devices, exchange(): return lax.all_to_all(values, axis, split_axis=0, concat_axis=0, tiled=True)  41.4 us
    ppermute x49, starting transfers between devices, bit_swap(): return lax.ppermute(values, 'dp', [(k, k ^ bit) for k in range(size)])  34.5 us
    pallas_call x2, Pallas kernels, attend_back(): pl.pallas_call(attend_back_kernel, grid=(count,), in_specs=head_specs(hea...  33.6 us
    pallas_call x4, Pallas kernels, assemble(): pl.pallas_call(partial(assemble_kernel, plan, relative, per), out_shape=j...  28.9 us
    pallas_call x5, Pallas kernels, step(): pl.pallas_call(partial(step_kernel, size, len(aliased)), grid=(steps,), i...  26.8 us
    pallas_call x2, Pallas kernels, attend(): pl.pallas_call(attend_kernel, grid=(count,), in_specs=head_specs(heads, s...  21.6 us
  transfers between devices with their start and end apart: 69, of which 20 were waited for; matrix products, arithmetic and copies ran while one was open for 17% of the time, Pallas kernels for 46%

profile of v4, /device:TPU:0, one launch (start us, length us, event | category | flops | bytes accessed | tf_op | source)
XLA Modules:
  0.0 551.5 jit_solution(8840899429097182366)
XLA Ops:
  0.6 2.9 convert_element_type.303
  4.8 4.0 collective-permute-start.2
  10.9 3.7 all-to-all-start
  22.3 5.5 all-to-all-start.1
  41.1 6.5 %all-to-all-start.2 = ((bf16[4,144,1152]{2,1,0:T(8,128)(2,1)}), bf16[4,144,1152]{2,1,0:T(8,128)(2,1)}, u32[]{:S(2)}, u32[]{:S(2)}) async-start(bf16[4,144,1152]{2,1,0:T(8,128)(2,1)} %broadcast_in_dim.49), calls=%async_computation.2 | async-start | bytes 2654208 | tf_op jit(solution)/shard_map/all_to_all | solution.py:96
  54.3 4.3 collective-permute-start.5
  59.1 15.2 %collective-permute-done.7.refs_5_ = bf16[2,2,144,864]{3,2,1,0:T(8,128)(2,1)} collective-permute-done((bf16[2,2,144,864]{3,2,1,0:T(8,128)(2,1)}, bf16[2,2,144,864]{3,2,1,0:T(8,128)(2,1)}, u32[]{:S(2)}, u32[]{:S(2)}) %collective-permute-start.7) | collective-permute-done | bytes 995360 | tf_op jit(solution)/shard_map/ppermute | solution.py:101
  74.3 3.0 collective-permute-done.6.refs_1_
  79.3 17.2 %collective-permute-done.5.others = bf16[512,1152]{1,0:T(8,128)(2,1)} collective-permute-done((bf16[512,1152]{1,0:T(8,128)(2,1)}, bf16[512,1152]{1,0:T(8,128)(2,1)}, u32[]{:S(2)}, u32[]{:S(2)}) %collective-permute-start.5) | collective-permute-done | bytes 1179680 | tf_op jit(solution)/shard_map/ppermute | solution.py:111
  96.5 5.8 %first.1 = (bf16[2,512,1152]{2,1,0:T(8,128)(2,1)}, bf16[576,1024]{1,0:T(8,128)(2,1)}, bf16[576,1024]{1,0:T(8,128)(2,1)}) custom-call(s32[2]{0:T(128)} %pad_add_fusion.where, bf16[512,1152]{1,0:T(8,128)(2,1)} %tokens.5, bf16[512,1152]{1,0:T(8,128)(2,1)} %collective-permute-done.5.others, f32[6,1152]{1,0:T(8,128)} %reshape.181.mods), custom_call_target="tpu_custom_call" | custom-call | flops 6900000 | bytes 1024 | tf_op jit(solution)/shard_map/first/pallas_call | solution.py:484
  103.1 4.6 all-to-all-start.3
  114.0 7.6 %assemble.4 = bf16[4,8,144,864]{3,2,1,0:T(8,128)(2,1)} custom-call(s32[2]{0:T(128)} %pad_add_fusion.where, bf16[2,2,144,864]{3,2,1,0:T(8,128)(2,1)} %pad_maximum_fusion.4.refs_0_, bf16[2,2,144,864]{3,2,1,0:T(8,128)(2,1)} %collective-permute-done.6.refs_1_, bf16[2,2,144,864]{3,2,1,0:T(8,128)(2,1)} %collective-permute-done.8.refs_2_, ...), custom_call_target="tpu_custom_call" | custom-call | flops 10005000 | bytes 1024 | tf_op jit(solution)/shard_map/assemble/pallas_call | solution.py:256
  123.1 16.2 %convolution_convert_fusion = bf16[4,864,1024]{2,1,0:T(8,128)(2,1)} fusion(bf16[4,1152,864]{2,1,0:T(8,128)(2,1)} %bitcast.157, bf16[1024,1152,1]{1,0,2:T(8,128)(2,1)} %bitcast.182), kind=kOutput, calls=%fused_computation | convolution fusion | flops 8157265920 | bytes 17399808 | tf_op jit(solution)/shard_map/tdc,rd->tcr/dot_general | solution.py:1316
  143.9 5.6 %all-to-all-start.4 = ((bf16[4,144,1152]{2,1,0:T(8,128)(2,1)}), bf16[4,144,1152]{2,1,0:T(8,128)(2,1)S(1)}, u32[]{:S(2)}, u32[]{:S(2)}) async-start(bf16[4,144,1152]{2,1,0:T(8,128)(2,1)} %broadcast_in_dim.54), calls=%async_computation.4 | async-start | bytes 2654208 | tf_op jit(solution)/shard_map/all_to_all | solution.py:96
  153.5 10.6 %attend.2 = (bf16[8,80,512]{2,1,0:T(8,128)(2,1)}, f32[8,1,512]{2,1,0:T(1,128)}) custom-call(bf16[4,12,72,1024]{3,2,1,0:T(8,128)(2,1)} %bitcast.133, bf16[4,12,72,1024]{3,2,1,0:T(8,128)(2,1)} %bitcast.134, bf16[4,12,72,1024]{3,2,1,0:T(8,128)(2,1)} %bitcast.135, bf16[4,12,72,1024]{3,2,1,0:T(8,128)(2,1)} %bitcast.136, bf16[4,12,72,1024]{3,2,1,0:T(8,128)(2,1)} %bitcast.137), custom_call_target="tpu_custom_call" | custom-call | flops 12190000 | bytes 1024 | tf_op jit(solution)/shard_map/attend/pallas_call | solution.py:349
  167.6 3.0 collective-permute-done.17.refs_6_
  172.5 11.0 %attend.3 = (bf16[8,80,512]{2,1,0:T(8,128)(2,1)}, f32[8,1,512]{2,1,0:T(1,128)}) custom-call(bf16[4,12,72,1024]{3,2,1,0:T(8,128)(2,1)} %bitcast.138, bf16[4,12,72,1024]{3,2,1,0:T(8,128)(2,1)} %bitcast.139, bf16[4,12,72,1024]{3,2,1,0:T(8,128)(2,1)} %bitcast.140, bf16[4,12,72,1024]{3,2,1,0:T(8,128)(2,1)} %bitcast.141, bf16[4,12,72,1024]{3,2,1,0:T(8,128)(2,1)} %bitcast.142), custom_call_target="tpu_custom_call" | custom-call | flops 12190000 | bytes 1024 | tf_op jit(solution)/shard_map/attend/pallas_call | solution.py:349
  185.6 4.0 assemble.5
  189.6 7.9 %middle.1 = (f32[512,1152]{1,0:T(8,128)}, f32[512,1152]{1,0:T(8,128)}, bf16[512,1152]{1,0:T(8,128)(2,1)}, bf16[576,512]{1,0:T(8,128)(2,1)}, bf16[576,512]{1,0:T(8,128)(2,1)}) custom-call(s32[2]{0:T(128)} %pad_add_fusion.where, bf16[8,80,512]{2,1,0:T(8,128)(2,1)} %get-tuple-element.156.one, bf16[8,80,512]{2,1,0:T(8,128)(2,1)} %get-tuple-element.159.two, ...), custom_call_target="tpu_custom_call" | custom-call | flops 9200000 | bytes 1024 | tf_op jit(solution)/shard_map/middle/pallas_call | solution.py:484
  203.0 8.7 %assemble.6 = bf16[4,8,144,1152]{3,2,1,0:T(8,128)(2,1)} custom-call(s32[2]{0:T(128)} %pad_add_fusion.where, bf16[2,2,144,1152]{3,2,1,0:T(8,128)(2,1)} %constant_dynamic-update-slice_fusion.refs_0_, bf16[2,2,144,1152]{3,2,1,0:T(8,128)(2,1)} %collective-permute-done.19.refs_1_, bf16[2,2,144,1152]{3,2,1,0:T(8,128)(2,1)} %copy-done.32, ...), custom_call_target="tpu_custom_call" | custom-call | flops 10005000 | bytes 1024 | tf_op jit(solution)/shard_map/assemble/pallas_call | solution.py:256
  211.6 3.6 collective-permute-done.22
  218.7 14.8 %up.1 = (bf16[4,512,1152]{2,1,0:T(8,128)(2,1)}, bf16[4,512,1152]{2,1,0:T(8,128)(2,1)}, bf16[4,576,512]{2,1,0:T(8,128)(2,1)}, bf16[4,576,512]{2,1,0:T(8,128)(2,1)}) custom-call(s32[2]{0:T(128)} %pad_add_fusion.where, bf16[512,1152]{1,0:T(8,128)(2,1)} %get-tuple-element.171.h, bf16[4,1152,1152]{2,1,0:T(8,128)(2,1)} %bitcast.155), custom_call_target="tpu_custom_call" | custom-call | flops 17250000 | bytes 1024 | tf_op jit(solution)/shard_map/up/pallas_call | solution.py:484
  233.6 13.0 %collective-permute-done.26.refs_5_ = bf16[2,2,144,1152]{3,2,1,0:T(8,128)(2,1)} collective-permute-done((bf16[2,2,144,1152]{3,2,1,0:T(8,128)(2,1)S(1)}, bf16[2,2,144,1152]{3,2,1,0:T(8,128)(2,1)}, u32[]{:S(2)}, u32[]{:S(2)}) %collective-permute-start.26) | collective-permute-done | bytes 1327136 | tf_op jit(solution)/shard_map/ppermute | solution.py:101
  250.1 6.1 %collective-permute-done.28.refs_6_ = bf16[2,2,144,1152]{3,2,1,0:T(8,128)(2,1)S(1)} collective-permute-done((bf16[2,2,144,1152]{3,2,1,0:T(8,128)(2,1)S(1)}, bf16[2,2,144,1152]{3,2,1,0:T(8,128)(2,1)S(1)}, u32[]{:S(2)}, u32[]{:S(2)}) %collective-permute-start.28) | collective-permute-done | bytes 1327136 | tf_op jit(solution)/shard_map/ppermute | solution.py:101
  258.1 3.4 collective-permute-done.30.refs_3_
  263.9 11.1 %weight_grads.4 = (bf16[2,2,144,1152]{3,2,1,0:T(8,128)(2,1)}, bf16[2,2,144,1152]{3,2,1,0:T(8,128)(2,1)}, bf16[2,2,144,1152]{3,2,1,0:T(8,128)(2,1)}, bf16[2,2,144,1152]{3,2,1,0:T(8,128)(2,1)}) custom-call(bf16[4,576,512]{2,1,0:T(8,128)(2,1)} %get-tuple-element.176.refs_0_, bf16[4,576,512]{2,1,0:T(8,128)(2,1)} %copy-done.13, bf16[512,1152]{1,0:T(8,128)(2,1)} %copy-done.3, ...), custom_call_target="tpu_custom_call" | custom-call | flops 12650000 | bytes 1024 | tf_op jit(solution)/shard_map/weight_grads/pallas_call | solution.py:484
  278.0 8.7 %assemble.7 = bf16[4,8,144,1152]{3,2,1,0:T(8,128)(2,1)} custom-call(s32[2]{0:T(128)} %pad_add_fusion.where, bf16[2,2,144,1152]{3,2,1,0:T(8,128)(2,1)} %copy-done.9, bf16[2,2,144,1152]{3,2,1,0:T(8,128)(2,1)} %collective-permute-done.25.refs_1_, bf16[2,2,144,1152]{3,2,1,0:T(8,128)(2,1)} %copy-done.34, ...), custom_call_target="tpu_custom_call" | custom-call | flops 10005000 | bytes 1024 | tf_op jit(solution)/shard_map/assemble/pallas_call | solution.py:256
  286.7 12.0 %down_back.1.gz.refs_2_ = bf16[4,512,1152]{2,1,0:T(8,128)(2,1)} custom-call(bf16[512,1152]{1,0:T(8,128)(2,1)} %copy-done.3, bf16[4,1152,1152]{2,1,0:T(8,128)(2,1)} %bitcast.153, bf16[4,512,1152]{2,1,0:T(8,128)(2,1)} %get-tuple-element.183.slope), custom_call_target="tpu_custom_call" | custom-call | flops 13800000 | bytes 1024 | tf_op jit(solution)/shard_map/down_back/pallas_call | solution.py:484
  298.7 16.1 %up_back.1 = (f32[512,1152]{1,0:T(8,128)}, bf16[512,1152]{1,0:T(8,128)(2,1)}, f32[8,1152]{1,0:T(8,128)}) custom-call(bf16[4,512,1152]{2,1,0:T(8,128)(2,1)} %down_back.1.gz.refs_2_, bf16[4,1152,1152]{2,1,0:T(8,128)(2,1)} %bitcast.156, f32[512,1152]{1,0:T(8,128)} %get-tuple-element.184.middle, bf16[512,1152]{1,0:T(8,128)(2,1)} %grad.3, ...), custom_call_target="tpu_custom_call" | custom-call | flops 18400000 | bytes 1024 | tf_op jit(solution)/shard_map/up_back/pallas_call | solution.py:484
  320.8 8.7 %out_back.1 = (bf16[16,80,512]{2,1,0:T(8,128)(2,1)}, bf16[4,4,80,576]{3,2,1,0:T(8,128)(2,1)}, bf16[4,4,80,576]{3,2,1,0:T(8,128)(2,1)}) custom-call(s32[2]{0:T(128)} %pad_add_fusion.where, bf16[8,80,512]{2,1,0:T(8,128)(2,1)} %get-tuple-element.156.one, bf16[8,80,512]{2,1,0:T(8,128)(2,1)} %get-tuple-element.159.two, bf16[2,1280,576]{2,1,0:T(8,128)(2,1)} %bitcast.166, ...), custom_call_target="tpu_custom_call" | custom-call | flops 10350000 | bytes 1024 | tf_op jit(solution)/shard_map/out_back/pallas_call | solution.py:484
  330.4 11.3 %weight_grads.5 = (bf16[2,2,144,1152]{3,2,1,0:T(8,128)(2,1)}, bf16[2,2,144,1152]{3,2,1,0:T(8,128)(2,1)}, bf16[2,2,144,1152]{3,2,1,0:T(8,128)(2,1)}, bf16[2,2,144,1152]{3,2,1,0:T(8,128)(2,1)}) custom-call(bf16[576,512]{1,0:T(8,128)(2,1)} %get-tuple-element.194.refs_0_, bf16[576,512]{1,0:T(8,128)(2,1)} %copy-done.39, ...), custom_call_target="tpu_custom_call" | custom-call | flops 12650000 | bytes 1024 | tf_op jit(solution)/shard_map/weight_grads/pallas_call | solution.py:484
  345.0 5.4 all-to-all-start.5
  356.6 16.5 %attend_back.2 = bf16[2,3,4,72,1024]{4,3,2,1,0:T(8,128)(2,1)} custom-call(bf16[4,12,72,1024]{3,2,1,0:T(8,128)(2,1)} %bitcast.143, bf16[4,12,72,1024]{3,2,1,0:T(8,128)(2,1)} %bitcast.144, bf16[4,12,72,1024]{3,2,1,0:T(8,128)(2,1)} %bitcast.145, bf16[4,12,72,1024]{3,2,1,0:T(8,128)(2,1)} %bitcast.146, bf16[4,12,72,1024]{3,2,1,0:T(8,128)(2,1)} %bitcast.147, ...), custom_call_target="tpu_custom_call" | custom-call | flops 19090000 | bytes 1024 | tf_op jit(solution)/shard_map/attend_back/pallas_call | solution.py:400
  373.4 17.1 %attend_back.3 = bf16[2,3,4,72,1024]{4,3,2,1,0:T(8,128)(2,1)} custom-call(bf16[4,12,72,1024]{3,2,1,0:T(8,128)(2,1)} %bitcast.148, bf16[4,12,72,1024]{3,2,1,0:T(8,128)(2,1)} %bitcast.149, bf16[4,12,72,1024]{3,2,1,0:T(8,128)(2,1)} %bitcast.150, bf16[4,12,72,1024]{3,2,1,0:T(8,128)(2,1)} %bitcast.151, bf16[4,12,72,1024]{3,2,1,0:T(8,128)(2,1)} %bitcast.152, ...), custom_call_target="tpu_custom_call" | custom-call | flops 19090000 | bytes 1024 | tf_op jit(solution)/shard_map/attend_back/pallas_call | solution.py:400
  399.0 16.0 %qkv_back.1 = (f32[512,1152]{1,0:T(8,128)}, bf16[512,1152]{1,0:T(8,128)(2,1)}) custom-call(bf16[2,864,1024]{2,1,0:T(8,128)(2,1)} %bitcast.163, bf16[2,864,1024]{2,1,0:T(8,128)(2,1)} %bitcast.159, bf16[4,1152,864]{2,1,0:T(8,128)(2,1)} %bitcast.158), custom_call_target="tpu_custom_call" | custom-call | flops 18400000 | bytes 1024 | tf_op jit(solution)/shard_map/qkv_back/pallas_call | solution.py:484
  422.3 9.6 %weight_grads.6 = (bf16[2,2,144,864]{3,2,1,0:T(8,128)(2,1)}, bf16[2,2,144,864]{3,2,1,0:T(8,128)(2,1)}) custom-call(bf16[576,1024]{1,0:T(8,128)(2,1)} %get-tuple-element.219.refs_0_, bf16[576,1024]{1,0:T(8,128)(2,1)} %copy-done.5, bf16[2,864,1024]{2,1,0:T(8,128)(2,1)} %bitcast.164, bf16[2,864,1024]{2,1,0:T(8,128)(2,1)} %collective-permute-done.45.refs_3_), custom_call_target="tpu_custom_call" | custom-call | flops 12650000 | bytes 1024 | tf_op jit(solution)/shard_map/weight_grads/pallas_call | solution.py:484
  435.6 9.2 %weight_grads.7 = (bf16[2,2,144,864]{3,2,1,0:T(8,128)(2,1)}, bf16[2,2,144,864]{3,2,1,0:T(8,128)(2,1)}) custom-call(bf16[576,1024]{1,0:T(8,128)(2,1)} %get-tuple-element.219.refs_0_, bf16[576,1024]{1,0:T(8,128)(2,1)} %copy-done.5, bf16[2,864,1024]{2,1,0:T(8,128)(2,1)} %bitcast.160, bf16[2,864,1024]{2,1,0:T(8,128)(2,1)} %collective-permute-done.46.refs_3_), custom_call_target="tpu_custom_call" | custom-call | flops 12650000 | bytes 1024 | tf_op jit(solution)/shard_map/weight_grads/pallas_call | solution.py:484
  454.8 5.8 %last.1 = (f32[512,1152]{1,0:T(8,128)}, f32[8,1152]{1,0:T(8,128)}) custom-call(f32[512,1152]{1,0:T(8,128)} %get-tuple-element.227.own, bf16[512,1152]{1,0:T(8,128)(2,1)} %collective-permute-done.47.far, bf16[512,1152]{1,0:T(8,128)(2,1)} %tokens.5, f32[512,1152]{1,0:T(8,128)} %get-tuple-element.230.gx, f32[6,1152]{1,0:T(8,128)} %reshape.181.mods), custom_call_target="tpu_custom_call" | custom-call | flops 6900000 | bytes 1024 | tf_op jit(solution)/shard_map/last/pallas_call | solution.py:484
  460.6 13.0 %down.1 = (bf16[512,1152]{1,0:T(8,128)(2,1)}, f32[8,1152]{1,0:T(8,128)}) custom-call(bf16[4,512,1152]{2,1,0:T(8,128)(2,1)} %get-tuple-element.232.u, bf16[4,1152,1152]{2,1,0:T(8,128)(2,1)} %bitcast.154, f32[512,1152]{1,0:T(8,128)} %get-tuple-element.184.middle, bf16[512,1152]{1,0:T(8,128)(2,1)} %grad.3, f32[6,1152]{1,0:T(8,128)} %reshape.181.mods), custom_call_target="tpu_custom_call" | custom-call | flops 14950000 | bytes 1024 | tf_op jit(solution)/shard_map/down/pallas_call | solution.py:484
  486.6 3.9 all-to-all-start.6
  492.5 7.8 %all-to-all-done.6 = f32[32,1,1728]{2,1,0:T(1,128)S(1)} async-done(((f32[32,1,1728]{2,1,0:T(1,128)}), f32[32,1,1728]{2,1,0:T(1,128)S(1)}, u32[]{:S(2)}, u32[]{:S(2)}) %all-to-all-start.6) | async-done | bytes 221216 | tf_op jit(solution)/shard_map/all_to_all | solution.py:96
  506.3 3.6 all-to-all-start.7
  509.9 3.0 collective-permute-start.55
  519.3 5.8 %step.5 = (f32[144,72,72]{2,1,0:T(8,128)}, f32[144,72,72]{2,1,0:T(8,128)}, f32[2,144,72,72]{3,2,1,0:T(8,128)}) custom-call(bf16[4,144,1152]{2,1,0:T(8,128)(2,1)} %copy-done.4, f32[144,72,72]{2,1,0:T(8,128)} %master_ref.9, f32[144,72,72]{2,1,0:T(8,128)} %moment_ref.9, f32[2,144,72,72]{3,2,1,0:T(8,128)} %stats_ref.9, f32[2,144,72,72]{3,2,1,0:T(8,128)} %roots_ref.9), custom_call_target="tpu_custom_call" | custom-call | flops 6900000 | bytes 1024 | tf_op jit(solution)/shard_map/step/pallas_call | solution.py:452
  525.0 5.8 %step.6 = (f32[144,72,72]{2,1,0:T(8,128)}, f32[144,72,72]{2,1,0:T(8,128)}, f32[2,144,72,72]{3,2,1,0:T(8,128)}) custom-call(bf16[4,144,1152]{2,1,0:T(8,128)(2,1)} %pad_maximum_fusion.3.grads_ref, f32[144,72,72]{2,1,0:T(8,128)} %master_ref.9, f32[144,72,72]{2,1,0:T(8,128)} %moment_ref.9, ...), custom_call_target="tpu_custom_call", output_to_operand_aliasing={{0}: (5, {}), {1}: (6, {}), {2}: (7, {})} | custom-call | flops 6900000 | bytes 1024 | tf_op jit(solution)/shard_map/step/pallas_call | solution.py:452
  530.8 7.2 %step.7 = (f32[144,72,72]{2,1,0:T(8,128)}, f32[144,72,72]{2,1,0:T(8,128)}, f32[2,144,72,72]{3,2,1,0:T(8,128)}) custom-call(f32[1,144,1728]{2,1,0:T(8,128)} %bitcast.169, f32[144,72,72]{2,1,0:T(8,128)} %master_ref.9, f32[144,72,72]{2,1,0:T(8,128)} %moment_ref.9, ...), custom_call_target="tpu_custom_call", output_to_operand_aliasing={{0}: (5, {}), {1}: (6, {}), {2}: (7, {})} | custom-call | flops 6900000 | bytes 1024 | tf_op jit(solution)/shard_map/step/pallas_call | solution.py:452
  542.6 3.1 step.8
  545.7 4.9 step.9
  (307 shorter events, 156.1 us)
Async XLA Ops:
  4.8 23.0 %collective-permute-start.2 = (bf16[144,864]{1,0:T(8,128)(2,1)}, bf16[144,864]{1,0:T(8,128)(2,1)}, u32[]{:S(2)}, u32[]{:S(2)}) collective-permute-start(bf16[144,864]{1,0:T(8,128)(2,1)} %reshape.173), channel_id=1, source_target_pairs={{0,2},{1,3},{2,0},{3,1},{4,6},{5,7},{6,4},{7,5},{8,10},{9,11},{10,... | collective-permute-start | bytes 746504 | tf_op jit(solution)/shard_map/ppermute | solution.py:120
  8.8 19.0 %collective-permute-start.3 = (bf16[144,864]{1,0:T(8,128)(2,1)}, bf16[144,864]{1,0:T(8,128)(2,1)}, u32[]{:S(2)}, u32[]{:S(2)}) collective-permute-start(bf16[144,864]{1,0:T(8,128)(2,1)} %reshape.173), channel_id=1, source_target_pairs={{0,3},{1,0},{2,1},{3,2},{4,7},{5,4},{6,5},{7,6},{8,11},{9,8},{10,9... | collective-permute-start | bytes 746504 | tf_op jit(solution)/shard_map/ppermute | solution.py:120
  41.1 61.2 %all-to-all-start.2 = ((bf16[4,144,1152]{2,1,0:T(8,128)(2,1)}), bf16[4,144,1152]{2,1,0:T(8,128)(2,1)}, u32[]{:S(2)}, u32[]{:S(2)}) async-start(bf16[4,144,1152]{2,1,0:T(8,128)(2,1)} %broadcast_in_dim.49), calls=%async_computation.2 | async-start | bytes 2654208 | tf_op jit(solution)/shard_map/all_to_all | solution.py:96
  49.9 24.4 %collective-permute-start.7 = (bf16[2,2,144,864]{3,2,1,0:T(8,128)(2,1)}, bf16[2,2,144,864]{3,2,1,0:T(8,128)(2,1)}, u32[]{:S(2)}, u32[]{:S(2)}) collective-permute-start(bf16[2,2,144,864]{3,2,1,0:T(8,128)(2,1)} %pad_maximum_fusion.5.refs_4_), channel_id=1, source_target_pairs={{0,8},{4,12},{8,0},{12,4},{16,24},{20,28},{24,16},{28,20},{1,9},{5... | collective-permute-start | bytes 2985992 | tf_op jit(solution)/shard_map/ppermute | solution.py:101
  53.3 24.0 %collective-permute-start.6 = (bf16[2,2,144,864]{3,2,1,0:T(8,128)(2,1)}, bf16[2,2,144,864]{3,2,1,0:T(8,128)(2,1)}, u32[]{:S(2)}, u32[]{:S(2)}) collective-permute-start(bf16[2,2,144,864]{3,2,1,0:T(8,128)(2,1)} %pad_maximum_fusion.4.refs_0_), channel_id=1, source_target_pairs={{0,16},{4,20},{8,24},{12,28},{16,0},{20,4},{24,8},{28,12},{1,17},{... | collective-permute-start | bytes 2985992 | tf_op jit(solution)/shard_map/ppermute | solution.py:101
  54.3 42.2 %collective-permute-start.5 = (bf16[512,1152]{1,0:T(8,128)(2,1)}, bf16[512,1152]{1,0:T(8,128)(2,1)}, u32[]{:S(2)}, u32[]{:S(2)}) collective-permute-start(bf16[512,1152]{1,0:T(8,128)(2,1)} %tokens.5), channel_id=1, source_target_pairs={{0,1},{1,0},{2,3},{3,2},{4,5},{5,4},{6,7},{7,6},{8,9},{9,8},{10,11... | collective-permute-start | bytes 3538952 | tf_op jit(solution)/shard_map/ppermute | solution.py:111
  58.6 54.9 %collective-permute-start.10 = (bf16[2,2,144,864]{3,2,1,0:T(8,128)(2,1)}, bf16[2,2,144,864]{3,2,1,0:T(8,128)(2,1)}, u32[]{:S(2)}, u32[]{:S(2)}) collective-permute-start(bf16[2,2,144,864]{3,2,1,0:T(8,128)(2,1)} %pad_maximum_fusion.5.refs_4_), channel_id=1, source_target_pairs={{0,4},{4,0},{8,12},{12,8},{16,20},{20,16},{24,28},{28,24},{1,5},{5... | collective-permute-start | bytes 2985992 | tf_op jit(solution)/shard_map/ppermute | solution.py:101
  58.6 55.4 %collective-permute-start.8 = (bf16[2,2,144,864]{3,2,1,0:T(8,128)(2,1)}, bf16[2,2,144,864]{3,2,1,0:T(8,128)(2,1)}, u32[]{:S(2)}, u32[]{:S(2)}) collective-permute-start(bf16[2,2,144,864]{3,2,1,0:T(8,128)(2,1)} %pad_maximum_fusion.4.refs_0_), channel_id=1, source_target_pairs={{0,4},{4,0},{8,12},{12,8},{16,20},{20,16},{24,28},{28,24},{1,5},{5... | collective-permute-start | bytes 2985992 | tf_op jit(solution)/shard_map/ppermute | solution.py:101
  77.3 36.7 %collective-permute-start.11 = (bf16[2,2,144,864]{3,2,1,0:T(8,128)(2,1)}, bf16[2,2,144,864]{3,2,1,0:T(8,128)(2,1)}, u32[]{:S(2)}, u32[]{:S(2)}) collective-permute-start(bf16[2,2,144,864]{3,2,1,0:T(8,128)(2,1)} %collective-permute-done.7.refs_5_), channel_id=1, source_target_pairs={{0,4},{4,0},{8,12},{12,8},{16,20},{20,16},{24,28},{28,24},{1,5},{5... | collective-permute-start | bytes 2985992 | tf_op jit(solution)/shard_map/ppermute | solution.py:101
  77.3 36.7 %collective-permute-start.9 = (bf16[2,2,144,864]{3,2,1,0:T(8,128)(2,1)}, bf16[2,2,144,864]{3,2,1,0:T(8,128)(2,1)}, u32[]{:S(2)}, u32[]{:S(2)}) collective-permute-start(bf16[2,2,144,864]{3,2,1,0:T(8,128)(2,1)} %collective-permute-done.6.refs_1_), channel_id=1, source_target_pairs={{0,4},{4,0},{8,12},{12,8},{16,20},{20,16},{24,28},{28,24},{1,5},{5... | collective-permute-start | bytes 2985992 | tf_op jit(solution)/shard_map/ppermute | solution.py:101
  103.1 18.5 %all-to-all-start.3 = ((bf16[4,80,576]{2,1,0:T(8,128)(2,1)}), bf16[4,80,576]{2,1,0:T(8,128)(2,1)S(1)}, u32[]{:S(2)}, u32[]{:S(2)}) async-start(bf16[4,80,576]{2,1,0:T(8,128)(2,1)} %broadcast_in_dim.52), calls=%async_computation.3 | async-start | bytes 819200 | tf_op jit(solution)/shard_map/all_to_all | solution.py:96
  109.9 39.6 %collective-permute-start.13 = (bf16[1,2,144,1152]{3,2,1,0:T(8,128)(2,1)}, bf16[1,2,144,1152]{3,2,1,0:T(8,128)(2,1)}, u32[]{:S(2)}, u32[]{:S(2)}) collective-permute-start(bf16[1,2,144,1152]{3,2,1,0:T(8,128)(2,1)} %get-tuple-element.147), channel_id=1, source_target_pairs={{0,16},{4,20},{8,24},{12,28},{16,0},{20,4},{24,8},{28,12},{1,17},{... | collective-permute-start | bytes 1990664 | tf_op jit(solution)/shard_map/ppermute | solution.py:101
  113.5 36.0 %collective-permute-start.12 = (bf16[1,2,144,1152]{3,2,1,0:T(8,128)(2,1)S(1)}, bf16[1,2,144,1152]{3,2,1,0:T(8,128)(2,1)}, u32[]{:S(2)}, u32[]{:S(2)}) collective-permute-start(bf16[1,2,144,1152]{3,2,1,0:T(8,128)(2,1)S(1)} %get-tuple-element.146), channel_id=1, source_target_pairs={{0,8},{4,12},{8,0},{12,4},{16,24},{20,28},{24,16},{28,20},{1,9},{5... | collective-permute-start | bytes 1990664 | tf_op jit(solution)/shard_map/ppermute | solution.py:101
  121.6 18.7 %collective-permute-start.14 = (bf16[1,4,80,576]{3,2,1,0:T(8,128)(2,1)S(1)}, bf16[1,4,80,576]{3,2,1,0:T(8,128)(2,1)S(1)}, u32[]{:S(2)}, u32[]{:S(2)}) collective-permute-start(bf16[1,4,80,576]{3,2,1,0:T(8,128)(2,1)S(1)} %bitcast.170), channel_id=1, source_target_pairs={{0,8},{4,12},{8,0},{12,4},{16,24},{20,28},{24,16},{28,20},{1,9},{5... | collective-permute-start | bytes 1105928 | tf_op jit(solution)/shard_map/ppermute | solution.py:101
  141.3 22.8 %collective-permute-start.15 = (bf16[2,4,80,576]{3,2,1,0:T(8,128)(2,1)}, bf16[2,4,80,576]{3,2,1,0:T(8,128)(2,1)S(1)}, u32[]{:S(2)}, u32[]{:S(2)}) collective-permute-start(bf16[2,4,80,576]{3,2,1,0:T(8,128)(2,1)} %get-tuple-element.289), channel_id=1, source_target_pairs={{0,16},{4,20},{8,24},{12,28},{16,0},{20,4},{24,8},{28,12},{1,17},{... | collective-permute-start | bytes 2211848 | tf_op jit(solution)/shard_map/ppermute | solution.py:101
  143.9 41.7 %all-to-all-start.4 = ((bf16[4,144,1152]{2,1,0:T(8,128)(2,1)}), bf16[4,144,1152]{2,1,0:T(8,128)(2,1)S(1)}, u32[]{:S(2)}, u32[]{:S(2)}) async-start(bf16[4,144,1152]{2,1,0:T(8,128)(2,1)} %broadcast_in_dim.54), calls=%async_computation.4 | async-start | bytes 2654208 | tf_op jit(solution)/shard_map/all_to_all | solution.py:96
  165.0 18.6 %collective-permute-start.18 = (bf16[4,4,80,576]{3,2,1,0:T(8,128)(2,1)}, bf16[4,4,80,576]{3,2,1,0:T(8,128)(2,1)S(1)}, u32[]{:S(2)}, u32[]{:S(2)}) collective-permute-start(bf16[4,4,80,576]{3,2,1,0:T(8,128)(2,1)} %constant_dynamic-update-slice_fusion.6), channel_id=1, source_target_pairs={{0,4},{4,0},{8,12},{12,8},{16,20},{20,16},{24,28},{28,24},{1,5},{5... | collective-permute-start | bytes 4423688 | tf_op jit(solution)/shard_map/ppermute | solution.py:101
  165.5 32.0 %collective-permute-start.20 = (bf16[2,2,144,1152]{3,2,1,0:T(8,128)(2,1)}, bf16[2,2,144,1152]{3,2,1,0:T(8,128)(2,1)}, u32[]{:S(2)}, u32[]{:S(2)}) collective-permute-start(bf16[2,2,144,1152]{3,2,1,0:T(8,128)(2,1)} %constant_dynamic-update-slice_fusion.2.refs_4_), channel_id=1, source_target_pairs={{0,8},{4,12},{8,0},{12,4},{16,24},{20,28},{24,16},{28,20},{1,9},{5... | collective-permute-start | bytes 3981320 | tf_op jit(solution)/shard_map/ppermute | solution.py:101
  166.1 31.6 %collective-permute-start.19 = (bf16[2,2,144,1152]{3,2,1,0:T(8,128)(2,1)}, bf16[2,2,144,1152]{3,2,1,0:T(8,128)(2,1)}, u32[]{:S(2)}, u32[]{:S(2)}) collective-permute-start(bf16[2,2,144,1152]{3,2,1,0:T(8,128)(2,1)} %constant_dynamic-update-slice_fusion.refs_0_), channel_id=1, source_target_pairs={{0,16},{4,20},{8,24},{12,28},{16,0},{20,4},{24,8},{28,12},{1,17},{... | collective-permute-start | bytes 3981320 | tf_op jit(solution)/shard_map/ppermute | solution.py:101
  216.5 30.1 %collective-permute-start.26 = (bf16[2,2,144,1152]{3,2,1,0:T(8,128)(2,1)S(1)}, bf16[2,2,144,1152]{3,2,1,0:T(8,128)(2,1)}, u32[]{:S(2)}, u32[]{:S(2)}) collective-permute-start(bf16[2,2,144,1152]{3,2,1,0:T(8,128)(2,1)S(1)} %constant_dynamic-update-slice_fusion.11.refs_4_), channel_id=1, source_target_pairs={{0,8},{4,12},{8,0},{12,4},{16,24},{20,28},{24,16},{28,20},{1,9},{5... | collective-permute-start | bytes 3981320 | tf_op jit(solution)/shard_map/ppermute | solution.py:101
  218.1 29.8 %collective-permute-start.25 = (bf16[2,2,144,1152]{3,2,1,0:T(8,128)(2,1)S(1)}, bf16[2,2,144,1152]{3,2,1,0:T(8,128)(2,1)}, u32[]{:S(2)}, u32[]{:S(2)}) collective-permute-start(bf16[2,2,144,1152]{3,2,1,0:T(8,128)(2,1)S(1)} %constant_dynamic-update-slice_fusion.9.refs_0_), channel_id=1, source_target_pairs={{0,16},{4,20},{8,24},{12,28},{16,0},{20,4},{24,8},{28,12},{1,17},{... | collective-permute-start | bytes 3981320 | tf_op jit(solution)/shard_map/ppermute | solution.py:101
  250.1 28.0 %collective-permute-start.31 = (bf16[2,2,144,1152]{3,2,1,0:T(8,128)(2,1)}, bf16[2,2,144,1152]{3,2,1,0:T(8,128)(2,1)}, u32[]{:S(2)}, u32[]{:S(2)}) collective-permute-start(bf16[2,2,144,1152]{3,2,1,0:T(8,128)(2,1)} %collective-permute-done.25.refs_1_), channel_id=1, source_target_pairs={{0,4},{4,0},{8,12},{12,8},{16,20},{20,16},{24,28},{28,24},{1,5},{5... | collective-permute-start | bytes 3981320 | tf_op jit(solution)/shard_map/ppermute | solution.py:101
  256.2 21.8 %collective-permute-start.32 = (bf16[2,2,144,1152]{3,2,1,0:T(8,128)(2,1)}, bf16[2,2,144,1152]{3,2,1,0:T(8,128)(2,1)}, u32[]{:S(2)}, u32[]{:S(2)}) collective-permute-start(bf16[2,2,144,1152]{3,2,1,0:T(8,128)(2,1)} %collective-permute-done.26.refs_5_), channel_id=1, source_target_pairs={{0,4},{4,0},{8,12},{12,8},{16,20},{20,16},{24,28},{28,24},{1,5},{5... | collective-permute-start | bytes 3981320 | tf_op jit(solution)/shard_map/ppermute | solution.py:101
  276.6 38.2 %collective-permute-start.33 = (bf16[2,2,144,1152]{3,2,0,1:T(8,128)(2,1)S(1)}, bf16[2,2,144,1152]{3,2,0,1:T(8,128)(2,1)}, u32[]{:S(2)}, u32[]{:S(2)}) collective-permute-start(bf16[2,2,144,1152]{3,2,0,1:T(8,128)(2,1)S(1)} %copy.142), channel_id=1, source_target_pairs={{0,16},{4,20},{8,24},{12,28},{16,0},{20,4},{24,8},{28,12},{1,17},{... | collective-permute-start | bytes 3981320 | tf_op jit(solution)/shard_map/ppermute | solution.py:101
  277.3 37.5 %collective-permute-start.34 = (bf16[2,2,144,1152]{3,2,0,1:T(8,128)(2,1)S(1)}, bf16[2,2,144,1152]{3,2,0,1:T(8,128)(2,1)}, u32[]{:S(2)}, u32[]{:S(2)}) collective-permute-start(bf16[2,2,144,1152]{3,2,0,1:T(8,128)(2,1)S(1)} %copy.143), channel_id=1, source_target_pairs={{0,8},{4,12},{8,0},{12,4},{16,24},{20,28},{24,16},{28,20},{1,9},{5... | collective-permute-start | bytes 3981320 | tf_op jit(solution)/shard_map/ppermute | solution.py:101
  317.9 23.8 %collective-permute-start.39 = (bf16[2,144,1152]{2,1,0:T(8,128)(2,1)S(1)}, bf16[2,144,1152]{2,1,0:T(8,128)(2,1)S(1)}, u32[]{:S(2)}, u32[]{:S(2)}) collective-permute-start(bf16[2,144,1152]{2,1,0:T(8,128)(2,1)S(1)} %fusion.8), channel_id=1, source_target_pairs={{0,16},{4,20},{8,24},{12,28},{16,0},{20,4},{24,8},{28,12},{1,17},{... | collective-permute-start | bytes 1990664 | tf_op jit(solution)/shard_map/ppermute | solution.py:101
  319.4 22.4 %collective-permute-start.38 = (bf16[2,144,1152]{2,1,0:T(8,128)(2,1)S(1)}, bf16[2,144,1152]{2,1,0:T(8,128)(2,1)}, u32[]{:S(2)}, u32[]{:S(2)}) collective-permute-start(bf16[2,144,1152]{2,1,0:T(8,128)(2,1)S(1)} %fusion.7), channel_id=1, source_target_pairs={{0,8},{4,12},{8,0},{12,4},{16,24},{20,28},{24,16},{28,20},{1,9},{5... | collective-permute-start | bytes 1990664 | tf_op jit(solution)/shard_map/ppermute | solution.py:101
  345.0 45.6 %all-to-all-start.5 = ((bf16[4,144,1152]{2,1,0:T(8,128)(2,1)}), bf16[4,144,1152]{2,1,0:T(8,128)(2,1)S(1)}, u32[]{:S(2)}, u32[]{:S(2)}) async-start(bf16[4,144,1152]{2,1,0:T(8,128)(2,1)} %pad_maximum_fusion.1), calls=%async_computation.5 | async-start | bytes 2654208 | tf_op jit(solution)/shard_map/all_to_all | solution.py:96
  351.8 38.7 %collective-permute-start.41 = (bf16[2,2,144,1152]{3,2,0,1:T(8,128)(2,1)S(1)}, bf16[2,2,144,1152]{3,2,0,1:T(8,128)(2,1)S(1)}, u32[]{:S(2)}, u32[]{:S(2)}) collective-permute-start(bf16[2,2,144,1152]{3,2,0,1:T(8,128)(2,1)S(1)} %copy.151), channel_id=1, source_target_pairs={{0,8},{4,12},{8,0},{12,4},{16,24},{20,28},{24,16},{28,20},{1,9},{5... | collective-permute-start | bytes 3981320 | tf_op jit(solution)/shard_map/ppermute | solution.py:101
  354.2 36.3 %collective-permute-start.40 = (bf16[2,2,144,1152]{3,2,0,1:T(8,128)(2,1)}, bf16[2,2,144,1152]{3,2,0,1:T(8,128)(2,1)}, u32[]{:S(2)}, u32[]{:S(2)}) collective-permute-start(bf16[2,2,144,1152]{3,2,0,1:T(8,128)(2,1)} %copy.150), channel_id=1, source_target_pairs={{0,16},{4,20},{8,24},{12,28},{16,0},{20,4},{24,8},{28,12},{1,17},{... | collective-permute-start | bytes 3981320 | tf_op jit(solution)/shard_map/ppermute | solution.py:101
  354.8 18.6 %collective-permute-start.42 = (bf16[576,1024]{1,0:T(8,128)(2,1)}, bf16[576,1024]{1,0:T(8,128)(2,1)S(1)}, u32[]{:S(2)}, u32[]{:S(2)}) collective-permute-start(bf16[576,1024]{1,0:T(8,128)(2,1)} %get-tuple-element.212), channel_id=1, source_target_pairs={{0,4},{4,0},{8,12},{12,8},{16,20},{20,16},{24,28},{28,24},{1,5},{5... | collective-permute-start | bytes 3538952 | tf_op jit(solution)/shard_map/ppermute | solution.py:101
  373.1 49.2 %collective-permute-start.45 = (bf16[2,864,1024]{2,1,0:T(8,128)(2,1)}, bf16[2,864,1024]{2,1,0:T(8,128)(2,1)}, u32[]{:S(2)}, u32[]{:S(2)}) collective-permute-start(bf16[2,864,1024]{2,1,0:T(8,128)(2,1)} %bitcast.162), channel_id=1, source_target_pairs={{0,4},{4,0},{8,12},{12,8},{16,20},{20,16},{24,28},{28,24},{1,5},{5... | collective-permute-start | bytes 10616840 | tf_op jit(solution)/shard_map/ppermute | solution.py:101
  396.5 39.0 %collective-permute-start.46 = (bf16[2,864,1024]{2,1,0:T(8,128)(2,1)S(1)}, bf16[2,864,1024]{2,1,0:T(8,128)(2,1)}, u32[]{:S(2)}, u32[]{:S(2)}) collective-permute-start(bf16[2,864,1024]{2,1,0:T(8,128)(2,1)S(1)} %bitcast.161), channel_id=1, source_target_pairs={{0,4},{4,0},{8,12},{12,8},{16,20},{20,16},{24,28},{28,24},{1,5},{5... | collective-permute-start | bytes 10616840 | tf_op jit(solution)/shard_map/ppermute | solution.py:101
  396.7 18.3 %collective-permute-start.44 = (bf16[2,144,1152]{2,1,0:T(8,128)(2,1)}, bf16[2,144,1152]{2,1,0:T(8,128)(2,1)S(1)}, u32[]{:S(2)}, u32[]{:S(2)}) collective-permute-start(bf16[2,144,1152]{2,1,0:T(8,128)(2,1)} %fusion.12), channel_id=1, source_target_pairs={{0,16},{4,20},{8,24},{12,28},{16,0},{20,4},{24,8},{28,12},{1,17},{... | collective-permute-start | bytes 1990664 | tf_op jit(solution)/shard_map/ppermute | solution.py:101
  418.8 29.5 %collective-permute-start.47 = (bf16[512,1152]{1,0:T(8,128)(2,1)}, bf16[512,1152]{1,0:T(8,128)(2,1)}, u32[]{:S(2)}, u32[]{:S(2)}) collective-permute-start(bf16[512,1152]{1,0:T(8,128)(2,1)} %get-tuple-element.229), channel_id=1, source_target_pairs={{0,1},{1,0},{2,3},{3,2},{4,5},{5,4},{6,7},{7,6},{8,9},{9,8},{10,11... | collective-permute-start | bytes 3538952 | tf_op jit(solution)/shard_map/ppermute | solution.py:111
  420.9 27.5 %collective-permute-start.50 = (bf16[4,2,80,576]{3,2,0,1:T(8,128)(2,1)}, bf16[4,2,80,576]{3,2,0,1:T(8,128)(2,1)}, u32[]{:S(2)}, u32[]{:S(2)}) collective-permute-start(bf16[4,2,80,576]{3,2,0,1:T(8,128)(2,1)} %get-tuple-element.239), channel_id=1, source_target_pairs={{0,16},{4,20},{8,24},{12,28},{16,0},{20,4},{24,8},{28,12},{1,17},{... | collective-permute-start | bytes 2211848 | tf_op jit(solution)/shard_map/ppermute | solution.py:101
  434.1 41.2 %collective-permute-start.48 = (bf16[2,2,144,864]{3,2,0,1:T(8,128)(2,1)}, bf16[2,2,144,864]{3,2,0,1:T(8,128)(2,1)}, u32[]{:S(2)}, u32[]{:S(2)}) collective-permute-start(bf16[2,2,144,864]{3,2,0,1:T(8,128)(2,1)} %copy.156), channel_id=1, source_target_pairs={{0,16},{4,20},{8,24},{12,28},{16,0},{20,4},{24,8},{28,12},{1,17},{... | collective-permute-start | bytes 2985992 | tf_op jit(solution)/shard_map/ppermute | solution.py:101
  447.1 32.8 %collective-permute-start.49 = (bf16[2,2,144,864]{3,2,0,1:T(8,128)(2,1)}, bf16[2,2,144,864]{3,2,0,1:T(8,128)(2,1)}, u32[]{:S(2)}, u32[]{:S(2)}) collective-permute-start(bf16[2,2,144,864]{3,2,0,1:T(8,128)(2,1)} %copy.157), channel_id=1, source_target_pairs={{0,8},{4,12},{8,0},{12,4},{16,24},{20,28},{24,16},{28,20},{1,9},{5... | collective-permute-start | bytes 2985992 | tf_op jit(solution)/shard_map/ppermute | solution.py:101
  449.7 30.2 %collective-permute-start.51 = (bf16[4,80,576]{2,1,0:T(8,128)(2,1)S(1)}, bf16[4,80,576]{2,1,0:T(8,128)(2,1)}, u32[]{:S(2)}, u32[]{:S(2)}) collective-permute-start(bf16[4,80,576]{2,1,0:T(8,128)(2,1)S(1)} %get-tuple-element.275), channel_id=1, source_target_pairs={{0,8},{4,12},{8,0},{12,4},{16,24},{20,28},{24,16},{28,20},{1,9},{5... | collective-permute-start | bytes 1105928 | tf_op jit(solution)/shard_map/ppermute | solution.py:101
  451.8 62.6 %collective-permute-start.57 = (bf16[144,1152]{1,0:T(8,128)(2,1)}, bf16[144,1152]{1,0:T(8,128)(2,1)}, u32[]{:S(2)}, u32[]{:S(2)}) collective-permute-start(bf16[144,1152]{1,0:T(8,128)(2,1)} %get-tuple-element.279), channel_id=1, source_target_pairs={{0,1},{1,2},{2,3},{3,0},{4,5},{5,6},{6,7},{7,4},{8,9},{9,10},{10,1... | collective-permute-start | bytes 995336 | tf_op jit(solution)/shard_map/ppermute | solution.py:120
  452.5 64.4 %collective-permute-start.58 = (bf16[144,1152]{1,0:T(8,128)(2,1)}, bf16[144,1152]{1,0:T(8,128)(2,1)}, u32[]{:S(2)}, u32[]{:S(2)}) collective-permute-start(bf16[144,1152]{1,0:T(8,128)(2,1)} %get-tuple-element.278), channel_id=1, source_target_pairs={{0,2},{1,3},{2,0},{3,1},{4,6},{5,7},{6,4},{7,5},{8,10},{9,11},{10,... | collective-permute-start | bytes 995336 | tf_op jit(solution)/shard_map/ppermute | solution.py:120
  475.4 41.5 %collective-permute-start.59 = (bf16[144,1152]{1,0:T(8,128)(2,1)}, bf16[144,1152]{1,0:T(8,128)(2,1)}, u32[]{:S(2)}, u32[]{:S(2)}) collective-permute-start(bf16[144,1152]{1,0:T(8,128)(2,1)} %get-tuple-element.277), channel_id=1, source_target_pairs={{0,3},{1,0},{2,1},{3,2},{4,7},{5,4},{6,5},{7,6},{8,11},{9,8},{10,9... | collective-permute-start | bytes 995336 | tf_op jit(solution)/shard_map/ppermute | solution.py:120
  483.9 19.6 %collective-permute-start.53 = (bf16[2,144,864]{2,1,0:T(8,128)(2,1)}, bf16[2,144,864]{2,1,0:T(8,128)(2,1)}, u32[]{:S(2)}, u32[]{:S(2)}) collective-permute-start(bf16[2,144,864]{2,1,0:T(8,128)(2,1)} %fusion.16), channel_id=1, source_target_pairs={{0,16},{4,20},{8,24},{12,28},{16,0},{20,4},{24,8},{28,12},{1,17},{... | collective-permute-start | bytes 1493000 | tf_op jit(solution)/shard_map/ppermute | solution.py:101
  484.4 19.0 %collective-permute-start.52 = (bf16[2,144,864]{2,1,0:T(8,128)(2,1)}, bf16[2,144,864]{2,1,0:T(8,128)(2,1)}, u32[]{:S(2)}, u32[]{:S(2)}) collective-permute-start(bf16[2,144,864]{2,1,0:T(8,128)(2,1)} %fusion.15), channel_id=1, source_target_pairs={{0,8},{4,12},{8,0},{12,4},{16,24},{20,28},{24,16},{28,20},{1,9},{5... | collective-permute-start | bytes 1493000 | tf_op jit(solution)/shard_map/ppermute | solution.py:101
  506.3 31.8 %all-to-all-start.7 = ((bf16[4,72,576]{2,1,0:T(8,128)(2,1)}), bf16[4,72,576]{2,1,0:T(8,128)(2,1)S(1)}, u32[]{:S(2)}, u32[]{:S(2)}) async-start(bf16[4,72,576]{2,1,0:T(8,128)(2,1)} %pad_maximum_fusion.7), calls=%async_computation.7 | async-start | bytes 737280 | tf_op jit(solution)/shard_map/all_to_all | solution.py:96
  509.9 31.5 %collective-permute-start.55 = (bf16[144,864]{1,0:T(8,128)(2,1)S(1)}, bf16[144,864]{1,0:T(8,128)(2,1)S(1)}, u32[]{:S(2)}, u32[]{:S(2)}) collective-permute-start(bf16[144,864]{1,0:T(8,128)(2,1)S(1)} %get-tuple-element.286), channel_id=1, source_target_pairs={{0,2},{1,3},{2,0},{3,1},{4,6},{5,7},{6,4},{7,5},{8,10},{9,11},{10,... | collective-permute-start | bytes 746504 | tf_op jit(solution)/shard_map/ppermute | solution.py:120
  512.9 28.5 %collective-permute-start.56 = (bf16[144,864]{1,0:T(8,128)(2,1)S(1)}, bf16[144,864]{1,0:T(8,128)(2,1)S(1)}, u32[]{:S(2)}, u32[]{:S(2)}) collective-permute-start(bf16[144,864]{1,0:T(8,128)(2,1)S(1)} %get-tuple-element.287), channel_id=1, source_target_pairs={{0,1},{1,2},{2,3},{3,0},{4,5},{5,6},{6,7},{7,4},{8,9},{9,10},{10,1... | collective-permute-start | bytes 746504 | tf_op jit(solution)/shard_map/ppermute | solution.py:120
  514.4 27.0 %collective-permute-start.54 = (bf16[144,864]{1,0:T(8,128)(2,1)S(1)}, bf16[144,864]{1,0:T(8,128)(2,1)S(1)}, u32[]{:S(2)}, u32[]{:S(2)}) collective-permute-start(bf16[144,864]{1,0:T(8,128)(2,1)S(1)} %get-tuple-element.285), channel_id=1, source_target_pairs={{0,3},{1,0},{2,1},{3,2},{4,7},{5,4},{6,5},{7,6},{8,11},{9,8},{10,9... | collective-permute-start | bytes 746504 | tf_op jit(solution)/shard_map/ppermute | solution.py:120
  (66 other events, 649.4 us)
